TPU v7x, 512 devices: a whole 4x4x16 slice. The times are simulated.
512 devices in a mesh: row: 16 (over y, x), col: 32 (over z, core).
Axes of the slice: x: 4, y: 4, z: 16, core: 2. Of those that a mesh axis runs over, the one named last changes fastest.
Arguments:
- factor_panel: bfloat16 [2, 2048, 98304], P(None, 'row', 'col'), may hold values from -0.01953125 to 0.01953125
- solved_earlier: bfloat16 [1024, 98304], P('row', 'col'), may hold values from -6 to 6
- right_side: bfloat16 [2, 2048, 1024], P(None, 'row'), may hold values from -6 to 6
- coupling: bfloat16 [2048, 2048], P('row', 'col'), may hold values from -0.125 to 0.125
- inverses: bfloat16 [2, 2048, 2048], P(None, 'col', 'row'), as said below
Outputs:
- solved: bfloat16 [2, 2048, 1024], P(None, 'col')
Inputs may be any that keep to these rules, and one draw needn't show every extreme that they name: `inverses`: each of the two blocks is lower triangular with a positive diagonal.
All inputs are finite; a program needn't handle non-finite values.
Results may differ from a plain program's by a relative error of at most 0.006.
Values may be sent and summed in bfloat16 or wider, within the bound.
No kernel may reach another device: no remote copies, remote signals or barrier semaphores. Data moves between devices by JAX's collectives and lax.ppermute only.
A program may use at most 64 MiB of HBM per device.

v0:
```python
import jax
import jax.numpy as jnp
from jax import lax
from jax.sharding import PartitionSpec as P


def per_device(factor_panel, solved_earlier, right_side, coupling, inverses):
    partial_terms = lax.dot_general(
        factor_panel,
        lax.all_gather(solved_earlier, "row", axis=0, tiled=True),
        (((2,), (1,)), ((), ())),
        preferred_element_type=jnp.float32,
    )
    whole_inverses = lax.all_gather(inverses, "row", axis=2, tiled=True)

    def apply_inverse(residual, block_index):
        own_rows = whole_inverses[block_index]
        total = jnp.dot(
            own_rows,
            lax.all_gather(residual, "row", axis=0, tiled=True),
            preferred_element_type=jnp.float32,
        )
        return total.astype(jnp.bfloat16)

    summed = lax.psum(partial_terms, "col")
    first_total = summed[0]
    second_part = summed[1]
    residual_first = (right_side[0].astype(jnp.float32) - first_total).astype(jnp.bfloat16)
    solved_first = apply_inverse(residual_first, 0)
    cross_local = jnp.dot(coupling, solved_first, preferred_element_type=jnp.float32)
    second_total = second_part + lax.psum(cross_local, "col")
    residual_second = (right_side[1].astype(jnp.float32) - second_total).astype(jnp.bfloat16)
    solved_second = apply_inverse(residual_second, 1)
    return jnp.stack([solved_first, solved_second])


def solution(mesh):
    return jax.shard_map(
        per_device,
        mesh=mesh,
        in_specs=(
            P(None, "row", "col"),
            P("row", "col"),
            P(None, "row", None),
            P("row", "col"),
            P(None, "col", "row"),
        ),
        out_specs=P(None, "col", None),
        check_vma=False,
    )
```

profile of v0, /device:TPU:1, one launch (start us, length us, event | category | flops | bytes accessed | tf_op | source)
XLA Modules:
  0.0 670.3 jit_solution(16458569568675160284)
XLA Ops:
  6.5 0.0 copy-start
  6.5 0.0 all-gather.5.cloned.1.call-start
  6.5 0.7 all-gather.5.cloned.1.call-update
  7.3 0.0 copy-start.2
  7.3 0.0 copy-start.3
  7.3 0.0 all-reduce.3.cloned.1.call-start
  7.3 85.0 %all-gather.5.cloned.1.call-done = bf16[1024,3072]{1,0:T(8,128)(2,1)} async-done(((bf16[64,3072]{1,0:T(8,128)(2,1)}), bf16[1024,3072]{1,0:T(8,128)(2,1)}) %all-gather.5.cloned.1.call-update) | async-done | bytes 6291472 | tf_op jit(solution)/shard_map/all_gather | solution.py:10
  92.4 0.0 copy-done
  92.4 5.6 fusion
  98.0 0.0 copy-start.4
  98.0 0.0 all-reduce.3.cloned.1.call-update
  98.0 0.0 all-gather.9.cloned.1.call-start
  98.1 210.4 %all-reduce.3.cloned.1.call-done = f32[2,128,1024]{2,1,0:T(8,128)} async-done(((f32[2,128,1024]{2,1,0:T(8,128)}), f32[2,128,1024]{2,1,0:T(8,128)}) %all-reduce.3.cloned.1.call-update) | async-done | bytes 1048592 | tf_op jit(solution)/shard_map/psum | solution.py:25
  308.5 0.0 copy-done.2
  308.5 0.0 copy-start.1
  308.5 1.9 fusion.11
  310.4 0.0 all-gather.9.cloned.1.call-update
  310.4 0.0 all-reduce.5.cloned.1.call-start
  310.4 0.0 copy-done.3
  310.4 19.5 %all_gather.14 = bf16[2,64,2048]{2,1,0:T(8,128)(2,1)S(1)} all-gather(bf16[2,64,128]{2,1,0:T(8,128)(2,1)S(1)} %copy-done.3), channel_id=1, replica_groups=mesh['row'=16,'col'=32] {'row'}, dimensions={2}, use_global_device_ids=true | all-gather | bytes 557056 | tf_op jit(solution)/shard_map/all_gather | solution.py:14
  329.9 48.6 %all-gather.9.cloned.1.call-done = bf16[1,2048,1024]{2,1,0:T(8,128)(2,1)} async-done(((bf16[1,128,1024]{2,1,0:T(8,128)(2,1)}), bf16[1,2048,1024]{2,1,0:T(8,128)(2,1)}) %all-gather.9.cloned.1.call-update) | async-done | bytes 4194320 | tf_op jit(solution)/shard_map/all_gather | solution.py:20
  378.5 3.0 fusion.4
  381.5 0.0 copy-done.4
  381.5 1.1 convolution_bitcast_fusion
  382.6 0.0 all-reduce.5.cloned.1.call-update
  382.6 0.0 all-gather.7.cloned.1.call-start
  382.7 207.9 %all-reduce.5.cloned.1.call-done = f32[128,1024]{1,0:T(8,128)} async-done(((f32[128,1024]{1,0:T(8,128)}), f32[128,1024]{1,0:T(8,128)}) %all-reduce.5.cloned.1.call-update) | async-done | bytes 524304 | tf_op jit(solution)/shard_map/psum | solution.py:31
  590.5 0.0 copy-done.1
  590.5 1.9 fusion.10
  592.5 0.0 all-gather.7.cloned.1.call-update
  592.5 67.5 %all-gather.7.cloned.1.call-done = bf16[2048,1024]{1,0:T(8,128)(2,1)} async-done(((bf16[128,1024]{1,0:T(8,128)(2,1)}), bf16[2048,1024]{1,0:T(8,128)(2,1)}) %all-gather.7.cloned.1.call-update) | async-done | bytes 4194320 | tf_op jit(solution)/shard_map/all_gather | solution.py:20
  660.0 3.0 fusion.7
  663.0 0.7 pad_maximum_fusion
Async XLA Ops:
  6.5 85.8 %copy-start = (bf16[2,128,3072]{2,1,0:T(8,128)(2,1)S(1)}, bf16[2,128,3072]{2,1,0:T(8,128)(2,1)}, u32[]{:S(2)}) copy-start(bf16[2,128,3072]{2,1,0:T(8,128)(2,1)} %param.5) | copy-start | bytes 4718596
  6.5 85.8 %all-gather.5.cloned.1.call-start = ((), (), s32[]{:S(2)}) async-start(), calls=%async_computation | async-start | bytes 6684672 | tf_op jit(solution)/shard_map/all_gather | solution.py:10
  7.3 301.2 %copy-start.2 = (bf16[2,128,1024]{2,1,0:T(8,128)(2,1)S(1)}, bf16[2,128,1024]{2,1,0:T(8,128)(2,1)}, u32[]{:S(2)}) copy-start(bf16[2,128,1024]{2,1,0:T(8,128)(2,1)} %param.7) | copy-start | bytes 1572868
  7.3 303.2 %copy-start.3 = (bf16[2,64,128]{2,1,0:T(8,128)(2,1)S(1)}, bf16[2,64,128]{2,1,0:T(8,128)(2,1)}, u32[]{:S(2)}) copy-start(bf16[2,64,128]{2,1,0:T(8,128)(2,1)} %param.9) | copy-start | bytes 98308
  7.3 301.2 %all-reduce.3.cloned.1.call-start = ((), (), s32[]{:S(2)}) async-start(), calls=%async_computation.1 | async-start | bytes 2097152 | tf_op jit(solution)/shard_map/psum | solution.py:25
  98.0 283.6 %copy-start.4 = (bf16[128,64]{0,1:T(8,128)(2,1)S(1)}, bf16[128,64]{0,1:T(8,128)(2,1)}, u32[]{:S(2)}) copy-start(bf16[128,64]{0,1:T(8,128)(2,1)} %param.8) | copy-start | bytes 49156
  98.0 280.5 %all-gather.9.cloned.1.call-start = ((), (), s32[]{:S(2)}) async-start(), calls=%async_computation.4 | async-start | bytes 4456448 | tf_op jit(solution)/shard_map/all_gather | solution.py:20
  308.5 282.1 %copy-start.1 = (f32[2,128,1024]{2,1,0:T(8,128)S(1)}, f32[2,128,1024]{2,1,0:T(8,128)}, u32[]{:S(2)}) copy-start(f32[2,128,1024]{2,1,0:T(8,128)} %all-reduce.3.cloned.1.call-done) | copy-start | bytes 3145732
  310.4 280.2 %all-reduce.5.cloned.1.call-start = ((), (), s32[]{:S(2)}) async-start(), calls=%async_computation.2 | async-start | bytes 1048576 | tf_op jit(solution)/shard_map/psum | solution.py:31
  382.6 277.3 %all-gather.7.cloned.1.call-start = ((), (), s32[]{:S(2)}) async-start(), calls=%async_computation.3 | async-start | bytes 4456448 | tf_op jit(solution)/shard_map/all_gather | solution.py:20
Sparse Core Ops, SparseCore 0:
  10.4 81.9 all-gather.4
  98.1 210.2 all-reduce.2
  311.9 66.5 all-gather.8
  382.8 207.7 all-reduce.4
  593.4 66.5 all-gather.6
where the time goes:
time: 671 us; the launch traced here: 670 us
  waiting for transfers between devices  620 us (92%)
  blocking collectives  19.5 us (3%)
  between operations  13.2 us (2%)
  matrix products  12.7 us (2%)
    psum x1, waiting for transfers between devices, per_device(): summed = lax.psum(partial_terms, 'col')  210 us
    psum x1, waiting for transfers between devices, per_device(): second_total = second_part + lax.psum(cross_local, 'col')  208 us
    all_gather x2, waiting for transfers between devices, apply_inverse(): lax.all_gather(residual, 'row', axis=0, tiled=True)  116 us
    all_gather x1, waiting for transfers between devices, per_device(): lax.all_gather(solved_earlier, 'row', axis=0, tiled=True)  85 us
    all_gather x1, blocking collectives, per_device(): whole_inverses = lax.all_gather(inverses, 'row', axis=2, tiled=True)  19.5 us
  transfers between devices with their start and end apart: 5, of which 5 were waited for; matrix products, arithmetic and copies ran while one was open for 0% of the time, Pallas kernels for 0%

commit v1 on v0

v1 whole, which is shorter than its diff:
```python
import jax
import jax.numpy as jnp
from jax import lax
from jax.sharding import Mesh, PartitionSpec as P

BF16 = jnp.bfloat16
F32 = jnp.float32


def spread(block, axis, size):
    copies = jnp.broadcast_to(block[None], (size,) + block.shape)
    return lax.all_to_all(copies, axis, 0, 0)


def sum_rows(terms, axis, size):
    rows, cols = terms.shape
    pieces = lax.all_to_all(terms.reshape(size, rows // size, cols), axis, 0, 0)
    return jnp.sum(pieces.astype(F32), axis=0)


def swap_cores(block):
    return lax.ppermute(block, "core", [(0, 1), (1, 0)])


def matmul(a, b, contract):
    return lax.dot_general(a, b, ((contract[0:1], contract[1:2]), ((), ())), preferred_element_type=F32)


def make_per_device(n_row, n_z):
    def per_device(factor_panel, solved_earlier, right_side, coupling, inverses):
        core = lax.axis_index("core")
        z = lax.axis_index("z")
        blocks, rows, depth = factor_panel.shape
        own = coupling.shape[1]

        earlier = lax.all_gather(solved_earlier, "row", axis=0, tiled=True)

        packed = jnp.concatenate([coupling.T, inverses[0]], axis=0)
        mine = spread(packed, "z", n_z)
        other = swap_cores(mine)

        def pick(part, first):
            return part[:, :own] if first else part[:, own:]

        left = [
            matmul(inverses[1], pick(part, True).reshape(-1, rows), (1, 1)).astype(BF16)
            for part in (mine, other)
        ]
        left = spread(sum_rows(jnp.concatenate(left, axis=0), "row", n_row).astype(BF16), "row", n_row)
        left = left.reshape(2, own, -1)
        cross = -(
            matmul(left[0], pick(mine, False).reshape(-1, rows), (1, 0))
            + matmul(left[1], pick(other, False).reshape(-1, rows), (1, 0))
        )
        from_first = jnp.concatenate([inverses[0], cross.astype(BF16)], axis=0)
        from_second = jnp.concatenate([jnp.zeros_like(inverses[1]), inverses[1]], axis=0)
        weights_mine = jnp.where(core == 0, from_first, from_second)
        weights_other = jnp.where(core == 0, from_second, from_first)

        earlier, weights_mine, weights_other = lax.optimization_barrier((earlier, weights_mine, weights_other))

        terms = matmul(factor_panel.reshape(blocks * rows, depth), earlier, (1, 1))
        terms = terms.reshape(blocks, rows, -1)
        kept = jnp.where(core == 0, terms[0], terms[1])
        sent = jnp.where(core == 0, terms[1], terms[0]).astype(BF16)
        kept = (kept + swap_cores(sent).astype(F32)).astype(BF16)
        prefix = sum_rows(kept, "z", n_z)
        part = rows // n_z
        right = jnp.where(core == 0, right_side[0], right_side[1])
        right = lax.dynamic_slice_in_dim(right, z * part, part, axis=0)
        residual = (right.astype(F32) - prefix).astype(BF16)
        residual = spread(residual, "z", n_z).reshape(rows, -1)
        residual_other = swap_cores(residual)

        out = matmul(weights_mine, residual, (1, 0)) + matmul(weights_other, residual_other, (1, 0))
        out = sum_rows(out.astype(BF16), "row", n_row).astype(BF16)
        return spread(out, "row", n_row).reshape(blocks, own, -1)

    return per_device


def solution(mesh):
    n_row, n_col = mesh.shape["row"], mesh.shape["col"]
    n_z = n_col // 2
    split = Mesh(mesh.devices.reshape(n_row, n_z, 2), ("row", "z", "core"))
    col = ("z", "core")
    return jax.shard_map(
        make_per_device(n_row, n_z),
        mesh=split,
        in_specs=(
            P(None, "row", col),
            P("row", col),
            P(None, "row", None),
            P("row", col),
            P(None, col, "row"),
        ),
        out_specs=P(None, col, None),
        check_vma=False,
    )
```

time: 671 us -> 196 us (0.29)
  waiting for transfers between devices: 620 us -> 33.7 us
  blocking collectives: 19.5 us -> 102 us
  starting transfers between devices: 0.17 us -> 33.1 us
    psum x2 -> x0, waiting for transfers between devices: 418 us -> none  [the longest x1 210 us: per_device(): summed = lax.psum(partial_terms, 'col')]
    all_gather x3 -> x1, waiting for transfers between devices: 201 us -> 5.48 us  [per_device(): earlier = lax.all_gather(solved_earlier, 'row', axis=0, tiled=True)]
    all_to_all x0 -> x5, blocking collectives: none -> 102 us  [the longest x3 72.1 us: spread(): return lax.all_to_all(copies, axis, 0, 0)]
    all_to_all x0 -> x2, waiting for transfers between devices: none -> 24.9 us  [the longest x1 14 us: sum_rows(): pieces = lax.all_to_all(terms.reshape(size, rows // size, cols), axis, 0, 0)]
    all_gather x1 -> x0, blocking collectives: 19.5 us -> none  [per_device(): whole_inverses = lax.all_gather(inverses, 'row', axis=2, tiled=True)]
    ppermute x0 -> x3, starting transfers between devices: none -> 19.4 us  [swap_cores(): return lax.ppermute(block, 'core', [(0, 1), (1, 0)])]
    all_to_all x0 -> x2, starting transfers between devices: none -> 13.7 us  [the longest x1 10.2 us: sum_rows(): pieces = lax.all_to_all(terms.reshape(size, rows // size, cols), axis, 0, 0)]
  transfers between devices with their start and end apart: 5 -> 6, of which waited for: 5 -> 6; matrix products, arithmetic and copies ran while one was open for 0% -> 3% of each run, Pallas kernels for 0% -> 0%
where the time goes in v1:
time: 196 us; the launch traced here: 194 us
  blocking collectives  102 us (52%)
  waiting for transfers between devices  33.7 us (17%)
  starting transfers between devices  33.1 us (17%)
  between operations  13.6 us (7%)
  matrix products  7.29 us (4%)
  local copies, waits for them, and re-layouts  2.42 us (1%)
    all_to_all x3, blocking collectives, spread(): return lax.all_to_all(copies, axis, 0, 0)  72.1 us
    all_to_all x2, blocking collectives, sum_rows(): pieces = lax.all_to_all(terms.reshape(size, rows // size, cols), axis, 0, 0)  29.8 us
    ppermute x3, starting transfers between devices, swap_cores(): return lax.ppermute(block, 'core', [(0, 1), (1, 0)])  19.4 us
    all_to_all x1, waiting for transfers between devices, sum_rows(): pieces = lax.all_to_all(terms.reshape(size, rows // size, cols), axis, 0, 0)  14 us
    all_to_all x1, waiting for transfers between devices, spread(): return lax.all_to_all(copies, axis, 0, 0)  10.9 us
    all_to_all x1, starting transfers between devices, sum_rows(): pieces = lax.all_to_all(terms.reshape(size, rows // size, cols), axis, 0, 0)  10.2 us
    dot_general x7, matrix products, matmul(): lax.dot_general(a, b, ((contract[0:1], contract[1:2]), ((), ())), preferr...  7.29 us
    all_gather x1, waiting for transfers between devices, per_device(): earlier = lax.all_gather(solved_earlier, 'row', axis=0, tiled=True)  5.48 us
  transfers between devices with their start and end apart: 6, of which 6 were waited for; matrix products, arithmetic and copies ran while one was open for 3% of the time, Pallas kernels for 0%

profile of v1, /device:TPU:1, one launch (start us, length us, event | category | flops | bytes accessed | tf_op | source)
XLA Modules:
  0.0 193.7 jit_solution(14918652327895011509)
XLA Ops:
  6.5 0.0 copy-start
  6.5 0.0 all-gather.2.cloned.1.call-start
  6.5 0.7 all-gather.2.cloned.1.call-update
  7.3 0.7 slice_bitcast_fusion.5
  8.0 0.7 pad_maximum_fusion
  8.7 0.1 broadcast_in_dim.8
  8.8 38.4 %all_to_all.35 = bf16[16,128,128]{2,1,0:T(8,128)(2,1)S(1)} all-to-all(bf16[16,128,128]{2,1,0:T(8,128)(2,1)S(1)} %broadcast_in_dim.8), channel_id=1, replica_groups=mesh['row'=16,'z'=16,'core'=2] {'z'}, dimensions={0} | all-to-all | bytes 1048576 | tf_op jit(solution)/shard_map/all_to_all | solution.py:12
  47.2 9.1 %collective-permute-start = (bf16[16,128,128]{2,1,0:T(8,128)(2,1)S(1)}, bf16[16,128,128]{2,1,0:T(8,128)(2,1)S(1)}, u32[]{:S(2)}, u32[]{:S(2)}) collective-permute-start(bf16[16,128,128]{2,1,0:T(8,128)(2,1)S(1)} %all_to_all.35), channel_id=1, source_target_pairs={{0,1},{1,0},{2,3},{3,2},{4,5},{5,4},{6,7},{7,6},{8,9},{9,8},{10,11... | collective-permute-start | bytes 1572872 | tf_op jit(solution)/shard_map/ppermute | solution.py:22
  56.4 0.9 fusion.2
  57.3 0.5 collective-permute-done
  57.9 0.9 fusion.3
  58.8 17.9 %all_to_all.36 = bf16[16,8,1024]{2,1,0:T(8,128)(2,1)S(1)} all-to-all(bf16[16,8,1024]{2,1,0:T(8,128)(2,1)S(1)} %maximum_bitcast_fusion), channel_id=1, replica_groups=mesh['row'=16,'z'=16,'core'=2] {'row'}, dimensions={0} | all-to-all | bytes 524288 | tf_op jit(solution)/shard_map/all_to_all | solution.py:17
  76.8 0.7 broadcast_in_dim.9
  77.5 3.5 %all-to-all-start.2 = ((bf16[16,8,1024]{2,1,0:T(8,128)(2,1)}), bf16[16,8,1024]{2,1,0:T(8,128)(2,1)S(1)}, u32[]{:S(2)}, u32[]{:S(2)}) async-start(bf16[16,8,1024]{2,1,0:T(8,128)(2,1)} %broadcast_in_dim.9), calls=%async_computation.2 | async-start | bytes 524288 | tf_op jit(solution)/shard_map/all_to_all | solution.py:12
  81.1 10.9 %all-to-all-done.2 = bf16[16,8,1024]{2,1,0:T(8,128)(2,1)S(1)} async-done(((bf16[16,8,1024]{2,1,0:T(8,128)(2,1)}), bf16[16,8,1024]{2,1,0:T(8,128)(2,1)S(1)}, u32[]{:S(2)}, u32[]{:S(2)}) %all-to-all-start.2) | async-done | bytes 262176 | tf_op jit(solution)/shard_map/all_to_all | solution.py:12
  92.0 0.2 fusion.7
  92.2 0.2 fusion.5
  92.4 5.5 %all-gather.2.cloned.1.call-done = bf16[1024,3072]{1,0:T(8,128)(2,1)} async-done(((bf16[64,3072]{1,0:T(8,128)(2,1)}), bf16[1024,3072]{1,0:T(8,128)(2,1)}) %all-gather.2.cloned.1.call-update) | async-done | bytes 6291472 | tf_op jit(solution)/shard_map/all_gather | solution.py:36
  97.9 0.0 copy-done
  97.9 0.0 copy-start.1
  97.9 4.7 %convolution_bitcast_fusion = f32[256,1024]{1,0:T(8,128)S(1)} fusion(bf16[1024,3072]{1,0:T(8,128)(2,1)} %all-gather.2.cloned.1.call-done, bf16[256,3072]{1,0:T(8,128)(2,1)S(1)} %bitcast.48), kind=kOutput, calls=%fused_computation | convolution fusion | flops 1610612736 | bytes 8912896 | tf_op jit(solution)/shard_map/dot_general | solution.py:26
  102.6 0.1 select_convert_fusion
  102.6 2.6 %collective-permute-start.1 = (bf16[128,1024]{1,0:T(8,128)(2,1)S(1)}, bf16[128,1024]{1,0:T(8,128)(2,1)S(1)}, u32[]{:S(2)}, u32[]{:S(2)}) collective-permute-start(bf16[128,1024]{1,0:T(8,128)(2,1)S(1)} %select_convert_fusion), channel_id=1, source_target_pairs={{0,1},{1,0},{2,3},{3,2},{4,5},{5,4},{6,7},{7,6},{8,9},{9,8},{10,11... | collective-permute-start | bytes 786440 | tf_op jit(solution)/shard_map/ppermute | solution.py:22
  105.2 1.1 collective-permute-done.1
  106.3 0.8 fusion.6
  107.2 10.2 %all-to-all-start.3 = ((bf16[16,8,1024]{2,1,0:T(8,128)(2,1)}), bf16[16,8,1024]{2,1,0:T(8,128)(2,1)S(1)}, u32[]{:S(2)}, u32[]{:S(2)}) async-start(bf16[16,8,1024]{2,1,0:T(8,128)(2,1)} %fusion.6), calls=%async_computation.3 | async-start | bytes 524288 | tf_op jit(solution)/shard_map/all_to_all | solution.py:17
  117.4 0.0 copy-done.1
  117.4 14.0 %all-to-all-done.3 = bf16[16,8,1024]{2,1,0:T(8,128)(2,1)S(1)} async-done(((bf16[16,8,1024]{2,1,0:T(8,128)(2,1)}), bf16[16,8,1024]{2,1,0:T(8,128)(2,1)S(1)}, u32[]{:S(2)}, u32[]{:S(2)}) %all-to-all-start.3) | async-done | bytes 262176 | tf_op jit(solution)/shard_map/all_to_all | solution.py:17
  131.5 23.4 %all_to_all.37 = bf16[16,8,1024]{2,1,0:T(8,128)(2,1)S(1)} all-to-all(bf16[16,8,1024]{2,1,0:T(8,128)(2,1)S(1)} %broadcast_in_dim.10), channel_id=1, replica_groups=mesh['row'=16,'z'=16,'core'=2] {'z'}, dimensions={0} | all-to-all | bytes 524288 | tf_op jit(solution)/shard_map/all_to_all | solution.py:12
  154.9 7.6 %collective-permute-start.2 = (bf16[128,1024]{1,0:T(8,128)(2,1)S(1)}, bf16[128,1024]{1,0:T(8,128)(2,1)S(1)}, u32[]{:S(2)}, u32[]{:S(2)}) collective-permute-start(bf16[128,1024]{1,0:T(8,128)(2,1)S(1)} %bitcast.49), channel_id=1, source_target_pairs={{0,1},{1,0},{2,3},{3,2},{4,5},{5,4},{6,7},{7,6},{8,9},{9,8},{10,11... | collective-permute-start | bytes 786440 | tf_op jit(solution)/shard_map/ppermute | solution.py:22
  162.6 0.2 fusion.10
  162.8 0.9 collective-permute-done.2
  163.7 0.2 fusion.1
  163.9 11.9 %all_to_all.38 = bf16[16,8,1024]{2,1,0:T(8,128)(2,1)S(1)} all-to-all(bf16[16,8,1024]{2,1,0:T(8,128)(2,1)S(1)} %fusion.1), channel_id=1, replica_groups=mesh['row'=16,'z'=16,'core'=2] {'row'}, dimensions={0} | all-to-all | bytes 524288 | tf_op jit(solution)/shard_map/all_to_all | solution.py:17
  175.9 10.2 %all_to_all.39 = bf16[16,8,1024]{2,1,0:T(8,128)(2,1)S(1)} all-to-all(bf16[16,8,1024]{2,1,0:T(8,128)(2,1)S(1)} %broadcast_in_dim.11), channel_id=1, replica_groups=mesh['row'=16,'z'=16,'core'=2] {'row'}, dimensions={0} | all-to-all | bytes 524288 | tf_op jit(solution)/shard_map/all_to_all | solution.py:12
  186.1 0.7 copy.7
  (11 shorter events, 0.3 us)
Async XLA Ops:
  6.5 91.3 %copy-start = (bf16[2,128,3072]{2,1,0:T(8,128)(2,1)S(1)}, bf16[2,128,3072]{2,1,0:T(8,128)(2,1)}, u32[]{:S(2)}) copy-start(bf16[2,128,3072]{2,1,0:T(8,128)(2,1)} %param.5) | copy-start | bytes 4718596
  6.5 91.3 %all-gather.2.cloned.1.call-start = ((), (), s32[]{:S(2)}) async-start(), calls=%async_computation.7 | async-start | bytes 6684672 | tf_op jit(solution)/shard_map/all_gather | solution.py:36
  47.2 10.6 %collective-permute-start = (bf16[16,128,128]{2,1,0:T(8,128)(2,1)S(1)}, bf16[16,128,128]{2,1,0:T(8,128)(2,1)S(1)}, u32[]{:S(2)}, u32[]{:S(2)}) collective-permute-start(bf16[16,128,128]{2,1,0:T(8,128)(2,1)S(1)} %all_to_all.35), channel_id=1, source_target_pairs={{0,1},{1,0},{2,3},{3,2},{4,5},{5,4},{6,7},{7,6},{8,9},{9,8},{10,11... | collective-permute-start | bytes 1572872 | tf_op jit(solution)/shard_map/ppermute | solution.py:22
  77.5 14.5 %all-to-all-start.2 = ((bf16[16,8,1024]{2,1,0:T(8,128)(2,1)}), bf16[16,8,1024]{2,1,0:T(8,128)(2,1)S(1)}, u32[]{:S(2)}, u32[]{:S(2)}) async-start(bf16[16,8,1024]{2,1,0:T(8,128)(2,1)} %broadcast_in_dim.9), calls=%async_computation.2 | async-start | bytes 524288 | tf_op jit(solution)/shard_map/all_to_all | solution.py:12
  97.9 19.5 %copy-start.1 = (bf16[2,128,1024]{2,1,0:T(8,128)(2,1)S(1)}, bf16[2,128,1024]{2,1,0:T(8,128)(2,1)}, u32[]{:S(2)}) copy-start(bf16[2,128,1024]{2,1,0:T(8,128)(2,1)} %param.7) | copy-start | bytes 1572868
  102.6 3.7 %collective-permute-start.1 = (bf16[128,1024]{1,0:T(8,128)(2,1)S(1)}, bf16[128,1024]{1,0:T(8,128)(2,1)S(1)}, u32[]{:S(2)}, u32[]{:S(2)}) collective-permute-start(bf16[128,1024]{1,0:T(8,128)(2,1)S(1)} %select_convert_fusion), channel_id=1, source_target_pairs={{0,1},{1,0},{2,3},{3,2},{4,5},{5,4},{6,7},{7,6},{8,9},{9,8},{10,11... | collective-permute-start | bytes 786440 | tf_op jit(solution)/shard_map/ppermute | solution.py:22
  107.2 24.2 %all-to-all-start.3 = ((bf16[16,8,1024]{2,1,0:T(8,128)(2,1)}), bf16[16,8,1024]{2,1,0:T(8,128)(2,1)S(1)}, u32[]{:S(2)}, u32[]{:S(2)}) async-start(bf16[16,8,1024]{2,1,0:T(8,128)(2,1)} %fusion.6), calls=%async_computation.3 | async-start | bytes 524288 | tf_op jit(solution)/shard_map/all_to_all | solution.py:17
  154.9 8.8 %collective-permute-start.2 = (bf16[128,1024]{1,0:T(8,128)(2,1)S(1)}, bf16[128,1024]{1,0:T(8,128)(2,1)S(1)}, u32[]{:S(2)}, u32[]{:S(2)}) collective-permute-start(bf16[128,1024]{1,0:T(8,128)(2,1)S(1)} %bitcast.49), channel_id=1, source_target_pairs={{0,1},{1,0},{2,3},{3,2},{4,5},{5,4},{6,7},{7,6},{8,9},{9,8},{10,11... | collective-permute-start | bytes 786440 | tf_op jit(solution)/shard_map/ppermute | solution.py:22
Sparse Core Ops, SparseCore 0:
  10.4 87.4 all-gather.1

commit v2 on v1

--- a/solution.py
+++ b/solution.py
@@ -5,6 +5,7 @@
 
 BF16 = jnp.bfloat16
 F32 = jnp.float32
+ROW = ("y", "x")
 
 
 def spread(block, axis, size):
@@ -26,14 +27,14 @@
     return lax.dot_general(a, b, ((contract[0:1], contract[1:2]), ((), ())), preferred_element_type=F32)
 
 
-def make_per_device(n_row, n_z):
+def make_per_device(n_row, n_x, n_z):
     def per_device(factor_panel, solved_earlier, right_side, coupling, inverses):
         core = lax.axis_index("core")
         z = lax.axis_index("z")
         blocks, rows, depth = factor_panel.shape
         own = coupling.shape[1]
 
-        earlier = lax.all_gather(solved_earlier, "row", axis=0, tiled=True)
+        earlier = lax.all_gather(solved_earlier, ROW, axis=0, tiled=True)
 
         packed = jnp.concatenate([coupling.T, inverses[0]], axis=0)
         mine = spread(packed, "z", n_z)
@@ -46,8 +47,11 @@
             matmul(inverses[1], pick(part, True).reshape(-1, rows), (1, 1)).astype(BF16)
             for part in (mine, other)
         ]
-        left = spread(sum_rows(jnp.concatenate(left, axis=0), "row", n_row).astype(BF16), "row", n_row)
-        left = left.reshape(2, own, -1)
+        left = sum_rows(jnp.concatenate(left, axis=0), "x", n_x).astype(BF16)
+        earlier, left = lax.optimization_barrier((earlier, left))
+        quarters = lax.all_gather(left, ROW, axis=0, tiled=False)
+        quarters = quarters.reshape(n_row // n_x, n_x * left.shape[0], -1)
+        left = jnp.sum(quarters.astype(F32), axis=0).astype(BF16).reshape(2, own, -1)
         cross = -(
             matmul(left[0], pick(mine, False).reshape(-1, rows), (1, 0))
             + matmul(left[1], pick(other, False).reshape(-1, rows), (1, 0))
@@ -56,8 +60,6 @@
         from_second = jnp.concatenate([jnp.zeros_like(inverses[1]), inverses[1]], axis=0)
         weights_mine = jnp.where(core == 0, from_first, from_second)
         weights_other = jnp.where(core == 0, from_second, from_first)
-
-        earlier, weights_mine, weights_other = lax.optimization_barrier((earlier, weights_mine, weights_other))
 
         terms = matmul(factor_panel.reshape(blocks * rows, depth), earlier, (1, 1))
         terms = terms.reshape(blocks, rows, -1)
@@ -73,8 +75,8 @@
         residual_other = swap_cores(residual)
 
         out = matmul(weights_mine, residual, (1, 0)) + matmul(weights_other, residual_other, (1, 0))
-        out = sum_rows(out.astype(BF16), "row", n_row).astype(BF16)
-        return spread(out, "row", n_row).reshape(blocks, own, -1)
+        out = sum_rows(out.astype(BF16), ROW, n_row).astype(BF16)
+        return spread(out, ROW, n_row).reshape(blocks, own, -1)
 
     return per_device
 
@@ -82,17 +84,18 @@
 def solution(mesh):
     n_row, n_col = mesh.shape["row"], mesh.shape["col"]
     n_z = n_col // 2
-    split = Mesh(mesh.devices.reshape(n_row, n_z, 2), ("row", "z", "core"))
+    n_x = 4
+    split = Mesh(mesh.devices.reshape(n_row // n_x, n_x, n_z, 2), ("y", "x", "z", "core"))
     col = ("z", "core")
     return jax.shard_map(
-        make_per_device(n_row, n_z),
+        make_per_device(n_row, n_x, n_z),
         mesh=split,
         in_specs=(
-            P(None, "row", col),
-            P("row", col),
-            P(None, "row", None),
-            P("row", col),
-            P(None, col, "row"),
+            P(None, ROW, col),
+            P(ROW, col),
+            P(None, ROW, None),
+            P(ROW, col),
+            P(None, col, ROW),
         ),
         out_specs=P(None, col, None),
         check_vma=False,

time: 196 us -> 213 us (1.087)
  waiting for transfers between devices: 33.7 us -> 82.8 us
  blocking collectives: 102 us -> 61.1 us
  starting transfers between devices: 33.1 us -> 39.2 us
  other arithmetic: 1.77 us -> 4.5 us
    all_gather x1 -> x2, waiting for transfers between devices: 5.48 us -> 56.5 us  [the longest x1 35 us: per_device(): quarters = lax.all_gather(left, ROW, axis=0, tiled=False)]
    all_to_all x3 -> x2, blocking collectives: 72.1 us -> 48.6 us  [spread(): return lax.all_to_all(copies, axis, 0, 0)]
    all_to_all x2 -> x1, blocking collectives: 29.8 us -> 12.5 us  [sum_rows(): pieces = lax.all_to_all(terms.reshape(size, rows // size, cols), axis, 0, 0)]
    all_to_all x1, waiting for transfers between devices: 10.9 us -> 0.01 us  [spread(): return lax.all_to_all(copies, axis, 0, 0)]
    all_to_all x1 -> x2, waiting for transfers between devices: 14 us -> 22.4 us  [sum_rows(): pieces = lax.all_to_all(terms.reshape(size, rows // size, cols), axis, 0, 0)]
    all_to_all x1, starting transfers between devices: 3.53 us -> 10.2 us  [spread(): return lax.all_to_all(copies, axis, 0, 0)]
    ppermute x3, starting transfers between devices: 19.4 us -> 15.7 us  [swap_cores(): return lax.ppermute(block, 'core', [(0, 1), (1, 0)])]
    all_to_all x1 -> x2, starting transfers between devices: 10.2 us -> 13.3 us  [sum_rows(): pieces = lax.all_to_all(terms.reshape(size, rows // size, cols), axis, 0, 0)]
  transfers between devices with their start and end apart: 6 -> 8, of which waited for: 6 -> 7; matrix products, arithmetic and copies ran while one was open for 3% -> 4% of each run, Pallas kernels for 0% -> 0%
where the time goes in v2:
time: 213 us; the launch traced here: 211 us
  waiting for transfers between devices  82.8 us (39%)
  blocking collectives  61.1 us (29%)
  starting transfers between devices  39.2 us (18%)
  between operations  13.6 us (6%)
  matrix products  7.29 us (3%)
  other arithmetic  4.5 us (2%)
  local copies, waits for them, and re-layouts  2.4 us (1%)
    all_to_all x2, blocking collectives, spread(): return lax.all_to_all(copies, axis, 0, 0)  48.6 us
    all_gather x1, waiting for transfers between devices, per_device(): quarters = lax.all_gather(left, ROW, axis=0, tiled=False)  35 us
    all_to_all x2, waiting for transfers between devices, sum_rows(): pieces = lax.all_to_all(terms.reshape(size, rows // size, cols), axis, 0, 0)  22.4 us
    all_gather x1, waiting for transfers between devices, per_device(): earlier = lax.all_gather(solved_earlier, ROW, axis=0, tiled=True)  21.6 us
    ppermute x3, starting transfers between devices, swap_cores(): return lax.ppermute(block, 'core', [(0, 1), (1, 0)])  15.7 us
    all_to_all x2, starting transfers between devices, sum_rows(): pieces = lax.all_to_all(terms.reshape(size, rows // size, cols), axis, 0, 0)  13.3 us
    all_to_all x1, blocking collectives, sum_rows(): pieces = lax.all_to_all(terms.reshape(size, rows // size, cols), axis, 0, 0)  12.5 us
    all_to_all x1, starting transfers between devices, spread(): return lax.all_to_all(copies, axis, 0, 0)  10.2 us
  transfers between devices with their start and end apart: 8, of which 7 were waited for; matrix products, arithmetic and copies ran while one was open for 4% of the time, Pallas kernels for 0%

profile of v2, /device:TPU:1, one launch (start us, length us, event | category | flops | bytes accessed | tf_op | source)
XLA Modules:
  0.0 210.9 jit_solution(2871520673713697515)
XLA Ops:
  6.5 0.0 copy-start
  6.5 0.0 all-gather.4.cloned.1.call-start
  6.5 0.7 all-gather.4.cloned.1.call-update
  7.3 0.7 slice_bitcast_fusion.1
  8.0 0.7 pad_maximum_fusion.1
  8.7 0.1 broadcast_in_dim.6
  8.8 38.4 %all_to_all.30 = bf16[16,128,128]{2,1,0:T(8,128)(2,1)S(1)} all-to-all(bf16[16,128,128]{2,1,0:T(8,128)(2,1)S(1)} %broadcast_in_dim.6), channel_id=1, replica_groups=mesh['y'=4,'x'=4,'z'=16,'core'=2] {'z'}, dimensions={0} | all-to-all | bytes 1048576 | tf_op jit(solution)/shard_map/all_to_all | solution.py:13
  47.2 9.1 %collective-permute-start = (bf16[16,128,128]{2,1,0:T(8,128)(2,1)S(1)}, bf16[16,128,128]{2,1,0:T(8,128)(2,1)S(1)}, u32[]{:S(2)}, u32[]{:S(2)}) collective-permute-start(bf16[16,128,128]{2,1,0:T(8,128)(2,1)S(1)} %all_to_all.30), channel_id=1, source_target_pairs={{0,1},{1,0},{2,3},{3,2},{4,5},{5,4},{6,7},{7,6},{8,9},{9,8},{10,11... | collective-permute-start | bytes 1572872 | tf_op jit(solution)/shard_map/ppermute | solution.py:23
  56.4 0.9 fusion.2
  57.3 0.5 collective-permute-done
  57.9 0.9 fusion.3
  58.8 0.7 pad_maximum_fusion
  59.5 4.0 %all-to-all-start.1 = ((bf16[4,32,1024]{2,1,0:T(8,128)(2,1)}), bf16[4,32,1024]{2,1,0:T(8,128)(2,1)S(1)}, u32[]{:S(2)}, u32[]{:S(2)}) async-start(bf16[4,32,1024]{2,1,0:T(8,128)(2,1)} %bitcast.7), calls=%async_computation.1 | async-start | bytes 524288 | tf_op jit(solution)/shard_map/all_to_all | solution.py:18
  63.5 9.2 %all-to-all-done.1 = bf16[4,32,1024]{2,1,0:T(8,128)(2,1)S(1)} async-done(((bf16[4,32,1024]{2,1,0:T(8,128)(2,1)}), bf16[4,32,1024]{2,1,0:T(8,128)(2,1)S(1)}, u32[]{:S(2)}, u32[]{:S(2)}) %all-to-all-start.1) | async-done | bytes 262176 | tf_op jit(solution)/shard_map/all_to_all | solution.py:18
  72.8 0.7 reduce_sum.45
  73.4 21.6 %all-gather.4.cloned.1.call-done = bf16[1024,3072]{1,0:T(8,128)(2,1)} async-done(((bf16[64,3072]{1,0:T(8,128)(2,1)}), bf16[1024,3072]{1,0:T(8,128)(2,1)}) %all-gather.4.cloned.1.call-update) | async-done | bytes 6291472 | tf_op jit(solution)/shard_map/all_gather | solution.py:37
  95.0 0.0 copy-done
  95.0 0.0 copy-start.1
  95.0 4.7 %convolution_bitcast_fusion = f32[256,1024]{1,0:T(8,128)S(1)} fusion(bf16[1024,3072]{1,0:T(8,128)(2,1)} %all-gather.4.cloned.1.call-done, bf16[256,3072]{1,0:T(8,128)(2,1)S(1)} %bitcast.40), kind=kOutput, calls=%fused_computation | convolution fusion | flops 1610612736 | bytes 8912896 | tf_op jit(solution)/shard_map/dot_general | solution.py:27
  99.7 0.1 select_convert_fusion
  99.7 2.6 %collective-permute-start.1 = (bf16[128,1024]{1,0:T(8,128)(2,1)S(1)}, bf16[128,1024]{1,0:T(8,128)(2,1)S(1)}, u32[]{:S(2)}, u32[]{:S(2)}) collective-permute-start(bf16[128,1024]{1,0:T(8,128)(2,1)S(1)} %select_convert_fusion), channel_id=1, source_target_pairs={{0,1},{1,0},{2,3},{3,2},{4,5},{5,4},{6,7},{7,6},{8,9},{9,8},{10,11... | collective-permute-start | bytes 786440 | tf_op jit(solution)/shard_map/ppermute | solution.py:23
  102.3 1.1 collective-permute-done.1
  103.5 0.8 fusion.6
  104.3 9.3 %all-to-all-start.2 = ((bf16[16,8,1024]{2,1,0:T(8,128)(2,1)}), bf16[16,8,1024]{2,1,0:T(8,128)(2,1)S(1)}, u32[]{:S(2)}, u32[]{:S(2)}) async-start(bf16[16,8,1024]{2,1,0:T(8,128)(2,1)} %fusion.6), calls=%async_computation.2 | async-start | bytes 524288 | tf_op jit(solution)/shard_map/all_to_all | solution.py:18
  113.6 0.0 all-gather.6.cloned.1.call-start
  113.6 0.7 all-gather.6.cloned.1.call-update
  114.3 0.0 copy-done.1
  114.4 13.2 %all-to-all-done.2 = bf16[16,8,1024]{2,1,0:T(8,128)(2,1)S(1)} async-done(((bf16[16,8,1024]{2,1,0:T(8,128)(2,1)}), bf16[16,8,1024]{2,1,0:T(8,128)(2,1)S(1)}, u32[]{:S(2)}, u32[]{:S(2)}) %all-to-all-start.2) | async-done | bytes 262176 | tf_op jit(solution)/shard_map/all_to_all | solution.py:18
  127.6 0.7 broadcast_in_dim.7
  128.4 10.2 %all-to-all-start.3 = ((bf16[16,8,1024]{2,1,0:T(8,128)(2,1)}), bf16[16,8,1024]{2,1,0:T(8,128)(2,1)S(1)}, u32[]{:S(2)}, u32[]{:S(2)}) async-start(bf16[16,8,1024]{2,1,0:T(8,128)(2,1)} %broadcast_in_dim.7), calls=%async_computation.3 | async-start | bytes 524288 | tf_op jit(solution)/shard_map/all_to_all | solution.py:13
  138.6 35.0 %all-gather.6.cloned.1.call-done = bf16[512,1024]{1,0:T(8,128)(2,1)} async-done(((bf16[32,1024]{1,0:T(8,128)(2,1)}), bf16[512,1024]{1,0:T(8,128)(2,1)}) %all-gather.6.cloned.1.call-update) | async-done | bytes 1048592 | tf_op jit(solution)/shard_map/all_gather | solution.py:52
  173.5 1.4 reduce_sum.46
  175.0 0.2 fusion.8
  175.1 0.0 all-to-all-done.3
  175.2 4.0 %collective-permute-start.2 = (bf16[128,1024]{1,0:T(8,128)(2,1)S(1)}, bf16[128,1024]{1,0:T(8,128)(2,1)S(1)}, u32[]{:S(2)}, u32[]{:S(2)}) collective-permute-start(bf16[128,1024]{1,0:T(8,128)(2,1)S(1)} %bitcast.41), channel_id=1, source_target_pairs={{0,1},{1,0},{2,3},{3,2},{4,5},{5,4},{6,7},{7,6},{8,9},{9,8},{10,11... | collective-permute-start | bytes 786440 | tf_op jit(solution)/shard_map/ppermute | solution.py:23
  179.2 0.2 fusion.5
  179.4 0.2 fusion.10
  179.6 0.7 collective-permute-done.2
  180.3 0.2 fusion.1
  180.5 12.5 %all_to_all.31 = bf16[16,8,1024]{2,1,0:T(8,128)(2,1)S(1)} all-to-all(bf16[16,8,1024]{2,1,0:T(8,128)(2,1)S(1)} %fusion.1), channel_id=1, replica_groups=mesh['y'=4,'x'=4,'z'=16,'core'=2] {'y','x'}, dimensions={0} | all-to-all | bytes 524288 | tf_op jit(solution)/shard_map/all_to_all | solution.py:18
  193.1 10.2 %all_to_all.32 = bf16[16,8,1024]{2,1,0:T(8,128)(2,1)S(1)} all-to-all(bf16[16,8,1024]{2,1,0:T(8,128)(2,1)S(1)} %broadcast_in_dim.8), channel_id=1, replica_groups=mesh['y'=4,'x'=4,'z'=16,'core'=2] {'y','x'}, dimensions={0} | all-to-all | bytes 524288 | tf_op jit(solution)/shard_map/all_to_all | solution.py:13
  203.3 0.7 copy.7
  (7 shorter events, 0.2 us)
Async XLA Ops:
  6.5 88.5 %copy-start = (bf16[2,128,3072]{2,1,0:T(8,128)(2,1)S(1)}, bf16[2,128,3072]{2,1,0:T(8,128)(2,1)}, u32[]{:S(2)}) copy-start(bf16[2,128,3072]{2,1,0:T(8,128)(2,1)} %param.5) | copy-start | bytes 4718596
  6.5 88.5 %all-gather.4.cloned.1.call-start = ((), (), s32[]{:S(2)}) async-start(), calls=%async_computation.6 | async-start | bytes 6684672 | tf_op jit(solution)/shard_map/all_gather | solution.py:37
  47.2 10.6 %collective-permute-start = (bf16[16,128,128]{2,1,0:T(8,128)(2,1)S(1)}, bf16[16,128,128]{2,1,0:T(8,128)(2,1)S(1)}, u32[]{:S(2)}, u32[]{:S(2)}) collective-permute-start(bf16[16,128,128]{2,1,0:T(8,128)(2,1)S(1)} %all_to_all.30), channel_id=1, source_target_pairs={{0,1},{1,0},{2,3},{3,2},{4,5},{5,4},{6,7},{7,6},{8,9},{9,8},{10,11... | collective-permute-start | bytes 1572872 | tf_op jit(solution)/shard_map/ppermute | solution.py:23
  59.5 13.2 %all-to-all-start.1 = ((bf16[4,32,1024]{2,1,0:T(8,128)(2,1)}), bf16[4,32,1024]{2,1,0:T(8,128)(2,1)S(1)}, u32[]{:S(2)}, u32[]{:S(2)}) async-start(bf16[4,32,1024]{2,1,0:T(8,128)(2,1)} %bitcast.7), calls=%async_computation.1 | async-start | bytes 524288 | tf_op jit(solution)/shard_map/all_to_all | solution.py:18
  95.0 19.3 %copy-start.1 = (bf16[2,128,1024]{2,1,0:T(8,128)(2,1)S(1)}, bf16[2,128,1024]{2,1,0:T(8,128)(2,1)}, u32[]{:S(2)}) copy-start(bf16[2,128,1024]{2,1,0:T(8,128)(2,1)} %param.7) | copy-start | bytes 1572868
  99.7 3.7 %collective-permute-start.1 = (bf16[128,1024]{1,0:T(8,128)(2,1)S(1)}, bf16[128,1024]{1,0:T(8,128)(2,1)S(1)}, u32[]{:S(2)}, u32[]{:S(2)}) collective-permute-start(bf16[128,1024]{1,0:T(8,128)(2,1)S(1)} %select_convert_fusion), channel_id=1, source_target_pairs={{0,1},{1,0},{2,3},{3,2},{4,5},{5,4},{6,7},{7,6},{8,9},{9,8},{10,11... | collective-permute-start | bytes 786440 | tf_op jit(solution)/shard_map/ppermute | solution.py:23
  104.3 23.3 %all-to-all-start.2 = ((bf16[16,8,1024]{2,1,0:T(8,128)(2,1)}), bf16[16,8,1024]{2,1,0:T(8,128)(2,1)S(1)}, u32[]{:S(2)}, u32[]{:S(2)}) async-start(bf16[16,8,1024]{2,1,0:T(8,128)(2,1)} %fusion.6), calls=%async_computation.2 | async-start | bytes 524288 | tf_op jit(solution)/shard_map/all_to_all | solution.py:18
  113.6 60.0 %all-gather.6.cloned.1.call-start = ((), (), s32[]{:S(2)}) async-start(), calls=%async_computation.7 | async-start | bytes 1114112 | tf_op jit(solution)/shard_map/all_gather | solution.py:52
  128.4 46.8 %all-to-all-start.3 = ((bf16[16,8,1024]{2,1,0:T(8,128)(2,1)}), bf16[16,8,1024]{2,1,0:T(8,128)(2,1)S(1)}, u32[]{:S(2)}, u32[]{:S(2)}) async-start(bf16[16,8,1024]{2,1,0:T(8,128)(2,1)} %broadcast_in_dim.7), calls=%async_computation.3 | async-start | bytes 524288 | tf_op jit(solution)/shard_map/all_to_all | solution.py:13
  175.2 5.2 %collective-permute-start.2 = (bf16[128,1024]{1,0:T(8,128)(2,1)S(1)}, bf16[128,1024]{1,0:T(8,128)(2,1)S(1)}, u32[]{:S(2)}, u32[]{:S(2)}) collective-permute-start(bf16[128,1024]{1,0:T(8,128)(2,1)S(1)} %bitcast.41), channel_id=1, source_target_pairs={{0,1},{1,0},{2,3},{3,2},{4,5},{5,4},{6,7},{7,6},{8,9},{9,8},{10,11... | collective-permute-start | bytes 786440 | tf_op jit(solution)/shard_map/ppermute | solution.py:23
Sparse Core Ops, SparseCore 0:
  10.4 84.5 all-gather.3
  117.4 56.0 all-gather.5

commit v3 on v2

v3 whole, which is shorter than its diff:
```python
import jax
import jax.numpy as jnp
from jax import lax
from jax.sharding import Mesh, PartitionSpec as P

BF16 = jnp.bfloat16
F32 = jnp.float32
ROW = ("y", "x")
SPLIT = 18


def spread(block, axis, size):
    copies = jnp.broadcast_to(block[None], (size,) + block.shape)
    return lax.all_to_all(copies, axis, 0, 0)


def sum_rows(terms, axis, size):
    rows, cols = terms.shape
    pieces = lax.all_to_all(terms.reshape(size, rows // size, cols), axis, 0, 0)
    return jnp.sum(pieces.astype(F32), axis=0)


def swap_cores(block):
    return lax.ppermute(block, "core", [(0, 1), (1, 0)])


def gather_both_ways(block, n_y, n_x, is_first):
    def place(y, x, core):
        return (y * n_x + x) * 2 + core

    def along_x(core):
        return [[place(y, x, core) for x in range(n_x)] for y in range(n_y)]

    def along_y(core):
        return [[place(y, x, core) for y in range(n_y)] for x in range(n_x)]

    for groups in (along_x(0) + along_y(1), along_y(0) + along_x(1)):
        copies = jnp.broadcast_to(block[None], (len(groups[0]),) + block.shape)
        block = lax.all_to_all(copies, ("y", "x", "core"), 0, 0, axis_index_groups=groups)
    block = jnp.where(is_first, block, jnp.swapaxes(block, 0, 1))
    return block.reshape(-1, block.shape[-1])


def matmul(a, b, contract):
    return lax.dot_general(a, b, ((contract[0:1], contract[1:2]), ((), ())), preferred_element_type=F32)


def make_per_device(n_row, n_y, n_x, n_z):
    def per_device(factor_panel, solved_earlier, right_side, coupling, inverses):
        core = lax.axis_index("core")
        z = lax.axis_index("z")
        _, rows, _ = factor_panel.shape
        own = coupling.shape[1]
        part = rows // n_z
        is_first = core == 0

        depth = solved_earlier.shape[1]
        split = depth * SPLIT // 24
        earlier = lax.all_gather(solved_earlier[:, :split], ROW, axis=0, tiled=True)

        right = jnp.where(is_first, right_side[0], right_side[1])
        right = lax.dynamic_slice_in_dim(right, z * part, part, axis=0)
        packed = jnp.concatenate([coupling.T, inverses[0]], axis=0)
        rest = gather_both_ways(solved_earlier[:, split:], n_y, n_x, core == 0)
        packed, right, is_first, rest = lax.optimization_barrier((packed, right, is_first, rest))

        mine = spread(packed, "z", n_z)
        other = swap_cores(mine)
        left = [
            matmul(inverses[1], part_[:, :own].reshape(-1, rows), (1, 1)).astype(BF16)
            for part_ in (mine, other)
        ]
        left = jnp.concatenate(left, axis=0)
        quarters = lax.all_gather(left, ROW, axis=0, tiled=False)
        panel = factor_panel.reshape(2 * rows, depth)
        rest = matmul(panel[:, split:], rest, (1, 1))
        earlier, _, rest = lax.optimization_barrier((earlier, left, rest))

        terms = (rest + matmul(panel[:, :split], earlier, (1, 1))).reshape(2, rows, -1)
        kept = jnp.where(is_first, terms[0], terms[1])
        sent = jnp.where(is_first, terms[1], terms[0]).astype(BF16)
        kept = (kept + swap_cores(sent).astype(F32)).astype(BF16)
        prefix = sum_rows(kept, "z", n_z)
        residual = (right.astype(F32) - prefix).astype(BF16)
        residual = spread(residual, "z", n_z).reshape(rows, -1)
        residual_other = swap_cores(residual)

        _, quarters = lax.optimization_barrier((residual, quarters))
        left = jnp.sum(quarters.astype(F32), axis=0).astype(BF16).reshape(2, own, -1)
        cross = -(
            matmul(left[0], mine[:, own:].reshape(-1, rows), (1, 0))
            + matmul(left[1], other[:, own:].reshape(-1, rows), (1, 0))
        )
        from_first = jnp.concatenate([inverses[0], cross.astype(BF16)], axis=0)
        from_second = jnp.concatenate([jnp.zeros_like(inverses[1]), inverses[1]], axis=0)
        weights_mine = jnp.where(is_first, from_first, from_second)
        weights_other = jnp.where(is_first, from_second, from_first)
        out = matmul(weights_mine, residual, (1, 0)) + matmul(weights_other, residual_other, (1, 0))
        out = sum_rows(out.astype(BF16), ROW, n_row).astype(BF16)
        return spread(out, ROW, n_row).reshape(2, own, -1)

    return per_device


def solution(mesh):
    n_row, n_col = mesh.shape["row"], mesh.shape["col"]
    n_x = 4
    n_y = n_row // n_x
    n_z = n_col // 2
    split = Mesh(mesh.devices.reshape(n_y, n_x, n_z, 2), ("y", "x", "z", "core"))
    col = ("z", "core")
    return jax.shard_map(
        make_per_device(n_row, n_y, n_x, n_z),
        mesh=split,
        in_specs=(
            P(None, ROW, col),
            P(ROW, col),
            P(None, ROW, None),
            P(ROW, col),
            P(None, col, ROW),
        ),
        out_specs=P(None, col, None),
        check_vma=False,
    )
```

time: 213 us -> 194 us (0.911)
  waiting for transfers between devices: 82.8 us -> 21 us
  blocking collectives: 61.1 us -> 115 us
  starting transfers between devices: 39.2 us -> 25.7 us
  local copies, waits for them, and re-layouts: 2.4 us -> 5.08 us
    all_gather x1, waiting for transfers between devices: 35 us -> 4.5 us  [per_device(): quarters = lax.all_gather(left, ROW, axis=0, tiled=False)]
    all_to_all x1 -> x2, blocking collectives: 12.5 us -> 34.3 us  [sum_rows(): pieces = lax.all_to_all(terms.reshape(size, rows // size, cols), axis, 0, 0)]
    all_gather x1, waiting for transfers between devices: 21.6 us -> 0.02 us  [per_device(): earlier = lax.all_gather(solved_earlier[:, :split], ROW, axis=0, tiled=True)]
    all_to_all x2 -> x3, blocking collectives: 48.6 us -> 70 us  [spread(): return lax.all_to_all(copies, axis, 0, 0)]
    all_to_all x3 -> x1, starting transfers between devices: 23.5 us -> 4.14 us  [gather_both_ways(): lax.all_to_all(copies, ('y', 'x', 'core'), 0, 0, axis_index_groups=groups)]
    all_to_all x0 -> x1, blocking collectives: none -> 11 us  [gather_both_ways(): lax.all_to_all(copies, ('y', 'x', 'core'), 0, 0, axis_index_groups=groups)]
    all_to_all x3 -> x1, waiting for transfers between devices: 22.4 us -> 14 us  [gather_both_ways(): lax.all_to_all(copies, ('y', 'x', 'core'), 0, 0, axis_index_groups=groups)]
    ppermute x3, starting transfers between devices: 15.7 us -> 21.6 us  [swap_cores(): return lax.ppermute(block, 'core', [(0, 1), (1, 0)])]
  transfers between devices with their start and end apart: 8 -> 6, of which waited for: 7 -> 4; matrix products, arithmetic and copies ran while one was open for 4% -> 7% of each run, Pallas kernels for 0% -> 0%
where the time goes in v3:
time: 194 us; the launch traced here: 192 us
  blocking collectives  115 us (59%)
  starting transfers between devices  25.7 us (13%)
  waiting for transfers between devices  21 us (11%)
  between operations  13.6 us (7%)
  matrix products  6.91 us (4%)
  local copies, waits for them, and re-layouts  5.08 us (3%)
  other arithmetic  4.26 us (2%)
    all_to_all x3, blocking collectives, spread(): return lax.all_to_all(copies, axis, 0, 0)  70 us
    all_to_all x2, blocking collectives, sum_rows(): pieces = lax.all_to_all(terms.reshape(size, rows // size, cols), axis, 0, 0)  34.3 us
    ppermute x3, starting transfers between devices, swap_cores(): return lax.ppermute(block, 'core', [(0, 1), (1, 0)])  21.6 us
    all_to_all x1, waiting for transfers between devices, gather_both_ways(): lax.all_to_all(copies, ('y', 'x', 'core'), 0, 0, axis_index_groups=groups)  14 us
    all_to_all x1, blocking collectives, gather_both_ways(): lax.all_to_all(copies, ('y', 'x', 'core'), 0, 0, axis_index_groups=groups)  11 us
    dot_general x8, matrix products, matmul(): lax.dot_general(a, b, ((contract[0:1], contract[1:2]), ((), ())), preferr...  6.91 us
    all_gather x1, waiting for transfers between devices, per_device(): quarters = lax.all_gather(left, ROW, axis=0, tiled=False)  4.5 us
    all_to_all x1, starting transfers between devices, gather_both_ways(): lax.all_to_all(copies, ('y', 'x', 'core'), 0, 0, axis_index_groups=groups)  4.14 us
  transfers between devices with their start and end apart: 6, of which 4 were waited for; matrix products, arithmetic and copies ran while one was open for 7% of the time, Pallas kernels for 0%

profile of v3, /device:TPU:1, one launch (start us, length us, event | category | flops | bytes accessed | tf_op | source)
XLA Modules:
  0.0 191.8 jit_solution(206304609758571121)
XLA Ops:
  6.5 0.0 all-gather.4.cloned.1.call-start
  6.5 1.7 slice.61
  8.3 0.0 all-gather.4.cloned.1.call-update
  8.3 0.9 slice.60
  9.2 11.0 %all_to_all.35 = bf16[4,64,768]{2,1,0:T(8,128)(2,1)S(1)} all-to-all(bf16[4,64,768]{2,1,0:T(8,128)(2,1)S(1)} %broadcast_in_dim.10), channel_id=1, replica_groups={{0,32,64,96},{128,160,192,224},{256,288,320,352},{384,416,448,480},{1,1..., dimensions={0} | all-to-all | bytes 786432 | tf_op jit(solution)/shard_map/all_to_all | solution.py:39
  20.3 1.3 broadcast_in_dim.11
  21.6 0.0 copy-start
  21.6 0.0 copy-start.1
  21.6 0.0 copy-start.2
  21.6 4.1 %all-to-all-start.1 = ((bf16[4,4,64,768]{3,2,1,0:T(8,128)(2,1)}), bf16[4,4,64,768]{3,2,1,0:T(8,128)(2,1)S(1)}, u32[]{:S(2)}, u32[]{:S(2)}) async-start(bf16[4,4,64,768]{3,2,1,0:T(8,128)(2,1)} %broadcast_in_dim.11), calls=%async_computation.1 | async-start | bytes 3145728 | tf_op jit(solution)/shard_map/all_to_all | solution.py:39
  25.7 0.0 all-gather.6.cloned.1.call-start
  25.7 0.0 copy-done
  25.8 0.0 copy-done.1
  25.8 0.0 copy-done.2
  25.9 14.0 %all-to-all-done.1 = bf16[4,4,64,768]{3,2,1,0:T(8,128)(2,1)S(1)} async-done(((bf16[4,4,64,768]{3,2,1,0:T(8,128)(2,1)}), bf16[4,4,64,768]{3,2,1,0:T(8,128)(2,1)S(1)}, u32[]{:S(2)}, u32[]{:S(2)}) %all-to-all-start.1) | async-done | bytes 1572896 | tf_op jit(solution)/shard_map/all_to_all | solution.py:39
  39.9 0.1 bitcast_select_fusion
  40.0 0.1 broadcast_in_dim.12
  40.1 36.1 %all_to_all.36 = bf16[16,128,128]{2,1,0:T(8,128)(2,1)S(1)} all-to-all(bf16[16,128,128]{2,1,0:T(8,128)(2,1)S(1)} %broadcast_in_dim.12), channel_id=1, replica_groups=mesh['y'=4,'x'=4,'z'=16,'core'=2] {'z'}, dimensions={0} | all-to-all | bytes 1048576 | tf_op jit(solution)/shard_map/all_to_all | solution.py:14
  76.2 11.6 %collective-permute-start = (bf16[16,128,128]{2,1,0:T(8,128)(2,1)S(1)}, bf16[16,128,128]{2,1,0:T(8,128)(2,1)S(1)}, u32[]{:S(2)}, u32[]{:S(2)}) collective-permute-start(bf16[16,128,128]{2,1,0:T(8,128)(2,1)S(1)} %all_to_all.36), channel_id=1, source_target_pairs={{0,1},{1,0},{2,3},{3,2},{4,5},{5,4},{6,7},{7,6},{8,9},{9,8},{10,11... | collective-permute-start | bytes 1572872 | tf_op jit(solution)/shard_map/ppermute | solution.py:24
  87.8 0.2 fusion.4
  88.1 1.3 collective-permute-done
  89.4 0.2 fusion.5
  89.6 0.7 pad_maximum_fusion
  90.3 0.0 all-gather.6.cloned.1.call-update
  90.3 1.6 convolution_bitcast_fusion.1
  91.9 0.0 all-gather.4.cloned.1.call-done
  92.0 4.1 %fusion = f32[256,1024]{0,1:T(8,128)S(1)} fusion(f32[256,1024]{0,1:T(8,128)S(1)} %convolution_bitcast_fusion.1, bf16[1024,2304]{1,0:T(8,128)(2,1)} %all-gather.4.cloned.1.call-done, bf16[256,3072]{1,0:T(8,128)(2,1)} %bitcast.52), kind=kOutput, calls=%fused_computation.3 | convolution fusion | flops 1208221696 | bytes 7995392 | tf_op jit(solution)/shard_map/dot_general | solution.py:45
  96.1 2.3 %collective-permute-start.1 = (bf16[128,1024]{0,1:T(8,128)(2,1)S(1)}, bf16[128,1024]{0,1:T(8,128)(2,1)S(1)}, u32[]{:S(2)}, u32[]{:S(2)}) collective-permute-start(bf16[128,1024]{0,1:T(8,128)(2,1)S(1)} %select_convert_fusion), channel_id=1, source_target_pairs={{0,1},{1,0},{2,3},{3,2},{4,5},{5,4},{6,7},{7,6},{8,9},{9,8},{10,11... | collective-permute-start | bytes 786440 | tf_op jit(solution)/shard_map/ppermute | solution.py:24
  98.4 1.1 collective-permute-done.1
  99.6 0.1 add_convert_fusion
  99.7 0.1 copy.13
  99.8 22.0 %all_to_all.37 = bf16[16,8,1024]{2,1,0:T(8,128)(2,1)S(1)} all-to-all(bf16[16,8,1024]{2,1,0:T(8,128)(2,1)S(1)} %bitcast.45), channel_id=1, replica_groups=mesh['y'=4,'x'=4,'z'=16,'core'=2] {'z'}, dimensions={0} | all-to-all | bytes 524288 | tf_op jit(solution)/shard_map/all_to_all | solution.py:19
  121.9 23.4 %all_to_all.38 = bf16[16,8,1024]{2,1,0:T(8,128)(2,1)S(1)} all-to-all(bf16[16,8,1024]{2,1,0:T(8,128)(2,1)S(1)} %broadcast_in_dim.13), channel_id=1, replica_groups=mesh['y'=4,'x'=4,'z'=16,'core'=2] {'z'}, dimensions={0} | all-to-all | bytes 524288 | tf_op jit(solution)/shard_map/all_to_all | solution.py:14
  145.3 7.6 %collective-permute-start.2 = (bf16[128,1024]{1,0:T(8,128)(2,1)S(1)}, bf16[128,1024]{1,0:T(8,128)(2,1)S(1)}, u32[]{:S(2)}, u32[]{:S(2)}) collective-permute-start(bf16[128,1024]{1,0:T(8,128)(2,1)S(1)} %bitcast.44), channel_id=1, source_target_pairs={{0,1},{1,0},{2,3},{3,2},{4,5},{5,4},{6,7},{7,6},{8,9},{9,8},{10,11... | collective-permute-start | bytes 786440 | tf_op jit(solution)/shard_map/ppermute | solution.py:24
  153.0 4.5 %all-gather.6.cloned.1.call-done = bf16[2048,1024]{1,0:T(8,128)(2,1)} async-done(((bf16[128,1024]{1,0:T(8,128)(2,1)}), bf16[2048,1024]{1,0:T(8,128)(2,1)}) %all-gather.6.cloned.1.call-update) | async-done | bytes 4194320 | tf_op jit(solution)/shard_map/all_gather | solution.py:74
  157.5 3.1 %reduce_sum.34 = bf16[128,1024]{1,0:T(8,128)(2,1)S(1)} reduce(bf16[16,128,1024]{2,1,0:T(8,128)(2,1)} %bitcast.43, bf16[]{:T(256)} %constant.20.clone.1), dimensions={0}, to_apply=%region_1.2 | reduce | flops 1966080 | bytes 4456450 | tf_op jit(solution)/shard_map/reduce_sum | solution.py:89
  160.6 0.2 fusion.10
  160.8 0.2 fusion.7
  161.0 0.2 fusion.12
  161.2 0.0 collective-permute-done.2
  161.2 0.2 fusion.3
  161.4 12.3 %all_to_all.39 = bf16[16,8,1024]{2,1,0:T(8,128)(2,1)S(1)} all-to-all(bf16[16,8,1024]{2,1,0:T(8,128)(2,1)S(1)} %fusion.3), channel_id=1, replica_groups=mesh['y'=4,'x'=4,'z'=16,'core'=2] {'y','x'}, dimensions={0} | all-to-all | bytes 524288 | tf_op jit(solution)/shard_map/all_to_all | solution.py:19
  173.8 10.5 %all_to_all.40 = bf16[16,8,1024]{2,1,0:T(8,128)(2,1)S(1)} all-to-all(bf16[16,8,1024]{2,1,0:T(8,128)(2,1)S(1)} %broadcast_in_dim.14), channel_id=1, replica_groups=mesh['y'=4,'x'=4,'z'=16,'core'=2] {'y','x'}, dimensions={0} | all-to-all | bytes 524288 | tf_op jit(solution)/shard_map/all_to_all | solution.py:14
  184.3 0.7 copy.17
  (13 shorter events, 0.3 us)
Async XLA Ops:
  6.5 85.4 %all-gather.4.cloned.1.call-start = ((), (), s32[]{:S(2)}) async-start(), calls=%async_computation.7 | async-start | bytes 5013504 | tf_op jit(solution)/shard_map/all_gather | solution.py:59
  21.6 4.2 %copy-start = (bf16[2,128,1024]{2,1,0:T(8,128)(2,1)S(1)}, bf16[2,128,1024]{2,1,0:T(8,128)(2,1)}, u32[]{:S(2)}) copy-start(bf16[2,128,1024]{2,1,0:T(8,128)(2,1)} %param.7) | copy-start | bytes 1572868
  21.6 4.2 %copy-start.1 = (bf16[2,64,128]{2,1,0:T(8,128)(2,1)S(1)}, bf16[2,64,128]{2,1,0:T(8,128)(2,1)}, u32[]{:S(2)}) copy-start(bf16[2,64,128]{2,1,0:T(8,128)(2,1)} %param.9) | copy-start | bytes 98308
  21.6 4.2 %copy-start.2 = (bf16[128,64]{0,1:T(8,128)(2,1)S(1)}, bf16[128,64]{0,1:T(8,128)(2,1)}, u32[]{:S(2)}) copy-start(bf16[128,64]{0,1:T(8,128)(2,1)} %param.8) | copy-start | bytes 49156
  21.6 18.3 %all-to-all-start.1 = ((bf16[4,4,64,768]{3,2,1,0:T(8,128)(2,1)}), bf16[4,4,64,768]{3,2,1,0:T(8,128)(2,1)S(1)}, u32[]{:S(2)}, u32[]{:S(2)}) async-start(bf16[4,4,64,768]{3,2,1,0:T(8,128)(2,1)} %broadcast_in_dim.11), calls=%async_computation.1 | async-start | bytes 3145728 | tf_op jit(solution)/shard_map/all_to_all | solution.py:39
  25.7 131.7 %all-gather.6.cloned.1.call-start = ((), (), s32[]{:S(2)}) async-start(), calls=%async_computation.8 | async-start | bytes 4456448 | tf_op jit(solution)/shard_map/all_gather | solution.py:74
  76.2 13.2 %collective-permute-start = (bf16[16,128,128]{2,1,0:T(8,128)(2,1)S(1)}, bf16[16,128,128]{2,1,0:T(8,128)(2,1)S(1)}, u32[]{:S(2)}, u32[]{:S(2)}) collective-permute-start(bf16[16,128,128]{2,1,0:T(8,128)(2,1)S(1)} %all_to_all.36), channel_id=1, source_target_pairs={{0,1},{1,0},{2,3},{3,2},{4,5},{5,4},{6,7},{7,6},{8,9},{9,8},{10,11... | collective-permute-start | bytes 1572872 | tf_op jit(solution)/shard_map/ppermute | solution.py:24
  96.1 3.4 %collective-permute-start.1 = (bf16[128,1024]{0,1:T(8,128)(2,1)S(1)}, bf16[128,1024]{0,1:T(8,128)(2,1)S(1)}, u32[]{:S(2)}, u32[]{:S(2)}) collective-permute-start(bf16[128,1024]{0,1:T(8,128)(2,1)S(1)} %select_convert_fusion), channel_id=1, source_target_pairs={{0,1},{1,0},{2,3},{3,2},{4,5},{5,4},{6,7},{7,6},{8,9},{9,8},{10,11... | collective-permute-start | bytes 786440 | tf_op jit(solution)/shard_map/ppermute | solution.py:24
  145.3 15.9 %collective-permute-start.2 = (bf16[128,1024]{1,0:T(8,128)(2,1)S(1)}, bf16[128,1024]{1,0:T(8,128)(2,1)S(1)}, u32[]{:S(2)}, u32[]{:S(2)}) collective-permute-start(bf16[128,1024]{1,0:T(8,128)(2,1)S(1)} %bitcast.44), channel_id=1, source_target_pairs={{0,1},{1,0},{2,3},{3,2},{4,5},{5,4},{6,7},{7,6},{8,9},{9,8},{10,11... | collective-permute-start | bytes 786440 | tf_op jit(solution)/shard_map/ppermute | solution.py:24
Sparse Core Ops, SparseCore 0:
  10.4 77.3 all-gather.3
  90.8 66.6 all-gather.5

commit v4 on v0

v4 whole, which is shorter than its diff:
```python
import jax
import jax.numpy as jnp
from jax import lax
from jax.sharding import Mesh, PartitionSpec as P

BF16 = jnp.bfloat16
F32 = jnp.float32
ROW = ("y", "x")
COL = ("z", "core")
PLANE = ("y", "x", "core")


def spread(block, axis, size, groups=None):
    copies = jnp.broadcast_to(block[None], (size,) + block.shape)
    return lax.all_to_all(copies, axis, 0, 0, axis_index_groups=groups)


def gather_both_ways(block, n_y, n_x):
    def place(y, x, core):
        return (y * n_x + x) * 2 + core

    def along_x(core):
        return [[place(y, x, core) for x in range(n_x)] for y in range(n_y)]

    def along_y(core):
        return [[place(y, x, core) for y in range(n_y)] for x in range(n_x)]

    for groups in (along_x(0) + along_y(1), along_y(0) + along_x(1)):
        block = spread(block, PLANE, n_x, groups)
    return block


def swap_cores(block):
    return lax.ppermute(block, "core", [(0, 1), (1, 0)])


def times_transposed(a, b):
    return lax.dot_general(a, b, (((1,), (1,)), ((), ())), preferred_element_type=F32)


def make_per_device(n_y, n_x, n_z):
    n_row = n_y * n_x

    def per_device(factor_panel, solved_earlier, right_side, coupling, inverses):
        core = lax.axis_index("core")
        z = lax.axis_index("z")
        is_first = core == 0
        blocks, rows, depth = factor_panel.shape
        rhs = right_side.shape[2]
        own = coupling.shape[1]
        step = 2 * own // n_row
        width = rhs // (2 * n_z)

        packed = jnp.concatenate([coupling.T, inverses[0], inverses[1]], axis=0)
        factors = lax.all_gather(packed, COL, axis=0, tiled=False)

        wanted = core * (rhs // 2) + z * width + lax.broadcasted_iota(jnp.int32, (width, rhs), 0)
        pick = (wanted == lax.broadcasted_iota(jnp.int32, (width, rhs), 1)).astype(BF16)
        right = times_transposed(pick, right_side.reshape(blocks * rows, rhs))

        def gather(block):
            return gather_both_ways(block, n_y, n_x)

        def gather_halves(block):
            return jnp.concatenate([gather(half_) for half_ in jnp.split(block, 2, axis=1)], axis=-1)

        earlier = lax.cond(z < n_z, gather, gather_halves, solved_earlier).reshape(-1, depth)
        earlier, right, is_first = lax.optimization_barrier((earlier, right, is_first))

        terms = times_transposed(earlier, factor_panel.reshape(blocks * rows, depth))
        terms = terms.reshape(n_y, n_x, -1, blocks * rows)
        turned = jnp.swapaxes(terms, 0, 1)
        half = n_y // 2
        kept = jnp.where(is_first, terms[:half], turned[half:])
        sent = jnp.where(is_first, terms[half:], turned[:half]).astype(BF16)
        kept = (kept + swap_cores(sent).astype(F32)).astype(BF16)
        prefix = lax.all_to_all(kept.reshape(n_z, width, blocks * rows), "z", 0, 0)
        prefix, factors = lax.optimization_barrier((prefix, factors))
        prefix = jnp.sum(prefix.astype(F32), axis=0)

        factors = factors.reshape(n_z, 2, 3, n_row // 2, step, rows)
        factors = factors.transpose(2, 1, 3, 0, 4, 5).reshape(3, n_row * n_z * step, rows)

        def solve(residual, inverse):
            terms = times_transposed(residual, inverse).astype(BF16)
            terms = terms.reshape(width, n_row, -1).transpose(1, 0, 2)
            terms = lax.all_to_all(terms, ROW, 0, 0)
            return jnp.sum(terms.astype(F32), axis=0).astype(BF16)

        residual_first = (right[:, :rows] - prefix[:, :rows]).astype(BF16)
        first = solve(residual_first, factors[1])
        all_first = spread(first, ROW, n_row).transpose(1, 0, 2).reshape(width, -1)
        cross = jnp.dot(all_first, factors[0], preferred_element_type=F32)
        residual_second = (right[:, rows:] - (prefix[:, rows:] + cross)).astype(BF16)
        second = solve(residual_second, factors[2])

        solved = jnp.stack([first.T, second.T]).reshape(2, n_z, step, width)
        solved = solved.transpose(1, 0, 2, 3).reshape(n_z, 2 * step, width)
        solved = lax.all_to_all(solved, "z", 0, 0)
        solved = solved.transpose(1, 0, 2).reshape(2 * step, rhs // 2)
        solved = spread(solved, PLANE, 2 * n_row)
        solved = solved.reshape(2, n_row // 2, 2, 2, step, rhs // 2)
        solved = jnp.where(is_first, solved[0], solved[1])
        return solved.transpose(2, 0, 3, 1, 4).reshape(2, own, rhs)

    return per_device


def solution(mesh):
    n_row, n_col = mesh.shape["row"], mesh.shape["col"]
    n_x = 4
    n_y = n_row // n_x
    n_z = n_col // 2
    split = Mesh(mesh.devices.reshape(n_y, n_x, n_z, 2), ("y", "x", "z", "core"))
    return jax.shard_map(
        make_per_device(n_y, n_x, n_z),
        mesh=split,
        in_specs=(
            P(None, ROW, COL),
            P(ROW, COL),
            P(None, ROW, None),
            P(ROW, COL),
            P(None, COL, ROW),
        ),
        out_specs=P(None, COL, None),
        check_vma=False,
    )
```

time: 671 us -> 196 us (0.29)
  waiting for transfers between devices: 620 us -> 14.4 us
  blocking collectives: 19.5 us -> 137 us
  starting transfers between devices: 0.17 us -> 15.1 us
  local copies, waits for them, and re-layouts: 0.02 us -> 8.06 us
  matrix products: 12.7 us -> 5.58 us
    psum x2 -> x0, waiting for transfers between devices: 418 us -> none  [the longest x1 210 us: per_device(): summed = lax.psum(partial_terms, 'col')]
    all_gather x3 -> x1, waiting for transfers between devices: 201 us -> 0.01 us  [per_device(): factors = lax.all_gather(packed, COL, axis=0, tiled=False)]
    all_to_all x0 -> x6, blocking collectives: none -> 137 us  [the longest x3 79.9 us: spread(): return lax.all_to_all(copies, axis, 0, 0, axis_index_groups=groups)]
    all_gather x1 -> x0, blocking collectives: 19.5 us -> none  [per_device(): whole_inverses = lax.all_gather(inverses, 'row', axis=2, tiled=True)]
    all_to_all x0 -> x2, waiting for transfers between devices: none -> 13.2 us  [the longest x1 6.68 us: solve(): terms = lax.all_to_all(terms, ROW, 0, 0)]
    ppermute x0 -> x1, starting transfers between devices: none -> 8.09 us  [swap_cores(): return lax.ppermute(block, 'core', [(0, 1), (1, 0)])]
    dot_general x4, matrix products: 12.7 us -> 5.58 us  [times_transposed(): lax.dot_general(a, b, (((1,), (1,)), ((), ())), preferred_element_type=F32)]
    all_to_all x0 -> x2, starting transfers between devices: none -> 7.03 us  [the longest x1 3.51 us: spread(): return lax.all_to_all(copies, axis, 0, 0, axis_index_groups=groups)]
  transfers between devices with their start and end apart: 5 -> 4, of which waited for: 5 -> 3; matrix products, arithmetic and copies ran while one was open for 0% -> 4% of each run, Pallas kernels for 0% -> 0%
where the time goes in v4:
time: 196 us; the launch traced here: 195 us
  blocking collectives  137 us (70%)
  starting transfers between devices  15.1 us (8%)
  waiting for transfers between devices  14.4 us (7%)
  between operations  13.6 us (7%)
  local copies, waits for them, and re-layouts  8.06 us (4%)
  matrix products  5.58 us (3%)
    all_to_all x3, blocking collectives, spread(): return lax.all_to_all(copies, axis, 0, 0, axis_index_groups=groups)  79.9 us
    all_to_all x1, blocking collectives, per_device(): prefix = lax.all_to_all(kept.reshape(n_z, width, blocks * rows), 'z', 0, 0)  25.8 us
    all_to_all x1, blocking collectives, per_device(): solved = lax.all_to_all(solved, 'z', 0, 0)  21.4 us
    all_to_all x1, blocking collectives, solve(): terms = lax.all_to_all(terms, ROW, 0, 0)  9.52 us
    ppermute x1, starting transfers between devices, swap_cores(): return lax.ppermute(block, 'core', [(0, 1), (1, 0)])  8.09 us
    all_to_all x1, waiting for transfers between devices, solve(): terms = lax.all_to_all(terms, ROW, 0, 0)  6.68 us
    all_to_all x1, waiting for transfers between devices, spread(): return lax.all_to_all(copies, axis, 0, 0, axis_index_groups=groups)  6.55 us
    dot_general x4, matrix products, times_transposed(): lax.dot_general(a, b, (((1,), (1,)), ((), ())), preferred_element_type=F32)  5.58 us
  transfers between devices with their start and end apart: 4, of which 3 were waited for; matrix products, arithmetic and copies ran while one was open for 4% of the time, Pallas kernels for 0%

profile of v4, /device:TPU:1, one launch (start us, length us, event | category | flops | bytes accessed | tf_op | source)
XLA Modules:
  0.0 194.9 jit_solution(6179249469936907500)
XLA Ops:
  6.5 0.0 copy-start
  6.5 0.0 all-gather.3.cloned.1.call-start
  6.5 0.9 slice_bitcast_fusion.1
  7.4 1.3 pad_maximum_fusion.1
  8.7 0.0 all-gather.3.cloned.1.call-update
  8.8 0.0 copy-start.1
  8.8 61.4 %conditional.1 = (bf16[1024,3072]{1,0:T(8,128)(2,1)}) conditional(s32[]{:T(128)} %convert_element_type.32, bf16[64,3072]{1,0:T(8,128)(2,1)} %param.8, bf16[64,3072]{1,0:T(8,128)(2,1)} %param.8), branch_computations={%region_0.0_spmd, %region_1.0_spmd} | conditional | bytes 38928392 | solution.py:67
  8.8 1.2 broadcast_in_dim.12
  10.0 17.7 %all_to_all.58 = bf16[4,64,3072]{2,1,0:T(8,128)(2,1)S(1)} all-to-all(bf16[4,64,3072]{2,1,0:T(8,128)(2,1)S(1)} %broadcast_in_dim.12), channel_id=1, replica_groups={{0,32,64,96},{128,160,192,224},{256,288,320,352},{384,416,448,480},{1,1..., dimensions={0} | all-to-all | bytes 3145728 | tf_op jit(solution)/shard_map/cond/branch_1_fun/all_to_all | solution.py:15
  27.7 0.8 broadcast_in_dim.13
  28.5 41.8 %all_to_all.59 = bf16[4,4,64,3072]{3,2,1,0:T(8,128)(2,1)} all-to-all(bf16[4,4,64,3072]{3,2,1,0:T(8,128)(2,1)S(1)} %broadcast_in_dim.13), channel_id=1, replica_groups={{0,128,256,384},{32,160,288,416},{64,192,320,448},{96,224,352,480},{1,3..., dimensions={0} | all-to-all | bytes 12582912 | tf_op jit(solution)/shard_map/cond/branch_1_fun/all_to_all | solution.py:15
  70.2 0.0 copy-done.1
  70.2 0.2 fusion.11
  70.5 0.0 copy-done
  70.5 4.6 %fusion.19 = f32[1024,256]{1,0:T(8,128)S(1)} fusion(bf16[1024,3072]{1,0:T(8,128)(2,1)} %get-tuple-element.28, bf16[256,3072]{1,0:T(8,128)(2,1)S(1)} %bitcast.68), kind=kOutput, calls=%fused_computation.35 | convolution fusion | flops 1610612736 | bytes 8912896 | tf_op jit(solution)/shard_map/dot_general | solution.py:38
  75.2 0.1 copy.52
  75.3 8.1 %collective-permute-start = (bf16[2,4,64,256]{3,2,1,0:T(8,128)(2,1)S(1)}, bf16[2,4,64,256]{3,2,1,0:T(8,128)(2,1)S(1)}, u32[]{:S(2)}, u32[]{:S(2)}) collective-permute-start(bf16[2,4,64,256]{3,2,1,0:T(8,128)(2,1)S(1)} %fusion.4), channel_id=1, source_target_pairs={{0,1},{1,0},{2,3},{3,2},{4,5},{5,4},{6,7},{7,6},{8,9},{9,8},{10,11... | collective-permute-start | bytes 786440 | tf_op jit(solution)/shard_map/ppermute | solution.py:34
  83.4 1.1 collective-permute-done
  84.5 0.1 fusion.6
  84.6 25.8 %all_to_all.60 = bf16[16,32,256]{2,1,0:T(8,128)(2,1)S(1)} all-to-all(bf16[16,32,256]{2,1,0:T(8,128)(2,1)S(1)} %bitcast.79), channel_id=1, replica_groups=mesh['y'=4,'x'=4,'z'=16,'core'=2] {'z'}, dimensions={0} | all-to-all | bytes 524288 | tf_op jit(solution)/shard_map/all_to_all | solution.py:77
  110.4 0.0 all-gather.3.cloned.1.call-done
  110.4 1.5 fusion.18
  112.0 0.1 copy.25
  112.1 0.3 fusion
  112.4 9.5 %all_to_all.61 = bf16[16,32,128]{2,1,0:T(8,128)(2,1)S(1)} all-to-all(bf16[16,32,128]{2,1,0:T(8,128)(2,1)S(1)} %bitcast.83), channel_id=1, replica_groups=mesh['y'=4,'x'=4,'z'=16,'core'=2] {'y','x'}, dimensions={0} | all-to-all | bytes 262144 | tf_op jit(solution)/shard_map/all_to_all | solution.py:87
  122.0 0.7 broadcast_in_dim.34
  122.6 3.5 %all-to-all-start.8 = ((bf16[16,32,128]{2,1,0:T(8,128)(2,1)}), bf16[16,32,128]{2,1,0:T(8,128)(2,1)S(1)}, u32[]{:S(2)}, u32[]{:S(2)}) async-start(bf16[16,32,128]{2,1,0:T(8,128)(2,1)} %broadcast_in_dim.34), calls=%async_computation.8 | async-start | bytes 262144 | tf_op jit(solution)/shard_map/all_to_all | solution.py:15
  126.2 0.1 copy.31
  126.3 0.1 copy.30
  126.4 6.6 %all-to-all-done.8 = bf16[16,32,128]{2,1,0:T(8,128)(2,1)S(1)} async-done(((bf16[16,32,128]{2,1,0:T(8,128)(2,1)}), bf16[16,32,128]{2,1,0:T(8,128)(2,1)S(1)}, u32[]{:S(2)}, u32[]{:S(2)}) %all-to-all-start.8) | async-done | bytes 131104 | tf_op jit(solution)/shard_map/all_to_all | solution.py:15
  133.0 0.4 fusion.1
  133.4 0.7 copy.53
  134.1 3.5 %all-to-all-start.9 = ((bf16[16,32,128]{2,1,0:T(8,128)(2,1)}), bf16[16,32,128]{2,1,0:T(8,128)(2,1)S(1)}, u32[]{:S(2)}, u32[]{:S(2)}) async-start(bf16[16,32,128]{2,1,0:T(8,128)(2,1)} %bitcast.65), calls=%async_computation.9 | async-start | bytes 262144 | tf_op jit(solution)/shard_map/all_to_all | solution.py:87
  137.6 0.1 copy.28
  137.7 6.7 %all-to-all-done.9 = bf16[16,32,128]{2,1,0:T(8,128)(2,1)S(1)} async-done(((bf16[16,32,128]{2,1,0:T(8,128)(2,1)}), bf16[16,32,128]{2,1,0:T(8,128)(2,1)S(1)}, u32[]{:S(2)}, u32[]{:S(2)}) %all-to-all-start.9) | async-done | bytes 131104 | tf_op jit(solution)/shard_map/all_to_all | solution.py:87
  144.5 0.1 copy.34
  144.6 0.1 reshape.77
  144.7 21.4 %all_to_all.62 = bf16[16,2,256]{2,1,0:T(2,128)(2,1)S(1)} all-to-all(bf16[16,2,256]{2,1,0:T(2,128)(2,1)S(1)} %reshape.77), channel_id=1, replica_groups=mesh['y'=4,'x'=4,'z'=16,'core'=2] {'z'}, dimensions={0} | all-to-all | bytes 32768 | tf_op jit(solution)/shard_map/all_to_all | solution.py:99
  166.1 0.1 reshape.78
  166.2 0.1 broadcast_in_dim.35
  166.3 0.1 broadcast_in_dim.36
  166.4 20.4 %all_to_all.63 = bf16[32,16,512]{2,1,0:T(8,128)(2,1)S(1)} all-to-all(bf16[32,16,512]{2,1,0:T(8,128)(2,1)S(1)} %broadcast_in_dim.36), channel_id=1, replica_groups=mesh['y'=4,'x'=4,'z'=16,'core'=2] {'y','x','core'}, dimensions={0} | all-to-all | bytes 1048576 | tf_op jit(solution)/shard_map/all_to_all | solution.py:15
  186.9 0.3 copy.37
  187.2 0.9 reshape.75
  (11 shorter events, 0.3 us)
Async XLA Ops:
  6.5 64.0 %copy-start = (bf16[2,128,3072]{2,1,0:T(8,128)(2,1)S(1)}, bf16[2,128,3072]{2,1,0:T(8,128)(2,1)}, u32[]{:S(2)}) copy-start(bf16[2,128,3072]{2,1,0:T(8,128)(2,1)} %param.7) | copy-start | bytes 4718596
  6.5 103.9 %all-gather.3.cloned.1.call-start = ((), (), s32[]{:S(2)}) async-start(), calls=%async_computation.12 | async-start | bytes 1622016 | tf_op jit(solution)/shard_map/all_gather | solution.py:55
  8.8 61.5 %copy-start.1 = (bf16[2,128,1024]{2,1,0:T(8,128)(2,1)S(1)}, bf16[2,128,1024]{2,1,0:T(8,128)(2,1)}, u32[]{:S(2)}) copy-start(bf16[2,128,1024]{2,1,0:T(8,128)(2,1)} %param.9) | copy-start | bytes 1572868
  75.3 9.2 %collective-permute-start = (bf16[2,4,64,256]{3,2,1,0:T(8,128)(2,1)S(1)}, bf16[2,4,64,256]{3,2,1,0:T(8,128)(2,1)S(1)}, u32[]{:S(2)}, u32[]{:S(2)}) collective-permute-start(bf16[2,4,64,256]{3,2,1,0:T(8,128)(2,1)S(1)} %fusion.4), channel_id=1, source_target_pairs={{0,1},{1,0},{2,3},{3,2},{4,5},{5,4},{6,7},{7,6},{8,9},{9,8},{10,11... | collective-permute-start | bytes 786440 | tf_op jit(solution)/shard_map/ppermute | solution.py:34
  122.6 10.3 %all-to-all-start.8 = ((bf16[16,32,128]{2,1,0:T(8,128)(2,1)}), bf16[16,32,128]{2,1,0:T(8,128)(2,1)S(1)}, u32[]{:S(2)}, u32[]{:S(2)}) async-start(bf16[16,32,128]{2,1,0:T(8,128)(2,1)} %broadcast_in_dim.34), calls=%async_computation.8 | async-start | bytes 262144 | tf_op jit(solution)/shard_map/all_to_all | solution.py:15
  134.1 10.3 %all-to-all-start.9 = ((bf16[16,32,128]{2,1,0:T(8,128)(2,1)}), bf16[16,32,128]{2,1,0:T(8,128)(2,1)S(1)}, u32[]{:S(2)}, u32[]{:S(2)}) async-start(bf16[16,32,128]{2,1,0:T(8,128)(2,1)} %bitcast.65), calls=%async_computation.9 | async-start | bytes 262144 | tf_op jit(solution)/shard_map/all_to_all | solution.py:87
Sparse Core Ops, SparseCore 0:
  9.5 77.0 all-gather.2

commit v5 on v3

--- a/solution.py
+++ b/solution.py
@@ -1,12 +1,14 @@
 import jax
 import jax.numpy as jnp
 from jax import lax
+from jax.experimental import pallas as pl
+from jax.experimental.pallas import tpu as pltpu
 from jax.sharding import Mesh, PartitionSpec as P
 
 BF16 = jnp.bfloat16
 F32 = jnp.float32
 ROW = ("y", "x")
-SPLIT = 18
+SPLIT = 20
 
 
 def spread(block, axis, size):
@@ -45,6 +47,37 @@
     return lax.dot_general(a, b, ((contract[0:1], contract[1:2]), ((), ())), preferred_element_type=F32)
 
 
+def add_terms(terms_ref, out_ref, total_ref):
+    @pl.when(pl.program_id(0) == 0)
+    def _():
+        total_ref[...] = jnp.zeros_like(total_ref)
+
+    total = total_ref[...]
+    for i in range(terms_ref.shape[0]):
+        total += terms_ref[i].astype(F32)
+    total_ref[...] = total
+
+    @pl.when(pl.program_id(0) == pl.num_programs(0) - 1)
+    def _():
+        out_ref[...] = total_ref[...].astype(BF16)
+
+
+def sum_terms(terms, at_once):
+    count, rows, cols = terms.shape
+    return pl.pallas_call(
+        add_terms,
+        grid=(count // at_once,),
+        in_specs=[pl.BlockSpec((at_once, rows, cols), lambda i: (i, 0, 0))],
+        out_specs=pl.BlockSpec((rows, cols), lambda i: (0, 0)),
+        out_shape=jax.ShapeDtypeStruct((rows, cols), BF16),
+        scratch_shapes=[pltpu.VMEM((rows, cols), F32)],
+        compiler_params=pltpu.CompilerParams(vmem_limit_bytes=32 * 2**20),
+        cost_estimate=pl.CostEstimate(
+            flops=count * rows * cols, bytes_accessed=2 * (count + 1) * rows * cols, transcendentals=0
+        ),
+    )(terms)
+
+
 def make_per_device(n_row, n_y, n_x, n_z):
     def per_device(factor_panel, solved_earlier, right_side, coupling, inverses):
         core = lax.axis_index("core")
@@ -70,7 +103,10 @@
             matmul(inverses[1], part_[:, :own].reshape(-1, rows), (1, 1)).astype(BF16)
             for part_ in (mine, other)
         ]
-        left = jnp.concatenate(left, axis=0)
+        even = lax.axis_index("x") % 2 == 0
+        pairs = [(x, x ^ 1) for x in range(n_x)]
+        received = lax.ppermute(jnp.where(even, left[1], left[0]), "x", pairs)
+        left = (jnp.where(even, left[0], left[1]).astype(F32) + received.astype(F32)).astype(BF16)
         quarters = lax.all_gather(left, ROW, axis=0, tiled=False)
         panel = factor_panel.reshape(2 * rows, depth)
         rest = matmul(panel[:, split:], rest, (1, 1))
@@ -86,7 +122,7 @@
         residual_other = swap_cores(residual)
 
         _, quarters = lax.optimization_barrier((residual, quarters))
-        left = jnp.sum(quarters.astype(F32), axis=0).astype(BF16).reshape(2, own, -1)
+        left = sum_terms(quarters.reshape(n_row // 2, 2 * own, -1), 4).reshape(2, own, -1)
         cross = -(
             matmul(left[0], mine[:, own:].reshape(-1, rows), (1, 0))
             + matmul(left[1], other[:, own:].reshape(-1, rows), (1, 0))

time: 194 us -> 192 us (0.990)
  waiting for transfers between devices: 21 us -> 16.5 us
  other arithmetic: 4.26 us -> 1.05 us
  starting transfers between devices: 25.7 us -> 28.3 us
  blocking collectives: 115 us -> 117 us
    all_gather x1, waiting for transfers between devices: 4.5 us -> 0.02 us  [per_device(): quarters = lax.all_gather(left, ROW, axis=0, tiled=False)]
    ppermute x0 -> x1, waiting for transfers between devices: none -> 4.38 us  [per_device(): received = lax.ppermute(jnp.where(even, left[1], left[0]), 'x', pairs)]
    all_to_all x1, waiting for transfers between devices: 14 us -> 9.63 us  [gather_both_ways(): lax.all_to_all(copies, ('y', 'x', 'core'), 0, 0, axis_index_groups=groups)]
    reduce_sum x1 -> x0, other arithmetic: 3.12 us -> none  [per_device(): jnp.sum(quarters.astype(F32), axis=0).astype(BF16).reshape(2, own, -1)]
    all_to_all x2, blocking collectives: 34.3 us -> 37.3 us  [sum_rows(): pieces = lax.all_to_all(terms.reshape(size, rows // size, cols), axis, 0, 0)]
    ppermute x0 -> x1, starting transfers between devices: none -> 2.22 us  [per_device(): received = lax.ppermute(jnp.where(even, left[1], left[0]), 'x', pairs)]
  transfers between devices with their start and end apart: 6 -> 7, of which waited for: 4 -> 4; matrix products, arithmetic and copies ran while one was open for 7% -> 5% of each run, Pallas kernels for 0% -> 0%
where the time goes in v5:
time: 192 us; the launch traced here: 190 us
  blocking collectives  117 us (61%)
  starting transfers between devices  28.3 us (15%)
  waiting for transfers between devices  16.5 us (9%)
  between operations  13.7 us (7%)
  matrix products  7.04 us (4%)
  local copies, waits for them, and re-layouts  6.38 us (3%)
    all_to_all x3, blocking collectives, spread(): return lax.all_to_all(copies, axis, 0, 0)  69.5 us
    all_to_all x2, blocking collectives, sum_rows(): pieces = lax.all_to_all(terms.reshape(size, rows // size, cols), axis, 0, 0)  37.3 us
    ppermute x3, starting transfers between devices, swap_cores(): return lax.ppermute(block, 'core', [(0, 1), (1, 0)])  21.9 us
    all_to_all x1, blocking collectives, gather_both_ways(): lax.all_to_all(copies, ('y', 'x', 'core'), 0, 0, axis_index_groups=groups)  10.3 us
    all_to_all x1, waiting for transfers between devices, gather_both_ways(): lax.all_to_all(copies, ('y', 'x', 'core'), 0, 0, axis_index_groups=groups)  9.63 us
    dot_general x8, matrix products, matmul(): lax.dot_general(a, b, ((contract[0:1], contract[1:2]), ((), ())), preferr...  7.04 us
    ppermute x1, waiting for transfers between devices, per_device(): received = lax.ppermute(jnp.where(even, left[1], left[0]), 'x', pairs)  4.38 us
    all_to_all x1, starting transfers between devices, gather_both_ways(): lax.all_to_all(copies, ('y', 'x', 'core'), 0, 0, axis_index_groups=groups)  4.14 us
  transfers between devices with their start and end apart: 7, of which 4 were waited for; matrix products, arithmetic and copies ran while one was open for 5% of the time, Pallas kernels for 0%

profile of v5, /device:TPU:1, one launch (start us, length us, event | category | flops | bytes accessed | tf_op | source)
XLA Modules:
  0.0 190.4 jit_solution(12312728762523011617)
XLA Ops:
  6.5 0.0 all-gather.4.cloned.1.call-start
  6.5 1.7 slice.61
  8.2 0.0 all-gather.4.cloned.1.call-update
  8.3 0.8 slice.60
  9.1 10.3 %all_to_all.35 = bf16[4,64,512]{2,1,0:T(8,128)(2,1)S(1)} all-to-all(bf16[4,64,512]{2,1,0:T(8,128)(2,1)S(1)} %broadcast_in_dim.10), channel_id=1, replica_groups={{0,32,64,96},{128,160,192,224},{256,288,320,352},{384,416,448,480},{1,1..., dimensions={0} | all-to-all | bytes 524288 | tf_op jit(solution)/shard_map/all_to_all | solution.py:41
  19.5 0.0 copy-start.1
  19.5 1.1 broadcast_in_dim.11
  20.6 0.0 copy-start.2
  20.6 0.0 copy-start.3
  20.6 4.1 %all-to-all-start.1 = ((bf16[4,4,64,512]{3,2,1,0:T(8,128)(2,1)}), bf16[4,4,64,512]{3,2,1,0:T(8,128)(2,1)S(1)}, u32[]{:S(2)}, u32[]{:S(2)}) async-start(bf16[4,4,64,512]{3,2,1,0:T(8,128)(2,1)} %broadcast_in_dim.11), calls=%async_computation.1 | async-start | bytes 2097152 | tf_op jit(solution)/shard_map/all_to_all | solution.py:41
  24.8 0.0 all-gather.6.cloned.1.call-start
  24.8 0.0 copy-done.1
  24.8 0.0 copy-done.2
  24.8 0.0 copy-done.3
  24.9 9.6 %all-to-all-done.1 = bf16[4,4,64,512]{3,2,1,0:T(8,128)(2,1)S(1)} async-done(((bf16[4,4,64,512]{3,2,1,0:T(8,128)(2,1)}), bf16[4,4,64,512]{3,2,1,0:T(8,128)(2,1)S(1)}, u32[]{:S(2)}, u32[]{:S(2)}) %all-to-all-start.1) | async-done | bytes 1048608 | tf_op jit(solution)/shard_map/all_to_all | solution.py:41
  34.5 0.1 bitcast_select_fusion
  34.6 0.1 broadcast_in_dim.12
  34.7 35.5 %all_to_all.36 = bf16[16,128,128]{2,1,0:T(8,128)(2,1)S(1)} all-to-all(bf16[16,128,128]{2,1,0:T(8,128)(2,1)S(1)} %broadcast_in_dim.12), channel_id=1, replica_groups=mesh['y'=4,'x'=4,'z'=16,'core'=2] {'z'}, dimensions={0} | all-to-all | bytes 1048576 | tf_op jit(solution)/shard_map/all_to_all | solution.py:16
  70.2 11.5 %collective-permute-start = (bf16[16,128,128]{2,1,0:T(8,128)(2,1)S(1)}, bf16[16,128,128]{2,1,0:T(8,128)(2,1)S(1)}, u32[]{:S(2)}, u32[]{:S(2)}) collective-permute-start(bf16[16,128,128]{2,1,0:T(8,128)(2,1)S(1)} %all_to_all.36), channel_id=1, source_target_pairs={{0,1},{1,0},{2,3},{3,2},{4,5},{5,4},{6,7},{7,6},{8,9},{9,8},{10,11... | collective-permute-start | bytes 1572872 | tf_op jit(solution)/shard_map/ppermute | solution.py:26
  81.7 0.2 convolution_convert_fusion.1
  82.0 1.2 collective-permute-done
  83.2 0.2 convolution_convert_fusion
  83.5 2.2 %collective-permute-start.1 = (bf16[64,1024]{1,0:T(8,128)(2,1)S(1)}, bf16[64,1024]{1,0:T(8,128)(2,1)S(1)}, u32[]{:S(2)}, u32[]{:S(2)}) collective-permute-start(bf16[64,1024]{1,0:T(8,128)(2,1)S(1)} %select_bitcast_fusion), channel_id=1, source_target_pairs={{0,32},{32,0},{64,96},{96,64},{1,33},{33,1},{65,97},{97,65},{2,34}... | collective-permute-start | bytes 393224 | tf_op jit(solution)/shard_map/ppermute | solution.py:108
  85.7 4.4 %collective-permute-done.1 = bf16[64,1024]{1,0:T(8,128)(2,1)S(1)} collective-permute-done((bf16[64,1024]{1,0:T(8,128)(2,1)S(1)}, bf16[64,1024]{1,0:T(8,128)(2,1)S(1)}, u32[]{:S(2)}, u32[]{:S(2)}) %collective-permute-start.1) | collective-permute-done | bytes 131104 | tf_op jit(solution)/shard_map/ppermute | solution.py:108
  90.1 0.7 fusion.9
  90.8 0.0 all-gather.6.cloned.1.call-update
  90.8 1.4 convolution_bitcast_fusion.1
  92.2 0.0 all-gather.4.cloned.1.call-done
  92.3 4.4 %fusion.1 = f32[256,1024]{0,1:T(8,128)S(1)} fusion(f32[256,1024]{0,1:T(8,128)S(1)} %convolution_bitcast_fusion.1, bf16[1024,2560]{1,0:T(8,128)(2,1)} %all-gather.4.cloned.1.call-done, bf16[256,3072]{1,0:T(8,128)(2,1)} %bitcast.55), kind=kOutput, calls=%fused_computation.3 | convolution fusion | flops 1342439424 | bytes 8650752 | tf_op jit(solution)/shard_map/dot_general | solution.py:47
  96.8 3.1 %collective-permute-start.2 = (bf16[128,1024]{0,1:T(8,128)(2,1)S(1)}, bf16[128,1024]{0,1:T(8,128)(2,1)S(1)}, u32[]{:S(2)}, u32[]{:S(2)}) collective-permute-start(bf16[128,1024]{0,1:T(8,128)(2,1)S(1)} %select_convert_fusion), channel_id=1, source_target_pairs={{0,1},{1,0},{2,3},{3,2},{4,5},{5,4},{6,7},{7,6},{8,9},{9,8},{10,11... | collective-permute-start | bytes 786440 | tf_op jit(solution)/shard_map/ppermute | solution.py:26
  99.9 1.1 collective-permute-done.2
  101.0 0.1 add_convert_fusion
  101.1 0.1 copy.13
  101.2 23.5 %all_to_all.37 = bf16[16,8,1024]{2,1,0:T(8,128)(2,1)S(1)} all-to-all(bf16[16,8,1024]{2,1,0:T(8,128)(2,1)S(1)} %bitcast.48), channel_id=1, replica_groups=mesh['y'=4,'x'=4,'z'=16,'core'=2] {'z'}, dimensions={0} | all-to-all | bytes 524288 | tf_op jit(solution)/shard_map/all_to_all | solution.py:21
  124.9 23.8 %all_to_all.38 = bf16[16,8,1024]{2,1,0:T(8,128)(2,1)S(1)} all-to-all(bf16[16,8,1024]{2,1,0:T(8,128)(2,1)S(1)} %broadcast_in_dim.13), channel_id=1, replica_groups=mesh['y'=4,'x'=4,'z'=16,'core'=2] {'z'}, dimensions={0} | all-to-all | bytes 524288 | tf_op jit(solution)/shard_map/all_to_all | solution.py:16
  148.7 7.4 %collective-permute-start.3 = (bf16[128,1024]{1,0:T(8,128)(2,1)S(1)}, bf16[128,1024]{1,0:T(8,128)(2,1)S(1)}, u32[]{:S(2)}, u32[]{:S(2)}) collective-permute-start(bf16[128,1024]{1,0:T(8,128)(2,1)S(1)} %bitcast.47), channel_id=1, source_target_pairs={{0,1},{1,0},{2,3},{3,2},{4,5},{5,4},{6,7},{7,6},{8,9},{9,8},{10,11... | collective-permute-start | bytes 786440 | tf_op jit(solution)/shard_map/ppermute | solution.py:26
  156.0 0.0 all-gather.6.cloned.1.call-done
  156.1 0.0 copy-start
  156.1 1.6 copy-done
  157.7 0.4 shard_map.55
  158.0 0.2 fusion.11
  158.2 0.2 fusion.7
  158.4 0.2 fusion.13
  158.6 0.0 collective-permute-done.3
  158.6 0.2 fusion.5
  158.9 13.8 %all_to_all.39 = bf16[16,8,1024]{2,1,0:T(8,128)(2,1)S(1)} all-to-all(bf16[16,8,1024]{2,1,0:T(8,128)(2,1)S(1)} %fusion.5), channel_id=1, replica_groups=mesh['y'=4,'x'=4,'z'=16,'core'=2] {'y','x'}, dimensions={0} | all-to-all | bytes 524288 | tf_op jit(solution)/shard_map/all_to_all | solution.py:21
  172.7 10.2 %all_to_all.40 = bf16[16,8,1024]{2,1,0:T(8,128)(2,1)S(1)} all-to-all(bf16[16,8,1024]{2,1,0:T(8,128)(2,1)S(1)} %broadcast_in_dim.14), channel_id=1, replica_groups=mesh['y'=4,'x'=4,'z'=16,'core'=2] {'y','x'}, dimensions={0} | all-to-all | bytes 524288 | tf_op jit(solution)/shard_map/all_to_all | solution.py:16
  182.9 0.7 copy.17
  (14 shorter events, 0.4 us)
Async XLA Ops:
  6.5 85.7 %all-gather.4.cloned.1.call-start = ((), (), s32[]{:S(2)}) async-start(), calls=%async_computation.7 | async-start | bytes 5570560 | tf_op jit(solution)/shard_map/all_gather | solution.py:92
  19.5 5.3 %copy-start.1 = (bf16[2,128,1024]{2,1,0:T(8,128)(2,1)S(1)}, bf16[2,128,1024]{2,1,0:T(8,128)(2,1)}, u32[]{:S(2)}) copy-start(bf16[2,128,1024]{2,1,0:T(8,128)(2,1)} %param.7) | copy-start | bytes 1572868
  20.6 4.2 %copy-start.2 = (bf16[2,64,128]{2,1,0:T(8,128)(2,1)S(1)}, bf16[2,64,128]{2,1,0:T(8,128)(2,1)}, u32[]{:S(2)}) copy-start(bf16[2,64,128]{2,1,0:T(8,128)(2,1)} %param.9) | copy-start | bytes 98308
  20.6 4.2 %copy-start.3 = (bf16[128,64]{0,1:T(8,128)(2,1)S(1)}, bf16[128,64]{0,1:T(8,128)(2,1)}, u32[]{:S(2)}) copy-start(bf16[128,64]{0,1:T(8,128)(2,1)} %param.8) | copy-start | bytes 49156
  20.6 13.9 %all-to-all-start.1 = ((bf16[4,4,64,512]{3,2,1,0:T(8,128)(2,1)}), bf16[4,4,64,512]{3,2,1,0:T(8,128)(2,1)S(1)}, u32[]{:S(2)}, u32[]{:S(2)}) async-start(bf16[4,4,64,512]{3,2,1,0:T(8,128)(2,1)} %broadcast_in_dim.11), calls=%async_computation.1 | async-start | bytes 2097152 | tf_op jit(solution)/shard_map/all_to_all | solution.py:41
  24.8 131.3 %all-gather.6.cloned.1.call-start = ((), (), s32[]{:S(2)}) async-start(), calls=%async_computation.8 | async-start | bytes 2228224 | tf_op jit(solution)/shard_map/all_gather | solution.py:110
  70.2 13.0 %collective-permute-start = (bf16[16,128,128]{2,1,0:T(8,128)(2,1)S(1)}, bf16[16,128,128]{2,1,0:T(8,128)(2,1)S(1)}, u32[]{:S(2)}, u32[]{:S(2)}) collective-permute-start(bf16[16,128,128]{2,1,0:T(8,128)(2,1)S(1)} %all_to_all.36), channel_id=1, source_target_pairs={{0,1},{1,0},{2,3},{3,2},{4,5},{5,4},{6,7},{7,6},{8,9},{9,8},{10,11... | collective-permute-start | bytes 1572872 | tf_op jit(solution)/shard_map/ppermute | solution.py:26
  83.5 6.6 %collective-permute-start.1 = (bf16[64,1024]{1,0:T(8,128)(2,1)S(1)}, bf16[64,1024]{1,0:T(8,128)(2,1)S(1)}, u32[]{:S(2)}, u32[]{:S(2)}) collective-permute-start(bf16[64,1024]{1,0:T(8,128)(2,1)S(1)} %select_bitcast_fusion), channel_id=1, source_target_pairs={{0,32},{32,0},{64,96},{96,64},{1,33},{33,1},{65,97},{97,65},{2,34}... | collective-permute-start | bytes 393224 | tf_op jit(solution)/shard_map/ppermute | solution.py:108
  96.8 4.3 %collective-permute-start.2 = (bf16[128,1024]{0,1:T(8,128)(2,1)S(1)}, bf16[128,1024]{0,1:T(8,128)(2,1)S(1)}, u32[]{:S(2)}, u32[]{:S(2)}) collective-permute-start(bf16[128,1024]{0,1:T(8,128)(2,1)S(1)} %select_convert_fusion), channel_id=1, source_target_pairs={{0,1},{1,0},{2,3},{3,2},{4,5},{5,4},{6,7},{7,6},{8,9},{9,8},{10,11... | collective-permute-start | bytes 786440 | tf_op jit(solution)/shard_map/ppermute | solution.py:26
  148.7 9.9 %collective-permute-start.3 = (bf16[128,1024]{1,0:T(8,128)(2,1)S(1)}, bf16[128,1024]{1,0:T(8,128)(2,1)S(1)}, u32[]{:S(2)}, u32[]{:S(2)}) collective-permute-start(bf16[128,1024]{1,0:T(8,128)(2,1)S(1)} %bitcast.47), channel_id=1, source_target_pairs={{0,1},{1,0},{2,3},{3,2},{4,5},{5,4},{6,7},{7,6},{8,9},{9,8},{10,11... | collective-permute-start | bytes 786440 | tf_op jit(solution)/shard_map/ppermute | solution.py:26
  156.1 1.6 copy-start
Sparse Core Ops, SparseCore 0:
  10.4 77.7 all-gather.3
  91.2 61.9 all-gather.5

commit v6 on v5

--- a/solution.py
+++ b/solution.py
@@ -106,10 +106,11 @@
         even = lax.axis_index("x") % 2 == 0
         pairs = [(x, x ^ 1) for x in range(n_x)]
         received = lax.ppermute(jnp.where(even, left[1], left[0]), "x", pairs)
+        panel = factor_panel.reshape(2 * rows, depth)
+        rest = matmul(panel[:, split:], rest, (1, 1))
+        received, rest = lax.optimization_barrier((received, rest))
         left = (jnp.where(even, left[0], left[1]).astype(F32) + received.astype(F32)).astype(BF16)
         quarters = lax.all_gather(left, ROW, axis=0, tiled=False)
-        panel = factor_panel.reshape(2 * rows, depth)
-        rest = matmul(panel[:, split:], rest, (1, 1))
         earlier, _, rest = lax.optimization_barrier((earlier, left, rest))
 
         terms = (rest + matmul(panel[:, :split], earlier, (1, 1))).reshape(2, rows, -1)

time: 192 us -> 192 us (level)
  no operation moved by 1% of the time
where the time goes in v6:
time: 192 us; the launch traced here: 190 us
  blocking collectives  118 us (61%)
  starting transfers between devices  28.6 us (15%)
  waiting for transfers between devices  15 us (8%)
  between operations  13.7 us (7%)
  matrix products  7.03 us (4%)
  local copies, waits for them, and re-layouts  6.38 us (3%)
    all_to_all x3, blocking collectives, spread(): return lax.all_to_all(copies, axis, 0, 0)  69.2 us
    all_to_all x2, blocking collectives, sum_rows(): pieces = lax.all_to_all(terms.reshape(size, rows // size, cols), axis, 0, 0)  38.8 us
    ppermute x3, starting transfers between devices, swap_cores(): return lax.ppermute(block, 'core', [(0, 1), (1, 0)])  22.2 us
    all_to_all x1, blocking collectives, gather_both_ways(): lax.all_to_all(copies, ('y', 'x', 'core'), 0, 0, axis_index_groups=groups)  10.3 us
    all_to_all x1, waiting for transfers between devices, gather_both_ways(): lax.all_to_all(copies, ('y', 'x', 'core'), 0, 0, axis_index_groups=groups)  9.63 us
    dot_general x8, matrix products, matmul(): lax.dot_general(a, b, ((contract[0:1], contract[1:2]), ((), ())), preferr...  7.03 us
    all_to_all x1, starting transfers between devices, gather_both_ways(): lax.all_to_all(copies, ('y', 'x', 'core'), 0, 0, axis_index_groups=groups)  4.14 us
  transfers between devices with their start and end apart: 7, of which 4 were waited for; matrix products, arithmetic and copies ran while one was open for 5% of the time, Pallas kernels for 0%

profile of v6, /device:TPU:1, one launch (start us, length us, event | category | flops | bytes accessed | tf_op | source)
XLA Modules:
  0.0 190.4 jit_solution(17996111282540386895)
XLA Ops:
  6.5 0.0 all-gather.4.cloned.1.call-start
  6.5 1.7 slice.61
  8.2 0.0 all-gather.4.cloned.1.call-update
  8.3 0.8 slice.60
  9.1 10.3 %all_to_all.35 = bf16[4,64,512]{2,1,0:T(8,128)(2,1)S(1)} all-to-all(bf16[4,64,512]{2,1,0:T(8,128)(2,1)S(1)} %broadcast_in_dim.10), channel_id=1, replica_groups={{0,32,64,96},{128,160,192,224},{256,288,320,352},{384,416,448,480},{1,1..., dimensions={0} | all-to-all | bytes 524288 | tf_op jit(solution)/shard_map/all_to_all | solution.py:41
  19.5 0.0 copy-start.1
  19.5 1.1 broadcast_in_dim.11
  20.6 0.0 copy-start.2
  20.6 0.0 copy-start.3
  20.6 4.1 %all-to-all-start.1 = ((bf16[4,4,64,512]{3,2,1,0:T(8,128)(2,1)}), bf16[4,4,64,512]{3,2,1,0:T(8,128)(2,1)S(1)}, u32[]{:S(2)}, u32[]{:S(2)}) async-start(bf16[4,4,64,512]{3,2,1,0:T(8,128)(2,1)} %broadcast_in_dim.11), calls=%async_computation.1 | async-start | bytes 2097152 | tf_op jit(solution)/shard_map/all_to_all | solution.py:41
  24.8 0.0 all-gather.6.cloned.1.call-start
  24.8 0.0 copy-done.1
  24.8 0.0 copy-done.2
  24.8 0.0 copy-done.3
  24.9 9.6 %all-to-all-done.1 = bf16[4,4,64,512]{3,2,1,0:T(8,128)(2,1)S(1)} async-done(((bf16[4,4,64,512]{3,2,1,0:T(8,128)(2,1)}), bf16[4,4,64,512]{3,2,1,0:T(8,128)(2,1)S(1)}, u32[]{:S(2)}, u32[]{:S(2)}) %all-to-all-start.1) | async-done | bytes 1048608 | tf_op jit(solution)/shard_map/all_to_all | solution.py:41
  34.5 0.1 bitcast_select_fusion
  34.6 0.1 broadcast_in_dim.12
  34.7 35.5 %all_to_all.36 = bf16[16,128,128]{2,1,0:T(8,128)(2,1)S(1)} all-to-all(bf16[16,128,128]{2,1,0:T(8,128)(2,1)S(1)} %broadcast_in_dim.12), channel_id=1, replica_groups=mesh['y'=4,'x'=4,'z'=16,'core'=2] {'z'}, dimensions={0} | all-to-all | bytes 1048576 | tf_op jit(solution)/shard_map/all_to_all | solution.py:16
  70.2 11.5 %collective-permute-start = (bf16[16,128,128]{2,1,0:T(8,128)(2,1)S(1)}, bf16[16,128,128]{2,1,0:T(8,128)(2,1)S(1)}, u32[]{:S(2)}, u32[]{:S(2)}) collective-permute-start(bf16[16,128,128]{2,1,0:T(8,128)(2,1)S(1)} %all_to_all.36), channel_id=1, source_target_pairs={{0,1},{1,0},{2,3},{3,2},{4,5},{5,4},{6,7},{7,6},{8,9},{9,8},{10,11... | collective-permute-start | bytes 1572872 | tf_op jit(solution)/shard_map/ppermute | solution.py:26
  81.7 0.2 convolution_convert_fusion.1
  82.0 1.2 collective-permute-done
  83.2 0.2 convolution_convert_fusion
  83.5 2.2 %collective-permute-start.1 = (bf16[64,1024]{1,0:T(8,128)(2,1)S(1)}, bf16[64,1024]{1,0:T(8,128)(2,1)S(1)}, u32[]{:S(2)}, u32[]{:S(2)}) collective-permute-start(bf16[64,1024]{1,0:T(8,128)(2,1)S(1)} %select_bitcast_fusion), channel_id=1, source_target_pairs={{0,32},{32,0},{64,96},{96,64},{1,33},{33,1},{65,97},{97,65},{2,34}... | collective-permute-start | bytes 393224 | tf_op jit(solution)/shard_map/ppermute | solution.py:108
  85.7 1.4 convolution_bitcast_fusion.1
  87.1 2.9 %collective-permute-done.1 = bf16[64,1024]{1,0:T(8,128)(2,1)S(1)} collective-permute-done((bf16[64,1024]{1,0:T(8,128)(2,1)S(1)}, bf16[64,1024]{1,0:T(8,128)(2,1)S(1)}, u32[]{:S(2)}, u32[]{:S(2)}) %collective-permute-start.1) | collective-permute-done | bytes 131104 | tf_op jit(solution)/shard_map/ppermute | solution.py:108
  90.1 0.7 fusion.9
  90.8 0.0 all-gather.6.cloned.1.call-update
  90.8 0.0 all-gather.4.cloned.1.call-done
  90.9 4.4 %fusion.1 = f32[256,1024]{0,1:T(8,128)S(1)} fusion(f32[256,1024]{0,1:T(8,128)S(1)} %convolution_bitcast_fusion.1, bf16[1024,2560]{1,0:T(8,128)(2,1)} %all-gather.4.cloned.1.call-done, bf16[256,3072]{1,0:T(8,128)(2,1)} %bitcast.55), kind=kOutput, calls=%fused_computation.3 | convolution fusion | flops 1342439424 | bytes 8650752 | tf_op jit(solution)/shard_map/dot_general | solution.py:47
  95.3 3.1 %collective-permute-start.2 = (bf16[128,1024]{0,1:T(8,128)(2,1)S(1)}, bf16[128,1024]{0,1:T(8,128)(2,1)S(1)}, u32[]{:S(2)}, u32[]{:S(2)}) collective-permute-start(bf16[128,1024]{0,1:T(8,128)(2,1)S(1)} %select_convert_fusion), channel_id=1, source_target_pairs={{0,1},{1,0},{2,3},{3,2},{4,5},{5,4},{6,7},{7,6},{8,9},{9,8},{10,11... | collective-permute-start | bytes 786440 | tf_op jit(solution)/shard_map/ppermute | solution.py:26
  98.5 1.1 collective-permute-done.2
  99.6 0.1 add_convert_fusion
  99.7 0.1 copy.13
  99.8 24.2 %all_to_all.37 = bf16[16,8,1024]{2,1,0:T(8,128)(2,1)S(1)} all-to-all(bf16[16,8,1024]{2,1,0:T(8,128)(2,1)S(1)} %bitcast.48), channel_id=1, replica_groups=mesh['y'=4,'x'=4,'z'=16,'core'=2] {'z'}, dimensions={0} | all-to-all | bytes 524288 | tf_op jit(solution)/shard_map/all_to_all | solution.py:21
  124.1 23.4 %all_to_all.38 = bf16[16,8,1024]{2,1,0:T(8,128)(2,1)S(1)} all-to-all(bf16[16,8,1024]{2,1,0:T(8,128)(2,1)S(1)} %broadcast_in_dim.13), channel_id=1, replica_groups=mesh['y'=4,'x'=4,'z'=16,'core'=2] {'z'}, dimensions={0} | all-to-all | bytes 524288 | tf_op jit(solution)/shard_map/all_to_all | solution.py:16
  147.5 7.6 %collective-permute-start.3 = (bf16[128,1024]{1,0:T(8,128)(2,1)S(1)}, bf16[128,1024]{1,0:T(8,128)(2,1)S(1)}, u32[]{:S(2)}, u32[]{:S(2)}) collective-permute-start(bf16[128,1024]{1,0:T(8,128)(2,1)S(1)} %bitcast.47), channel_id=1, source_target_pairs={{0,1},{1,0},{2,3},{3,2},{4,5},{5,4},{6,7},{7,6},{8,9},{9,8},{10,11... | collective-permute-start | bytes 786440 | tf_op jit(solution)/shard_map/ppermute | solution.py:26
  155.2 0.0 all-gather.6.cloned.1.call-done
  155.2 0.0 copy-start
  155.2 1.6 copy-done
  156.8 0.4 shard_map.55
  157.2 0.2 fusion.11
  157.3 0.2 fusion.7
  157.5 0.2 fusion.13
  157.8 0.0 collective-permute-done.3
  157.8 0.2 fusion.5
  158.0 14.7 %all_to_all.39 = bf16[16,8,1024]{2,1,0:T(8,128)(2,1)S(1)} all-to-all(bf16[16,8,1024]{2,1,0:T(8,128)(2,1)S(1)} %fusion.5), channel_id=1, replica_groups=mesh['y'=4,'x'=4,'z'=16,'core'=2] {'y','x'}, dimensions={0} | all-to-all | bytes 524288 | tf_op jit(solution)/shard_map/all_to_all | solution.py:21
  172.7 10.2 %all_to_all.40 = bf16[16,8,1024]{2,1,0:T(8,128)(2,1)S(1)} all-to-all(bf16[16,8,1024]{2,1,0:T(8,128)(2,1)S(1)} %broadcast_in_dim.14), channel_id=1, replica_groups=mesh['y'=4,'x'=4,'z'=16,'core'=2] {'y','x'}, dimensions={0} | all-to-all | bytes 524288 | tf_op jit(solution)/shard_map/all_to_all | solution.py:16
  182.9 0.7 copy.17
  (14 shorter events, 0.4 us)
Async XLA Ops:
  6.5 84.3 %all-gather.4.cloned.1.call-start = ((), (), s32[]{:S(2)}) async-start(), calls=%async_computation.7 | async-start | bytes 5570560 | tf_op jit(solution)/shard_map/all_gather | solution.py:92
  19.5 5.3 %copy-start.1 = (bf16[2,128,1024]{2,1,0:T(8,128)(2,1)S(1)}, bf16[2,128,1024]{2,1,0:T(8,128)(2,1)}, u32[]{:S(2)}) copy-start(bf16[2,128,1024]{2,1,0:T(8,128)(2,1)} %param.7) | copy-start | bytes 1572868
  20.6 4.2 %copy-start.2 = (bf16[2,64,128]{2,1,0:T(8,128)(2,1)S(1)}, bf16[2,64,128]{2,1,0:T(8,128)(2,1)}, u32[]{:S(2)}) copy-start(bf16[2,64,128]{2,1,0:T(8,128)(2,1)} %param.9) | copy-start | bytes 98308
  20.6 4.2 %copy-start.3 = (bf16[128,64]{0,1:T(8,128)(2,1)S(1)}, bf16[128,64]{0,1:T(8,128)(2,1)}, u32[]{:S(2)}) copy-start(bf16[128,64]{0,1:T(8,128)(2,1)} %param.8) | copy-start | bytes 49156
  20.6 13.9 %all-to-all-start.1 = ((bf16[4,4,64,512]{3,2,1,0:T(8,128)(2,1)}), bf16[4,4,64,512]{3,2,1,0:T(8,128)(2,1)S(1)}, u32[]{:S(2)}, u32[]{:S(2)}) async-start(bf16[4,4,64,512]{3,2,1,0:T(8,128)(2,1)} %broadcast_in_dim.11), calls=%async_computation.1 | async-start | bytes 2097152 | tf_op jit(solution)/shard_map/all_to_all | solution.py:41
  24.8 130.4 %all-gather.6.cloned.1.call-start = ((), (), s32[]{:S(2)}) async-start(), calls=%async_computation.8 | async-start | bytes 2228224 | tf_op jit(solution)/shard_map/all_gather | solution.py:113
  70.2 13.0 %collective-permute-start = (bf16[16,128,128]{2,1,0:T(8,128)(2,1)S(1)}, bf16[16,128,128]{2,1,0:T(8,128)(2,1)S(1)}, u32[]{:S(2)}, u32[]{:S(2)}) collective-permute-start(bf16[16,128,128]{2,1,0:T(8,128)(2,1)S(1)} %all_to_all.36), channel_id=1, source_target_pairs={{0,1},{1,0},{2,3},{3,2},{4,5},{5,4},{6,7},{7,6},{8,9},{9,8},{10,11... | collective-permute-start | bytes 1572872 | tf_op jit(solution)/shard_map/ppermute | solution.py:26
  83.5 6.6 %collective-permute-start.1 = (bf16[64,1024]{1,0:T(8,128)(2,1)S(1)}, bf16[64,1024]{1,0:T(8,128)(2,1)S(1)}, u32[]{:S(2)}, u32[]{:S(2)}) collective-permute-start(bf16[64,1024]{1,0:T(8,128)(2,1)S(1)} %select_bitcast_fusion), channel_id=1, source_target_pairs={{0,32},{32,0},{64,96},{96,64},{1,33},{33,1},{65,97},{97,65},{2,34}... | collective-permute-start | bytes 393224 | tf_op jit(solution)/shard_map/ppermute | solution.py:108
  95.3 4.3 %collective-permute-start.2 = (bf16[128,1024]{0,1:T(8,128)(2,1)S(1)}, bf16[128,1024]{0,1:T(8,128)(2,1)S(1)}, u32[]{:S(2)}, u32[]{:S(2)}) collective-permute-start(bf16[128,1024]{0,1:T(8,128)(2,1)S(1)} %select_convert_fusion), channel_id=1, source_target_pairs={{0,1},{1,0},{2,3},{3,2},{4,5},{5,4},{6,7},{7,6},{8,9},{9,8},{10,11... | collective-permute-start | bytes 786440 | tf_op jit(solution)/shard_map/ppermute | solution.py:26
  147.5 10.2 %collective-permute-start.3 = (bf16[128,1024]{1,0:T(8,128)(2,1)S(1)}, bf16[128,1024]{1,0:T(8,128)(2,1)S(1)}, u32[]{:S(2)}, u32[]{:S(2)}) collective-permute-start(bf16[128,1024]{1,0:T(8,128)(2,1)S(1)} %bitcast.47), channel_id=1, source_target_pairs={{0,1},{1,0},{2,3},{3,2},{4,5},{5,4},{6,7},{7,6},{8,9},{9,8},{10,11... | collective-permute-start | bytes 786440 | tf_op jit(solution)/shard_map/ppermute | solution.py:26
  155.2 1.6 copy-start
Sparse Core Ops, SparseCore 0:
  10.4 77.7 all-gather.3
  91.2 61.9 all-gather.5

commit v7 on v6

--- a/solution.py
+++ b/solution.py
@@ -8,7 +8,7 @@
 BF16 = jnp.bfloat16
 F32 = jnp.float32
 ROW = ("y", "x")
-SPLIT = 20
+SPLIT = 21
 
 
 def spread(block, axis, size):

time: 192 us -> 193 us (level)
  blocking collectives: 118 us -> 108 us
  starting transfers between devices: 28.6 us -> 34.3 us
  waiting for transfers between devices: 15 us -> 19.8 us
    all_to_all x1 -> x0, blocking collectives: 10.3 us -> none  [gather_both_ways(): lax.all_to_all(copies, ('y', 'x', 'core'), 0, 0, axis_index_groups=groups)]
    all_to_all x1 -> x2, starting transfers between devices: 4.14 us -> 9.16 us  [gather_both_ways(): lax.all_to_all(copies, ('y', 'x', 'core'), 0, 0, axis_index_groups=groups)]
    all_to_all x1 -> x2, waiting for transfers between devices: 9.63 us -> 13.4 us  [gather_both_ways(): lax.all_to_all(copies, ('y', 'x', 'core'), 0, 0, axis_index_groups=groups)]
  transfers between devices with their start and end apart: 7 -> 8, of which waited for: 4 -> 5; matrix products, arithmetic and copies ran while one was open for 5% -> 6% of each run, Pallas kernels for 0% -> 0%
where the time goes in v7:
time: 193 us; the launch traced here: 191 us
  blocking collectives  108 us (56%)
  starting transfers between devices  34.3 us (18%)
  waiting for transfers between devices  19.8 us (10%)
  between operations  13.7 us (7%)
  matrix products  7.24 us (4%)
  local copies, waits for them, and re-layouts  6.93 us (4%)
    all_to_all x3, blocking collectives, spread(): return lax.all_to_all(copies, axis, 0, 0)  67.7 us
    all_to_all x2, blocking collectives, sum_rows(): pieces = lax.all_to_all(terms.reshape(size, rows // size, cols), axis, 0, 0)  40.2 us
    ppermute x3, starting transfers between devices, swap_cores(): return lax.ppermute(block, 'core', [(0, 1), (1, 0)])  22.3 us
    all_to_all x2, waiting for transfers between devices, gather_both_ways(): lax.all_to_all(copies, ('y', 'x', 'core'), 0, 0, axis_index_groups=groups)  13.4 us
    all_to_all x2, starting transfers between devices, gather_both_ways(): lax.all_to_all(copies, ('y', 'x', 'core'), 0, 0, axis_index_groups=groups)  9.16 us
    dot_general x8, matrix products, matmul(): lax.dot_general(a, b, ((contract[0:1], contract[1:2]), ((), ())), preferr...  7.24 us
    ppermute x1, waiting for transfers between devices, per_device(): received = lax.ppermute(jnp.where(even, left[1], left[0]), 'x', pairs)  3.92 us
  transfers between devices with their start and end apart: 8, of which 5 were waited for; matrix products, arithmetic and copies ran while one was open for 6% of the time, Pallas kernels for 0%

profile of v7, /device:TPU:1, one launch (start us, length us, event | category | flops | bytes accessed | tf_op | source)
XLA Modules:
  0.0 191.2 jit_solution(10884530539617221526)
XLA Ops:
  6.5 0.0 all-gather.4.cloned.1.call-start
  6.5 1.7 slice.61
  8.3 0.0 all-gather.4.cloned.1.call-update
  8.3 0.8 slice.60
  9.1 0.0 copy-start.1
  9.1 0.7 broadcast_in_dim.10
  9.8 5.0 %all-to-all-start = ((bf16[4,64,384]{2,1,0:T(8,128)(2,1)}), bf16[4,64,384]{2,1,0:T(8,128)(2,1)S(1)}, u32[]{:S(2)}, u32[]{:S(2)}) async-start(bf16[4,64,384]{2,1,0:T(8,128)(2,1)} %broadcast_in_dim.10), calls=%async_computation | async-start | bytes 393216 | tf_op jit(solution)/shard_map/all_to_all | solution.py:41
  14.8 5.2 %all-to-all-done = bf16[4,64,384]{2,1,0:T(8,128)(2,1)S(1)} async-done(((bf16[4,64,384]{2,1,0:T(8,128)(2,1)}), bf16[4,64,384]{2,1,0:T(8,128)(2,1)S(1)}, u32[]{:S(2)}, u32[]{:S(2)}) %all-to-all-start) | async-done | bytes 196640 | tf_op jit(solution)/shard_map/all_to_all | solution.py:41
  20.0 1.0 broadcast_in_dim.11
  21.0 0.0 copy-start.2
  21.0 0.0 copy-start.3
  21.0 4.1 %all-to-all-start.1 = ((bf16[4,4,64,384]{3,2,1,0:T(8,128)(2,1)}), bf16[4,4,64,384]{3,2,1,0:T(8,128)(2,1)S(1)}, u32[]{:S(2)}, u32[]{:S(2)}) async-start(bf16[4,4,64,384]{3,2,1,0:T(8,128)(2,1)} %broadcast_in_dim.11), calls=%async_computation.1 | async-start | bytes 1572864 | tf_op jit(solution)/shard_map/all_to_all | solution.py:41
  25.1 0.0 all-gather.6.cloned.1.call-start
  25.2 0.0 copy-done.1
  25.2 0.0 copy-done.2
  25.2 0.0 copy-done.3
  25.3 8.2 %all-to-all-done.1 = bf16[4,4,64,384]{3,2,1,0:T(8,128)(2,1)S(1)} async-done(((bf16[4,4,64,384]{3,2,1,0:T(8,128)(2,1)}), bf16[4,4,64,384]{3,2,1,0:T(8,128)(2,1)S(1)}, u32[]{:S(2)}, u32[]{:S(2)}) %all-to-all-start.1) | async-done | bytes 786464 | tf_op jit(solution)/shard_map/all_to_all | solution.py:41
  33.5 0.1 bitcast_select_fusion
  33.6 0.1 broadcast_in_dim.12
  33.7 34.1 %all_to_all.35 = bf16[16,128,128]{2,1,0:T(8,128)(2,1)S(1)} all-to-all(bf16[16,128,128]{2,1,0:T(8,128)(2,1)S(1)} %broadcast_in_dim.12), channel_id=1, replica_groups=mesh['y'=4,'x'=4,'z'=16,'core'=2] {'z'}, dimensions={0} | all-to-all | bytes 1048576 | tf_op jit(solution)/shard_map/all_to_all | solution.py:16
  67.7 12.1 %collective-permute-start = (bf16[16,128,128]{2,1,0:T(8,128)(2,1)S(1)}, bf16[16,128,128]{2,1,0:T(8,128)(2,1)S(1)}, u32[]{:S(2)}, u32[]{:S(2)}) collective-permute-start(bf16[16,128,128]{2,1,0:T(8,128)(2,1)S(1)} %all_to_all.35), channel_id=1, source_target_pairs={{0,1},{1,0},{2,3},{3,2},{4,5},{5,4},{6,7},{7,6},{8,9},{9,8},{10,11... | collective-permute-start | bytes 1572872 | tf_op jit(solution)/shard_map/ppermute | solution.py:26
  79.9 0.2 convolution_convert_fusion.1
  80.1 1.2 collective-permute-done
  81.4 0.2 convolution_convert_fusion
  81.7 2.8 %collective-permute-start.1 = (bf16[64,1024]{1,0:T(8,128)(2,1)S(1)}, bf16[64,1024]{1,0:T(8,128)(2,1)S(1)}, u32[]{:S(2)}, u32[]{:S(2)}) collective-permute-start(bf16[64,1024]{1,0:T(8,128)(2,1)S(1)} %select_bitcast_fusion), channel_id=1, source_target_pairs={{0,32},{32,0},{64,96},{96,64},{1,33},{33,1},{65,97},{97,65},{2,34}... | collective-permute-start | bytes 393224 | tf_op jit(solution)/shard_map/ppermute | solution.py:108
  84.4 1.4 convolution_bitcast_fusion
  85.8 3.9 %collective-permute-done.1 = bf16[64,1024]{1,0:T(8,128)(2,1)S(1)} collective-permute-done((bf16[64,1024]{1,0:T(8,128)(2,1)S(1)}, bf16[64,1024]{1,0:T(8,128)(2,1)S(1)}, u32[]{:S(2)}, u32[]{:S(2)}) %collective-permute-start.1) | collective-permute-done | bytes 131104 | tf_op jit(solution)/shard_map/ppermute | solution.py:108
  89.7 0.7 fusion.12
  90.4 0.0 all-gather.6.cloned.1.call-update
  90.5 0.0 all-gather.4.cloned.1.call-done
  90.5 4.7 %fusion.5 = f32[256,1024]{0,1:T(8,128)S(1)} fusion(f32[256,1024]{0,1:T(8,128)S(1)} %convolution_bitcast_fusion, bf16[1024,2688]{1,0:T(8,128)(2,1)} %all-gather.4.cloned.1.call-done, bf16[256,3072]{1,0:T(8,128)(2,1)} %bitcast.55), kind=kOutput, calls=%fused_computation.4 | convolution fusion | flops 1409548288 | bytes 8978432 | tf_op jit(solution)/shard_map/dot_general | solution.py:47
  95.2 2.6 %collective-permute-start.2 = (bf16[128,1024]{0,1:T(8,128)(2,1)S(1)}, bf16[128,1024]{0,1:T(8,128)(2,1)S(1)}, u32[]{:S(2)}, u32[]{:S(2)}) collective-permute-start(bf16[128,1024]{0,1:T(8,128)(2,1)S(1)} %select_convert_fusion), channel_id=1, source_target_pairs={{0,1},{1,0},{2,3},{3,2},{4,5},{5,4},{6,7},{7,6},{8,9},{9,8},{10,11... | collective-permute-start | bytes 786440 | tf_op jit(solution)/shard_map/ppermute | solution.py:26
  97.8 1.1 collective-permute-done.2
  98.9 0.1 add_convert_fusion
  99.0 0.1 copy.13
  99.2 25.5 %all_to_all.36 = bf16[16,8,1024]{2,1,0:T(8,128)(2,1)S(1)} all-to-all(bf16[16,8,1024]{2,1,0:T(8,128)(2,1)S(1)} %bitcast.48), channel_id=1, replica_groups=mesh['y'=4,'x'=4,'z'=16,'core'=2] {'z'}, dimensions={0} | all-to-all | bytes 524288 | tf_op jit(solution)/shard_map/all_to_all | solution.py:21
  124.8 23.4 %all_to_all.37 = bf16[16,8,1024]{2,1,0:T(8,128)(2,1)S(1)} all-to-all(bf16[16,8,1024]{2,1,0:T(8,128)(2,1)S(1)} %broadcast_in_dim.13), channel_id=1, replica_groups=mesh['y'=4,'x'=4,'z'=16,'core'=2] {'z'}, dimensions={0} | all-to-all | bytes 524288 | tf_op jit(solution)/shard_map/all_to_all | solution.py:16
  148.3 7.6 %collective-permute-start.3 = (bf16[128,1024]{1,0:T(8,128)(2,1)S(1)}, bf16[128,1024]{1,0:T(8,128)(2,1)S(1)}, u32[]{:S(2)}, u32[]{:S(2)}) collective-permute-start(bf16[128,1024]{1,0:T(8,128)(2,1)S(1)} %bitcast.47), channel_id=1, source_target_pairs={{0,1},{1,0},{2,3},{3,2},{4,5},{5,4},{6,7},{7,6},{8,9},{9,8},{10,11... | collective-permute-start | bytes 786440 | tf_op jit(solution)/shard_map/ppermute | solution.py:26
  155.9 0.0 all-gather.6.cloned.1.call-done
  155.9 0.0 copy-start
  156.0 1.6 copy-done
  157.5 0.4 shard_map.55
  157.9 0.2 fusion.15
  158.1 0.2 fusion.11
  158.3 0.2 fusion.17
  158.5 0.0 collective-permute-done.3
  158.5 0.2 fusion.9
  158.7 14.6 %all_to_all.38 = bf16[16,8,1024]{2,1,0:T(8,128)(2,1)S(1)} all-to-all(bf16[16,8,1024]{2,1,0:T(8,128)(2,1)S(1)} %fusion.9), channel_id=1, replica_groups=mesh['y'=4,'x'=4,'z'=16,'core'=2] {'y','x'}, dimensions={0} | all-to-all | bytes 524288 | tf_op jit(solution)/shard_map/all_to_all | solution.py:21
  173.4 10.2 %all_to_all.39 = bf16[16,8,1024]{2,1,0:T(8,128)(2,1)S(1)} all-to-all(bf16[16,8,1024]{2,1,0:T(8,128)(2,1)S(1)} %broadcast_in_dim.14), channel_id=1, replica_groups=mesh['y'=4,'x'=4,'z'=16,'core'=2] {'y','x'}, dimensions={0} | all-to-all | bytes 524288 | tf_op jit(solution)/shard_map/all_to_all | solution.py:16
  183.6 0.7 copy.17
  (13 shorter events, 0.3 us)
Async XLA Ops:
  6.5 83.9 %all-gather.4.cloned.1.call-start = ((), (), s32[]{:S(2)}) async-start(), calls=%async_computation.7 | async-start | bytes 5849088 | tf_op jit(solution)/shard_map/all_gather | solution.py:92
  9.1 16.0 %copy-start.1 = (bf16[2,128,1024]{2,1,0:T(8,128)(2,1)S(1)}, bf16[2,128,1024]{2,1,0:T(8,128)(2,1)}, u32[]{:S(2)}) copy-start(bf16[2,128,1024]{2,1,0:T(8,128)(2,1)} %param.7) | copy-start | bytes 1572868
  9.8 10.2 %all-to-all-start = ((bf16[4,64,384]{2,1,0:T(8,128)(2,1)}), bf16[4,64,384]{2,1,0:T(8,128)(2,1)S(1)}, u32[]{:S(2)}, u32[]{:S(2)}) async-start(bf16[4,64,384]{2,1,0:T(8,128)(2,1)} %broadcast_in_dim.10), calls=%async_computation | async-start | bytes 393216 | tf_op jit(solution)/shard_map/all_to_all | solution.py:41
  21.0 4.2 %copy-start.2 = (bf16[2,64,128]{2,1,0:T(8,128)(2,1)S(1)}, bf16[2,64,128]{2,1,0:T(8,128)(2,1)}, u32[]{:S(2)}) copy-start(bf16[2,64,128]{2,1,0:T(8,128)(2,1)} %param.9) | copy-start | bytes 98308
  21.0 4.2 %copy-start.3 = (bf16[128,64]{0,1:T(8,128)(2,1)S(1)}, bf16[128,64]{0,1:T(8,128)(2,1)}, u32[]{:S(2)}) copy-start(bf16[128,64]{0,1:T(8,128)(2,1)} %param.8) | copy-start | bytes 49156
  21.0 12.5 %all-to-all-start.1 = ((bf16[4,4,64,384]{3,2,1,0:T(8,128)(2,1)}), bf16[4,4,64,384]{3,2,1,0:T(8,128)(2,1)S(1)}, u32[]{:S(2)}, u32[]{:S(2)}) async-start(bf16[4,4,64,384]{3,2,1,0:T(8,128)(2,1)} %broadcast_in_dim.11), calls=%async_computation.1 | async-start | bytes 1572864 | tf_op jit(solution)/shard_map/all_to_all | solution.py:41
  25.1 130.8 %all-gather.6.cloned.1.call-start = ((), (), s32[]{:S(2)}) async-start(), calls=%async_computation.8 | async-start | bytes 2228224 | tf_op jit(solution)/shard_map/all_gather | solution.py:113
  67.7 13.6 %collective-permute-start = (bf16[16,128,128]{2,1,0:T(8,128)(2,1)S(1)}, bf16[16,128,128]{2,1,0:T(8,128)(2,1)S(1)}, u32[]{:S(2)}, u32[]{:S(2)}) collective-permute-start(bf16[16,128,128]{2,1,0:T(8,128)(2,1)S(1)} %all_to_all.35), channel_id=1, source_target_pairs={{0,1},{1,0},{2,3},{3,2},{4,5},{5,4},{6,7},{7,6},{8,9},{9,8},{10,11... | collective-permute-start | bytes 1572872 | tf_op jit(solution)/shard_map/ppermute | solution.py:26
  81.7 8.1 %collective-permute-start.1 = (bf16[64,1024]{1,0:T(8,128)(2,1)S(1)}, bf16[64,1024]{1,0:T(8,128)(2,1)S(1)}, u32[]{:S(2)}, u32[]{:S(2)}) collective-permute-start(bf16[64,1024]{1,0:T(8,128)(2,1)S(1)} %select_bitcast_fusion), channel_id=1, source_target_pairs={{0,32},{32,0},{64,96},{96,64},{1,33},{33,1},{65,97},{97,65},{2,34}... | collective-permute-start | bytes 393224 | tf_op jit(solution)/shard_map/ppermute | solution.py:108
  95.2 3.7 %collective-permute-start.2 = (bf16[128,1024]{0,1:T(8,128)(2,1)S(1)}, bf16[128,1024]{0,1:T(8,128)(2,1)S(1)}, u32[]{:S(2)}, u32[]{:S(2)}) collective-permute-start(bf16[128,1024]{0,1:T(8,128)(2,1)S(1)} %select_convert_fusion), channel_id=1, source_target_pairs={{0,1},{1,0},{2,3},{3,2},{4,5},{5,4},{6,7},{7,6},{8,9},{9,8},{10,11... | collective-permute-start | bytes 786440 | tf_op jit(solution)/shard_map/ppermute | solution.py:26
  148.3 10.2 %collective-permute-start.3 = (bf16[128,1024]{1,0:T(8,128)(2,1)S(1)}, bf16[128,1024]{1,0:T(8,128)(2,1)S(1)}, u32[]{:S(2)}, u32[]{:S(2)}) collective-permute-start(bf16[128,1024]{1,0:T(8,128)(2,1)S(1)} %bitcast.47), channel_id=1, source_target_pairs={{0,1},{1,0},{2,3},{3,2},{4,5},{5,4},{6,7},{7,6},{8,9},{9,8},{10,11... | collective-permute-start | bytes 786440 | tf_op jit(solution)/shard_map/ppermute | solution.py:26
  155.9 1.6 copy-start
Sparse Core Ops, SparseCore 0:
  10.4 78.2 all-gather.3
  91.7 61.9 all-gather.5

commit v8 on v5

--- a/solution.py
+++ b/solution.py
@@ -8,6 +8,7 @@
 BF16 = jnp.bfloat16
 F32 = jnp.float32
 ROW = ("y", "x")
+Z = ("far", "near")
 SPLIT = 20
 
 
@@ -78,13 +79,13 @@
     )(terms)
 
 
-def make_per_device(n_row, n_y, n_x, n_z):
+def make_per_device(n_row, n_y, n_x, n_z, n_near):
     def per_device(factor_panel, solved_earlier, right_side, coupling, inverses):
         core = lax.axis_index("core")
-        z = lax.axis_index("z")
+        near = lax.axis_index("near")
         _, rows, _ = factor_panel.shape
         own = coupling.shape[1]
-        part = rows // n_z
+        part = rows // n_near
         is_first = core == 0
 
         depth = solved_earlier.shape[1]
@@ -92,12 +93,12 @@
         earlier = lax.all_gather(solved_earlier[:, :split], ROW, axis=0, tiled=True)
 
         right = jnp.where(is_first, right_side[0], right_side[1])
-        right = lax.dynamic_slice_in_dim(right, z * part, part, axis=0)
+        right = lax.dynamic_slice_in_dim(right, near * part, part, axis=0)
         packed = jnp.concatenate([coupling.T, inverses[0]], axis=0)
         rest = gather_both_ways(solved_earlier[:, split:], n_y, n_x, core == 0)
         packed, right, is_first, rest = lax.optimization_barrier((packed, right, is_first, rest))
 
-        mine = spread(packed, "z", n_z)
+        mine = spread(packed, Z, n_z)
         other = swap_cores(mine)
         left = [
             matmul(inverses[1], part_[:, :own].reshape(-1, rows), (1, 1)).astype(BF16)
@@ -116,9 +117,10 @@
         kept = jnp.where(is_first, terms[0], terms[1])
         sent = jnp.where(is_first, terms[1], terms[0]).astype(BF16)
         kept = (kept + swap_cores(sent).astype(F32)).astype(BF16)
-        prefix = sum_rows(kept, "z", n_z)
+        quarter = sum_rows(kept, "near", n_near).astype(BF16)
+        prefix = jnp.sum(spread(quarter, "far", n_z // n_near).astype(F32), axis=0)
         residual = (right.astype(F32) - prefix).astype(BF16)
-        residual = spread(residual, "z", n_z).reshape(rows, -1)
+        residual = spread(residual, "near", n_near).reshape(rows, -1)
         residual_other = swap_cores(residual)
 
         _, quarters = lax.optimization_barrier((residual, quarters))
@@ -143,10 +145,11 @@
     n_x = 4
     n_y = n_row // n_x
     n_z = n_col // 2
-    split = Mesh(mesh.devices.reshape(n_y, n_x, n_z, 2), ("y", "x", "z", "core"))
-    col = ("z", "core")
+    n_near = 4
+    split = Mesh(mesh.devices.reshape(n_y, n_x, n_z // n_near, n_near, 2), ("y", "x", "far", "near", "core"))
+    col = ("far", "near", "core")
     return jax.shard_map(
-        make_per_device(n_row, n_y, n_x, n_z),
+        make_per_device(n_row, n_y, n_x, n_z, n_near),
         mesh=split,
         in_specs=(
             P(None, ROW, col),

time: 192 us -> 190 us (0.990)
    all_to_all x2, blocking collectives: 37.3 us -> 25.4 us  [sum_rows(): pieces = lax.all_to_all(terms.reshape(size, rows // size, cols), axis, 0, 0)]
    all_to_all x3 -> x4, blocking collectives: 69.5 us -> 81 us  [spread(): return lax.all_to_all(copies, axis, 0, 0)]
where the time goes in v8:
time: 190 us; the launch traced here: 189 us
  blocking collectives  117 us (62%)
  starting transfers between devices  28.9 us (15%)
  waiting for transfers between devices  15.2 us (8%)
  between operations  13.7 us (7%)
  matrix products  7.04 us (4%)
  local copies, waits for them, and re-layouts  6.38 us (3%)
    all_to_all x4, blocking collectives, spread(): return lax.all_to_all(copies, axis, 0, 0)  81 us
    all_to_all x2, blocking collectives, sum_rows(): pieces = lax.all_to_all(terms.reshape(size, rows // size, cols), axis, 0, 0)  25.4 us
    ppermute x3, starting transfers between devices, swap_cores(): return lax.ppermute(block, 'core', [(0, 1), (1, 0)])  22.8 us
    all_to_all x1, blocking collectives, gather_both_ways(): lax.all_to_all(copies, ('y', 'x', 'core'), 0, 0, axis_index_groups=groups)  10.3 us
    all_to_all x1, waiting for transfers between devices, gather_both_ways(): lax.all_to_all(copies, ('y', 'x', 'core'), 0, 0, axis_index_groups=groups)  9.62 us
    dot_general x8, matrix products, matmul(): lax.dot_general(a, b, ((contract[0:1], contract[1:2]), ((), ())), preferr...  7.04 us
    all_to_all x1, starting transfers between devices, gather_both_ways(): lax.all_to_all(copies, ('y', 'x', 'core'), 0, 0, axis_index_groups=groups)  4.01 us
  transfers between devices with their start and end apart: 7, of which 4 were waited for; matrix products, arithmetic and copies ran while one was open for 5% of the time, Pallas kernels for 0%

profile of v8, /device:TPU:1, one launch (start us, length us, event | category | flops | bytes accessed | tf_op | source)
XLA Modules:
  0.0 189.5 jit_solution(283172509702263534)
XLA Ops:
  6.5 0.0 all-gather.4.cloned.1.call-start
  6.5 1.7 slice.61
  8.2 0.0 all-gather.4.cloned.1.call-update
  8.3 0.8 slice.60
  9.1 10.3 %all_to_all.40 = bf16[4,64,512]{2,1,0:T(8,128)(2,1)S(1)} all-to-all(bf16[4,64,512]{2,1,0:T(8,128)(2,1)S(1)} %broadcast_in_dim.12), channel_id=1, replica_groups={{0,32,64,96},{128,160,192,224},{256,288,320,352},{384,416,448,480},{1,1..., dimensions={0} | all-to-all | bytes 524288 | tf_op jit(solution)/shard_map/all_to_all | solution.py:42
  19.5 0.0 copy-start.2
  19.5 0.0 copy-start.3
  19.5 0.0 copy-start.1
  19.5 1.1 broadcast_in_dim.13
  20.6 4.0 %all-to-all-start.1 = ((bf16[4,4,64,512]{3,2,1,0:T(8,128)(2,1)}), bf16[4,4,64,512]{3,2,1,0:T(8,128)(2,1)S(1)}, u32[]{:S(2)}, u32[]{:S(2)}) async-start(bf16[4,4,64,512]{3,2,1,0:T(8,128)(2,1)} %broadcast_in_dim.13), calls=%async_computation.1 | async-start | bytes 2097152 | tf_op jit(solution)/shard_map/all_to_all | solution.py:42
  24.6 0.0 all-gather.6.cloned.1.call-start
  24.6 0.0 copy-done.2
  24.6 0.0 copy-done.3
  24.6 0.0 copy-done.1
  24.7 9.6 %all-to-all-done.1 = bf16[4,4,64,512]{3,2,1,0:T(8,128)(2,1)S(1)} async-done(((bf16[4,4,64,512]{3,2,1,0:T(8,128)(2,1)}), bf16[4,4,64,512]{3,2,1,0:T(8,128)(2,1)S(1)}, u32[]{:S(2)}, u32[]{:S(2)}) %all-to-all-start.1) | async-done | bytes 1048608 | tf_op jit(solution)/shard_map/all_to_all | solution.py:42
  34.3 0.1 bitcast_select_fusion
  34.4 0.1 broadcast_in_dim.14
  34.5 34.8 %all_to_all.41 = bf16[16,128,128]{2,1,0:T(8,128)(2,1)S(1)} all-to-all(bf16[16,128,128]{2,1,0:T(8,128)(2,1)S(1)} %broadcast_in_dim.14), channel_id=1, replica_groups=mesh['y'=4,'x'=4,'far'=4,'near'=4,'core'=2] {'far','near'}, dimensions={0} | all-to-all | bytes 1048576 | tf_op jit(solution)/shard_map/all_to_all | solution.py:17
  69.4 12.2 %collective-permute-start = (bf16[16,128,128]{2,1,0:T(8,128)(2,1)S(1)}, bf16[16,128,128]{2,1,0:T(8,128)(2,1)S(1)}, u32[]{:S(2)}, u32[]{:S(2)}) collective-permute-start(bf16[16,128,128]{2,1,0:T(8,128)(2,1)S(1)} %all_to_all.41), channel_id=1, source_target_pairs={{0,1},{1,0},{2,3},{3,2},{4,5},{5,4},{6,7},{7,6},{8,9},{9,8},{10,11... | collective-permute-start | bytes 1572872 | tf_op jit(solution)/shard_map/ppermute | solution.py:27
  81.6 0.2 convolution_convert_fusion.1
  81.8 1.2 collective-permute-done
  83.1 0.2 convolution_convert_fusion
  83.3 2.1 %collective-permute-start.1 = (bf16[64,1024]{1,0:T(8,128)(2,1)S(1)}, bf16[64,1024]{1,0:T(8,128)(2,1)S(1)}, u32[]{:S(2)}, u32[]{:S(2)}) collective-permute-start(bf16[64,1024]{1,0:T(8,128)(2,1)S(1)} %select_bitcast_fusion), channel_id=1, source_target_pairs={{0,32},{32,0},{64,96},{96,64},{1,33},{33,1},{65,97},{97,65},{2,34}... | collective-permute-start | bytes 393224 | tf_op jit(solution)/shard_map/ppermute | solution.py:109
  85.4 1.4 convolution_bitcast_fusion.1
  86.9 3.1 %collective-permute-done.1 = bf16[64,1024]{1,0:T(8,128)(2,1)S(1)} collective-permute-done((bf16[64,1024]{1,0:T(8,128)(2,1)S(1)}, bf16[64,1024]{1,0:T(8,128)(2,1)S(1)}, u32[]{:S(2)}, u32[]{:S(2)}) %collective-permute-start.1) | collective-permute-done | bytes 131104 | tf_op jit(solution)/shard_map/ppermute | solution.py:109
  89.9 0.7 fusion.9
  90.7 0.0 all-gather.6.cloned.1.call-update
  90.7 0.0 all-gather.4.cloned.1.call-done
  90.7 4.4 %fusion.1 = f32[256,1024]{0,1:T(8,128)S(1)} fusion(f32[256,1024]{0,1:T(8,128)S(1)} %convolution_bitcast_fusion.1, bf16[1024,2560]{1,0:T(8,128)(2,1)} %all-gather.4.cloned.1.call-done, bf16[256,3072]{1,0:T(8,128)(2,1)} %bitcast.55), kind=kOutput, calls=%fused_computation.3 | convolution fusion | flops 1342439424 | bytes 8650752 | tf_op jit(solution)/shard_map/dot_general | solution.py:48
  95.2 3.1 %collective-permute-start.2 = (bf16[128,1024]{0,1:T(8,128)(2,1)S(1)}, bf16[128,1024]{0,1:T(8,128)(2,1)S(1)}, u32[]{:S(2)}, u32[]{:S(2)}) collective-permute-start(bf16[128,1024]{0,1:T(8,128)(2,1)S(1)} %select_convert_fusion), channel_id=1, source_target_pairs={{0,1},{1,0},{2,3},{3,2},{4,5},{5,4},{6,7},{7,6},{8,9},{9,8},{10,11... | collective-permute-start | bytes 786440 | tf_op jit(solution)/shard_map/ppermute | solution.py:27
  98.3 1.1 collective-permute-done.2
  99.5 0.1 add_convert_fusion
  99.5 0.1 copy.16
  99.7 10.9 %all_to_all.42 = bf16[4,32,1024]{2,1,0:T(8,128)(2,1)S(1)} all-to-all(bf16[4,32,1024]{2,1,0:T(8,128)(2,1)S(1)} %bitcast.48), channel_id=1, replica_groups=mesh['y'=4,'x'=4,'far'=4,'near'=4,'core'=2] {'near'}, dimensions={0} | all-to-all | bytes 524288 | tf_op jit(solution)/shard_map/all_to_all | solution.py:22
  110.6 26.1 %all_to_all.43 = bf16[4,32,1024]{2,1,0:T(8,128)(2,1)S(1)} all-to-all(bf16[4,32,1024]{2,1,0:T(8,128)(2,1)S(1)} %broadcast_in_dim.15), channel_id=1, replica_groups=mesh['y'=4,'x'=4,'far'=4,'near'=4,'core'=2] {'far'}, dimensions={0} | all-to-all | bytes 524288 | tf_op jit(solution)/shard_map/all_to_all | solution.py:17
  136.8 10.0 %all_to_all.44 = bf16[4,32,1024]{2,1,0:T(8,128)(2,1)S(1)} all-to-all(bf16[4,32,1024]{2,1,0:T(8,128)(2,1)S(1)} %broadcast_in_dim.16), channel_id=1, replica_groups=mesh['y'=4,'x'=4,'far'=4,'near'=4,'core'=2] {'near'}, dimensions={0} | all-to-all | bytes 524288 | tf_op jit(solution)/shard_map/all_to_all | solution.py:17
  146.8 7.5 %collective-permute-start.3 = (bf16[128,1024]{1,0:T(8,128)(2,1)S(1)}, bf16[128,1024]{1,0:T(8,128)(2,1)S(1)}, u32[]{:S(2)}, u32[]{:S(2)}) collective-permute-start(bf16[128,1024]{1,0:T(8,128)(2,1)S(1)} %bitcast.46), channel_id=1, source_target_pairs={{0,1},{1,0},{2,3},{3,2},{4,5},{5,4},{6,7},{7,6},{8,9},{9,8},{10,11... | collective-permute-start | bytes 786440 | tf_op jit(solution)/shard_map/ppermute | solution.py:27
  154.3 0.0 all-gather.6.cloned.1.call-done
  154.3 0.0 copy-start
  154.3 1.6 copy-done
  155.9 0.4 shard_map.55
  156.3 0.2 fusion.11
  156.5 0.2 fusion.7
  156.7 0.2 fusion.14
  156.9 0.0 collective-permute-done.3
  156.9 0.2 fusion.5
  157.1 14.6 %all_to_all.45 = bf16[16,8,1024]{2,1,0:T(8,128)(2,1)S(1)} all-to-all(bf16[16,8,1024]{2,1,0:T(8,128)(2,1)S(1)} %fusion.5), channel_id=1, replica_groups=mesh['y'=4,'x'=4,'far'=4,'near'=4,'core'=2] {'y','x'}, dimensions={0} | all-to-all | bytes 524288 | tf_op jit(solution)/shard_map/all_to_all | solution.py:22
  171.7 10.2 %all_to_all.46 = bf16[16,8,1024]{2,1,0:T(8,128)(2,1)S(1)} all-to-all(bf16[16,8,1024]{2,1,0:T(8,128)(2,1)S(1)} %broadcast_in_dim.17), channel_id=1, replica_groups=mesh['y'=4,'x'=4,'far'=4,'near'=4,'core'=2] {'y','x'}, dimensions={0} | all-to-all | bytes 524288 | tf_op jit(solution)/shard_map/all_to_all | solution.py:17
  181.9 0.7 copy.20
  (16 shorter events, 0.4 us)
Async XLA Ops:
  6.5 84.2 %all-gather.4.cloned.1.call-start = ((), (), s32[]{:S(2)}) async-start(), calls=%async_computation.8 | async-start | bytes 5570560 | tf_op jit(solution)/shard_map/all_gather | solution.py:93
  19.5 5.1 %copy-start.2 = (bf16[2,64,128]{2,1,0:T(8,128)(2,1)S(1)}, bf16[2,64,128]{2,1,0:T(8,128)(2,1)}, u32[]{:S(2)}) copy-start(bf16[2,64,128]{2,1,0:T(8,128)(2,1)} %param.9) | copy-start | bytes 98308
  19.5 5.1 %copy-start.3 = (bf16[128,64]{0,1:T(8,128)(2,1)S(1)}, bf16[128,64]{0,1:T(8,128)(2,1)}, u32[]{:S(2)}) copy-start(bf16[128,64]{0,1:T(8,128)(2,1)} %param.8) | copy-start | bytes 49156
  19.5 5.2 %copy-start.1 = (bf16[2,128,1024]{2,1,0:T(8,128)(2,1)S(1)}, bf16[2,128,1024]{2,1,0:T(8,128)(2,1)}, u32[]{:S(2)}) copy-start(bf16[2,128,1024]{2,1,0:T(8,128)(2,1)} %param.7) | copy-start | bytes 1572868
  20.6 13.8 %all-to-all-start.1 = ((bf16[4,4,64,512]{3,2,1,0:T(8,128)(2,1)}), bf16[4,4,64,512]{3,2,1,0:T(8,128)(2,1)S(1)}, u32[]{:S(2)}, u32[]{:S(2)}) async-start(bf16[4,4,64,512]{3,2,1,0:T(8,128)(2,1)} %broadcast_in_dim.13), calls=%async_computation.1 | async-start | bytes 2097152 | tf_op jit(solution)/shard_map/all_to_all | solution.py:42
  24.6 129.7 %all-gather.6.cloned.1.call-start = ((), (), s32[]{:S(2)}) async-start(), calls=%async_computation.9 | async-start | bytes 2228224 | tf_op jit(solution)/shard_map/all_gather | solution.py:111
  69.4 13.7 %collective-permute-start = (bf16[16,128,128]{2,1,0:T(8,128)(2,1)S(1)}, bf16[16,128,128]{2,1,0:T(8,128)(2,1)S(1)}, u32[]{:S(2)}, u32[]{:S(2)}) collective-permute-start(bf16[16,128,128]{2,1,0:T(8,128)(2,1)S(1)} %all_to_all.41), channel_id=1, source_target_pairs={{0,1},{1,0},{2,3},{3,2},{4,5},{5,4},{6,7},{7,6},{8,9},{9,8},{10,11... | collective-permute-start | bytes 1572872 | tf_op jit(solution)/shard_map/ppermute | solution.py:27
  83.3 6.6 %collective-permute-start.1 = (bf16[64,1024]{1,0:T(8,128)(2,1)S(1)}, bf16[64,1024]{1,0:T(8,128)(2,1)S(1)}, u32[]{:S(2)}, u32[]{:S(2)}) collective-permute-start(bf16[64,1024]{1,0:T(8,128)(2,1)S(1)} %select_bitcast_fusion), channel_id=1, source_target_pairs={{0,32},{32,0},{64,96},{96,64},{1,33},{33,1},{65,97},{97,65},{2,34}... | collective-permute-start | bytes 393224 | tf_op jit(solution)/shard_map/ppermute | solution.py:109
  95.2 4.3 %collective-permute-start.2 = (bf16[128,1024]{0,1:T(8,128)(2,1)S(1)}, bf16[128,1024]{0,1:T(8,128)(2,1)S(1)}, u32[]{:S(2)}, u32[]{:S(2)}) collective-permute-start(bf16[128,1024]{0,1:T(8,128)(2,1)S(1)} %select_convert_fusion), channel_id=1, source_target_pairs={{0,1},{1,0},{2,3},{3,2},{4,5},{5,4},{6,7},{7,6},{8,9},{9,8},{10,11... | collective-permute-start | bytes 786440 | tf_op jit(solution)/shard_map/ppermute | solution.py:27
  146.8 10.1 %collective-permute-start.3 = (bf16[128,1024]{1,0:T(8,128)(2,1)S(1)}, bf16[128,1024]{1,0:T(8,128)(2,1)S(1)}, u32[]{:S(2)}, u32[]{:S(2)}) collective-permute-start(bf16[128,1024]{1,0:T(8,128)(2,1)S(1)} %bitcast.46), channel_id=1, source_target_pairs={{0,1},{1,0},{2,3},{3,2},{4,5},{5,4},{6,7},{7,6},{8,9},{9,8},{10,11... | collective-permute-start | bytes 786440 | tf_op jit(solution)/shard_map/ppermute | solution.py:27
  154.3 1.6 copy-start
Sparse Core Ops, SparseCore 0:
  10.4 77.7 all-gather.3
  91.2 61.9 all-gather.5

commit v9 on v8

--- a/solution.py
+++ b/solution.py
@@ -8,7 +8,6 @@
 BF16 = jnp.bfloat16
 F32 = jnp.float32
 ROW = ("y", "x")
-Z = ("far", "near")
 SPLIT = 20
 
 
@@ -98,7 +97,7 @@
         rest = gather_both_ways(solved_earlier[:, split:], n_y, n_x, core == 0)
         packed, right, is_first, rest = lax.optimization_barrier((packed, right, is_first, rest))
 
-        mine = spread(packed, Z, n_z)
+        mine = spread(spread(packed, "far", n_z // n_near), "near", n_near).reshape(n_z, *packed.shape)
         other = swap_cores(mine)
         left = [
             matmul(inverses[1], part_[:, :own].reshape(-1, rows), (1, 1)).astype(BF16)

time: 190 us -> 190 us (level)
  blocking collectives: 117 us -> 120 us
  starting transfers between devices: 28.9 us -> 26.2 us
    all_to_all x4 -> x5, blocking collectives: 81 us -> 84.1 us  [spread(): return lax.all_to_all(copies, axis, 0, 0)]
    ppermute x3, starting transfers between devices: 22.8 us -> 20 us  [swap_cores(): return lax.ppermute(block, 'core', [(0, 1), (1, 0)])]
where the time goes in v9:
time: 190 us; the launch traced here: 189 us
  blocking collectives  120 us (63%)
  starting transfers between devices  26.2 us (14%)
  waiting for transfers between devices  15.1 us (8%)
  between operations  13.7 us (7%)
  matrix products  7.04 us (4%)
  local copies, waits for them, and re-layouts  6.4 us (3%)
    all_to_all x5, blocking collectives, spread(): return lax.all_to_all(copies, axis, 0, 0)  84.1 us
    all_to_all x2, blocking collectives, sum_rows(): pieces = lax.all_to_all(terms.reshape(size, rows // size, cols), axis, 0, 0)  25.2 us
    ppermute x3, starting transfers between devices, swap_cores(): return lax.ppermute(block, 'core', [(0, 1), (1, 0)])  20 us
    all_to_all x1, blocking collectives, gather_both_ways(): lax.all_to_all(copies, ('y', 'x', 'core'), 0, 0, axis_index_groups=groups)  10.3 us
    all_to_all x1, waiting for transfers between devices, gather_both_ways(): lax.all_to_all(copies, ('y', 'x', 'core'), 0, 0, axis_index_groups=groups)  9.62 us
    dot_general x8, matrix products, matmul(): lax.dot_general(a, b, ((contract[0:1], contract[1:2]), ((), ())), preferr...  7.04 us
    all_to_all x1, starting transfers between devices, gather_both_ways(): lax.all_to_all(copies, ('y', 'x', 'core'), 0, 0, axis_index_groups=groups)  4.01 us
  transfers between devices with their start and end apart: 7, of which 4 were waited for; matrix products, arithmetic and copies ran while one was open for 5% of the time, Pallas kernels for 0%

profile of v9, /device:TPU:1, one launch (start us, length us, event | category | flops | bytes accessed | tf_op | source)
XLA Modules:
  0.0 189.5 jit_solution(3497357312130210971)
XLA Ops:
  6.5 0.0 all-gather.4.cloned.1.call-start
  6.5 1.7 slice.61
  8.2 0.0 all-gather.4.cloned.1.call-update
  8.3 0.8 slice.60
  9.1 10.3 %all_to_all.45 = bf16[4,64,512]{2,1,0:T(8,128)(2,1)S(1)} all-to-all(bf16[4,64,512]{2,1,0:T(8,128)(2,1)S(1)} %broadcast_in_dim.14), channel_id=1, replica_groups={{0,32,64,96},{128,160,192,224},{256,288,320,352},{384,416,448,480},{1,1..., dimensions={0} | all-to-all | bytes 524288 | tf_op jit(solution)/shard_map/all_to_all | solution.py:41
  19.5 0.0 copy-start.2
  19.5 0.0 copy-start.3
  19.5 0.0 copy-start.1
  19.5 1.1 broadcast_in_dim.15
  20.6 4.0 %all-to-all-start.1 = ((bf16[4,4,64,512]{3,2,1,0:T(8,128)(2,1)}), bf16[4,4,64,512]{3,2,1,0:T(8,128)(2,1)S(1)}, u32[]{:S(2)}, u32[]{:S(2)}) async-start(bf16[4,4,64,512]{3,2,1,0:T(8,128)(2,1)} %broadcast_in_dim.15), calls=%async_computation.1 | async-start | bytes 2097152 | tf_op jit(solution)/shard_map/all_to_all | solution.py:41
  24.6 0.0 all-gather.6.cloned.1.call-start
  24.6 0.0 copy-done.2
  24.6 0.0 copy-done.3
  24.6 0.0 copy-done.1
  24.7 9.6 %all-to-all-done.1 = bf16[4,4,64,512]{3,2,1,0:T(8,128)(2,1)S(1)} async-done(((bf16[4,4,64,512]{3,2,1,0:T(8,128)(2,1)}), bf16[4,4,64,512]{3,2,1,0:T(8,128)(2,1)S(1)}, u32[]{:S(2)}, u32[]{:S(2)}) %all-to-all-start.1) | async-done | bytes 1048608 | tf_op jit(solution)/shard_map/all_to_all | solution.py:41
  34.3 0.1 bitcast_select_fusion
  34.5 28.1 %all_to_all.46 = bf16[4,128,128]{2,1,0:T(8,128)(2,1)S(1)} all-to-all(bf16[4,128,128]{2,1,0:T(8,128)(2,1)S(1)} %broadcast_in_dim.16), channel_id=1, replica_groups=mesh['y'=4,'x'=4,'far'=4,'near'=4,'core'=2] {'far'}, dimensions={0} | all-to-all | bytes 262144 | tf_op jit(solution)/shard_map/all_to_all | solution.py:16
  62.5 0.1 broadcast_in_dim.17
  62.6 13.0 %all_to_all.47 = bf16[4,4,128,128]{3,2,1,0:T(8,128)(2,1)S(1)} all-to-all(bf16[4,4,128,128]{3,2,1,0:T(8,128)(2,1)S(1)} %broadcast_in_dim.17), channel_id=1, replica_groups=mesh['y'=4,'x'=4,'far'=4,'near'=4,'core'=2] {'near'}, dimensions={0} | all-to-all | bytes 1048576 | tf_op jit(solution)/shard_map/all_to_all | solution.py:16
  75.6 9.4 %collective-permute-start = (bf16[16,128,128]{2,1,0:T(8,128)(2,1)S(1)}, bf16[16,128,128]{2,1,0:T(8,128)(2,1)S(1)}, u32[]{:S(2)}, u32[]{:S(2)}) collective-permute-start(bf16[16,128,128]{2,1,0:T(8,128)(2,1)S(1)} %bitcast.47), channel_id=1, source_target_pairs={{0,1},{1,0},{2,3},{3,2},{4,5},{5,4},{6,7},{7,6},{8,9},{9,8},{10,11... | collective-permute-start | bytes 1572872 | tf_op jit(solution)/shard_map/ppermute | solution.py:26
  85.1 0.2 convolution_convert_fusion.1
  85.3 1.2 collective-permute-done
  86.5 0.2 convolution_convert_fusion
  86.8 2.2 %collective-permute-start.1 = (bf16[64,1024]{1,0:T(8,128)(2,1)S(1)}, bf16[64,1024]{1,0:T(8,128)(2,1)S(1)}, u32[]{:S(2)}, u32[]{:S(2)}) collective-permute-start(bf16[64,1024]{1,0:T(8,128)(2,1)S(1)} %select_bitcast_fusion), channel_id=1, source_target_pairs={{0,32},{32,0},{64,96},{96,64},{1,33},{33,1},{65,97},{97,65},{2,34}... | collective-permute-start | bytes 393224 | tf_op jit(solution)/shard_map/ppermute | solution.py:108
  89.0 1.4 convolution_bitcast_fusion.1
  90.4 3.0 %collective-permute-done.1 = bf16[64,1024]{1,0:T(8,128)(2,1)S(1)} collective-permute-done((bf16[64,1024]{1,0:T(8,128)(2,1)S(1)}, bf16[64,1024]{1,0:T(8,128)(2,1)S(1)}, u32[]{:S(2)}, u32[]{:S(2)}) %collective-permute-start.1) | collective-permute-done | bytes 131104 | tf_op jit(solution)/shard_map/ppermute | solution.py:108
  93.4 0.7 fusion.9
  94.1 0.0 all-gather.6.cloned.1.call-update
  94.1 0.0 all-gather.4.cloned.1.call-done
  94.2 4.4 %fusion.1 = f32[256,1024]{0,1:T(8,128)S(1)} fusion(f32[256,1024]{0,1:T(8,128)S(1)} %convolution_bitcast_fusion.1, bf16[1024,2560]{1,0:T(8,128)(2,1)} %all-gather.4.cloned.1.call-done, bf16[256,3072]{1,0:T(8,128)(2,1)} %bitcast.58), kind=kOutput, calls=%fused_computation.3 | convolution fusion | flops 1342439424 | bytes 8650752 | tf_op jit(solution)/shard_map/dot_general | solution.py:47
  98.6 3.1 %collective-permute-start.2 = (bf16[128,1024]{0,1:T(8,128)(2,1)S(1)}, bf16[128,1024]{0,1:T(8,128)(2,1)S(1)}, u32[]{:S(2)}, u32[]{:S(2)}) collective-permute-start(bf16[128,1024]{0,1:T(8,128)(2,1)S(1)} %select_convert_fusion), channel_id=1, source_target_pairs={{0,1},{1,0},{2,3},{3,2},{4,5},{5,4},{6,7},{7,6},{8,9},{9,8},{10,11... | collective-permute-start | bytes 786440 | tf_op jit(solution)/shard_map/ppermute | solution.py:26
  101.8 1.1 collective-permute-done.2
  102.9 0.1 add_convert_fusion
  103.0 0.1 copy.16
  103.1 10.7 %all_to_all.48 = bf16[4,32,1024]{2,1,0:T(8,128)(2,1)S(1)} all-to-all(bf16[4,32,1024]{2,1,0:T(8,128)(2,1)S(1)} %bitcast.51), channel_id=1, replica_groups=mesh['y'=4,'x'=4,'far'=4,'near'=4,'core'=2] {'near'}, dimensions={0} | all-to-all | bytes 524288 | tf_op jit(solution)/shard_map/all_to_all | solution.py:21
  113.9 22.8 %all_to_all.49 = bf16[4,32,1024]{2,1,0:T(8,128)(2,1)S(1)} all-to-all(bf16[4,32,1024]{2,1,0:T(8,128)(2,1)S(1)} %broadcast_in_dim.18), channel_id=1, replica_groups=mesh['y'=4,'x'=4,'far'=4,'near'=4,'core'=2] {'far'}, dimensions={0} | all-to-all | bytes 524288 | tf_op jit(solution)/shard_map/all_to_all | solution.py:16
  136.8 10.0 %all_to_all.50 = bf16[4,32,1024]{2,1,0:T(8,128)(2,1)S(1)} all-to-all(bf16[4,32,1024]{2,1,0:T(8,128)(2,1)S(1)} %broadcast_in_dim.19), channel_id=1, replica_groups=mesh['y'=4,'x'=4,'far'=4,'near'=4,'core'=2] {'near'}, dimensions={0} | all-to-all | bytes 524288 | tf_op jit(solution)/shard_map/all_to_all | solution.py:16
  146.8 7.5 %collective-permute-start.3 = (bf16[128,1024]{1,0:T(8,128)(2,1)S(1)}, bf16[128,1024]{1,0:T(8,128)(2,1)S(1)}, u32[]{:S(2)}, u32[]{:S(2)}) collective-permute-start(bf16[128,1024]{1,0:T(8,128)(2,1)S(1)} %bitcast.49), channel_id=1, source_target_pairs={{0,1},{1,0},{2,3},{3,2},{4,5},{5,4},{6,7},{7,6},{8,9},{9,8},{10,11... | collective-permute-start | bytes 786440 | tf_op jit(solution)/shard_map/ppermute | solution.py:26
  154.3 0.0 all-gather.6.cloned.1.call-done
  154.3 0.0 copy-start
  154.3 1.6 copy-done
  155.9 0.4 shard_map.55
  156.3 0.2 fusion.11
  156.5 0.2 fusion.7
  156.7 0.2 fusion.14
  156.9 0.0 collective-permute-done.3
  156.9 0.2 fusion.5
  157.1 14.6 %all_to_all.51 = bf16[16,8,1024]{2,1,0:T(8,128)(2,1)S(1)} all-to-all(bf16[16,8,1024]{2,1,0:T(8,128)(2,1)S(1)} %fusion.5), channel_id=1, replica_groups=mesh['y'=4,'x'=4,'far'=4,'near'=4,'core'=2] {'y','x'}, dimensions={0} | all-to-all | bytes 524288 | tf_op jit(solution)/shard_map/all_to_all | solution.py:21
  171.7 10.2 %all_to_all.52 = bf16[16,8,1024]{2,1,0:T(8,128)(2,1)S(1)} all-to-all(bf16[16,8,1024]{2,1,0:T(8,128)(2,1)S(1)} %broadcast_in_dim.20), channel_id=1, replica_groups=mesh['y'=4,'x'=4,'far'=4,'near'=4,'core'=2] {'y','x'}, dimensions={0} | all-to-all | bytes 524288 | tf_op jit(solution)/shard_map/all_to_all | solution.py:16
  181.9 0.7 copy.20
  (17 shorter events, 0.5 us)
Async XLA Ops:
  6.5 87.6 %all-gather.4.cloned.1.call-start = ((), (), s32[]{:S(2)}) async-start(), calls=%async_computation.9 | async-start | bytes 5570560 | tf_op jit(solution)/shard_map/all_gather | solution.py:92
  19.5 5.1 %copy-start.2 = (bf16[2,64,128]{2,1,0:T(8,128)(2,1)S(1)}, bf16[2,64,128]{2,1,0:T(8,128)(2,1)}, u32[]{:S(2)}) copy-start(bf16[2,64,128]{2,1,0:T(8,128)(2,1)} %param.9) | copy-start | bytes 98308
  19.5 5.1 %copy-start.3 = (bf16[128,64]{0,1:T(8,128)(2,1)S(1)}, bf16[128,64]{0,1:T(8,128)(2,1)}, u32[]{:S(2)}) copy-start(bf16[128,64]{0,1:T(8,128)(2,1)} %param.8) | copy-start | bytes 49156
  19.5 5.2 %copy-start.1 = (bf16[2,128,1024]{2,1,0:T(8,128)(2,1)S(1)}, bf16[2,128,1024]{2,1,0:T(8,128)(2,1)}, u32[]{:S(2)}) copy-start(bf16[2,128,1024]{2,1,0:T(8,128)(2,1)} %param.7) | copy-start | bytes 1572868
  20.6 13.8 %all-to-all-start.1 = ((bf16[4,4,64,512]{3,2,1,0:T(8,128)(2,1)}), bf16[4,4,64,512]{3,2,1,0:T(8,128)(2,1)S(1)}, u32[]{:S(2)}, u32[]{:S(2)}) async-start(bf16[4,4,64,512]{3,2,1,0:T(8,128)(2,1)} %broadcast_in_dim.15), calls=%async_computation.1 | async-start | bytes 2097152 | tf_op jit(solution)/shard_map/all_to_all | solution.py:41
  24.6 129.7 %all-gather.6.cloned.1.call-start = ((), (), s32[]{:S(2)}) async-start(), calls=%async_computation.10 | async-start | bytes 2228224 | tf_op jit(solution)/shard_map/all_gather | solution.py:110
  75.6 10.9 %collective-permute-start = (bf16[16,128,128]{2,1,0:T(8,128)(2,1)S(1)}, bf16[16,128,128]{2,1,0:T(8,128)(2,1)S(1)}, u32[]{:S(2)}, u32[]{:S(2)}) collective-permute-start(bf16[16,128,128]{2,1,0:T(8,128)(2,1)S(1)} %bitcast.47), channel_id=1, source_target_pairs={{0,1},{1,0},{2,3},{3,2},{4,5},{5,4},{6,7},{7,6},{8,9},{9,8},{10,11... | collective-permute-start | bytes 1572872 | tf_op jit(solution)/shard_map/ppermute | solution.py:26
  86.8 6.6 %collective-permute-start.1 = (bf16[64,1024]{1,0:T(8,128)(2,1)S(1)}, bf16[64,1024]{1,0:T(8,128)(2,1)S(1)}, u32[]{:S(2)}, u32[]{:S(2)}) collective-permute-start(bf16[64,1024]{1,0:T(8,128)(2,1)S(1)} %select_bitcast_fusion), channel_id=1, source_target_pairs={{0,32},{32,0},{64,96},{96,64},{1,33},{33,1},{65,97},{97,65},{2,34}... | collective-permute-start | bytes 393224 | tf_op jit(solution)/shard_map/ppermute | solution.py:108
  98.6 4.2 %collective-permute-start.2 = (bf16[128,1024]{0,1:T(8,128)(2,1)S(1)}, bf16[128,1024]{0,1:T(8,128)(2,1)S(1)}, u32[]{:S(2)}, u32[]{:S(2)}) collective-permute-start(bf16[128,1024]{0,1:T(8,128)(2,1)S(1)} %select_convert_fusion), channel_id=1, source_target_pairs={{0,1},{1,0},{2,3},{3,2},{4,5},{5,4},{6,7},{7,6},{8,9},{9,8},{10,11... | collective-permute-start | bytes 786440 | tf_op jit(solution)/shard_map/ppermute | solution.py:26
  146.8 10.1 %collective-permute-start.3 = (bf16[128,1024]{1,0:T(8,128)(2,1)S(1)}, bf16[128,1024]{1,0:T(8,128)(2,1)S(1)}, u32[]{:S(2)}, u32[]{:S(2)}) collective-permute-start(bf16[128,1024]{1,0:T(8,128)(2,1)S(1)} %bitcast.49), channel_id=1, source_target_pairs={{0,1},{1,0},{2,3},{3,2},{4,5},{5,4},{6,7},{7,6},{8,9},{9,8},{10,11... | collective-permute-start | bytes 786440 | tf_op jit(solution)/shard_map/ppermute | solution.py:26
  154.3 1.6 copy-start
Sparse Core Ops, SparseCore 0:
  10.4 77.7 all-gather.3
  94.2 58.9 all-gather.5

commit v10 on v9

--- a/solution.py
+++ b/solution.py
@@ -8,7 +8,7 @@
 BF16 = jnp.bfloat16
 F32 = jnp.float32
 ROW = ("y", "x")
-SPLIT = 20
+SPLIT = 22
 
 
 def spread(block, axis, size):

time: 190 us -> 192 us (1.011)
  blocking collectives: 120 us -> 113 us
  waiting for transfers between devices: 15.1 us -> 20 us
  starting transfers between devices: 26.2 us -> 29.8 us
    all_to_all x1 -> x0, blocking collectives: 10.3 us -> none  [gather_both_ways(): lax.all_to_all(copies, ('y', 'x', 'core'), 0, 0, axis_index_groups=groups)]
    all_to_all x1 -> x2, starting transfers between devices: 4.01 us -> 9.03 us  [gather_both_ways(): lax.all_to_all(copies, ('y', 'x', 'core'), 0, 0, axis_index_groups=groups)]
    ppermute x1, waiting for transfers between devices: 2.98 us -> 5.94 us  [per_device(): received = lax.ppermute(jnp.where(even, left[1], left[0]), 'x', pairs)]
    all_to_all x5, blocking collectives: 84.1 us -> 86.9 us  [spread(): return lax.all_to_all(copies, axis, 0, 0)]
    all_to_all x1 -> x2, waiting for transfers between devices: 9.62 us -> 11.6 us  [gather_both_ways(): lax.all_to_all(copies, ('y', 'x', 'core'), 0, 0, axis_index_groups=groups)]
  transfers between devices with their start and end apart: 7 -> 8, of which waited for: 4 -> 5; matrix products, arithmetic and copies ran while one was open for 5% -> 6% of each run, Pallas kernels for 0% -> 0%
where the time goes in v10:
time: 192 us
  blocking collectives  113 us (59%)
  starting transfers between devices  29.8 us (16%)
  waiting for transfers between devices  20 us (10%)
  between operations  13.7 us (7%)
  matrix products  7.16 us (4%)
  local copies, waits for them, and re-layouts  6.84 us (4%)
    all_to_all x5, blocking collectives, spread(): return lax.all_to_all(copies, axis, 0, 0)  86.9 us
    all_to_all x2, blocking collectives, sum_rows(): pieces = lax.all_to_all(terms.reshape(size, rows // size, cols), axis, 0, 0)  25.6 us
    ppermute x3, starting transfers between devices, swap_cores(): return lax.ppermute(block, 'core', [(0, 1), (1, 0)])  18.7 us
    all_to_all x2, waiting for transfers between devices, gather_both_ways(): lax.all_to_all(copies, ('y', 'x', 'core'), 0, 0, axis_index_groups=groups)  11.6 us
    all_to_all x2, starting transfers between devices, gather_both_ways(): lax.all_to_all(copies, ('y', 'x', 'core'), 0, 0, axis_index_groups=groups)  9.03 us
    dot_general x8, matrix products, matmul(): lax.dot_general(a, b, ((contract[0:1], contract[1:2]), ((), ())), preferr...  7.16 us
    ppermute x1, waiting for transfers between devices, per_device(): received = lax.ppermute(jnp.where(even, left[1], left[0]), 'x', pairs)  5.94 us
  transfers between devices with their start and end apart: 8, of which 5 were waited for; matrix products, arithmetic and copies ran while one was open for 6% of the time, Pallas kernels for 0%

profile of v10, /device:TPU:1, one launch (start us, length us, event | category | flops | bytes accessed | tf_op | source)
XLA Modules:
  0.0 191.5 jit_solution(2454700853759736990)
XLA Ops:
  6.5 0.0 copy-start.2
  6.5 0.0 copy-start.3
  6.5 0.0 copy-start.1
  6.5 0.0 all-gather.4.cloned.1.call-start
  6.5 1.8 slice.61
  8.4 0.0 all-gather.4.cloned.1.call-update
  8.4 0.8 slice.60
  9.2 0.7 broadcast_in_dim.14
  9.8 5.0 %all-to-all-start = ((bf16[4,64,256]{2,1,0:T(8,128)(2,1)}), bf16[4,64,256]{2,1,0:T(8,128)(2,1)S(1)}, u32[]{:S(2)}, u32[]{:S(2)}) async-start(bf16[4,64,256]{2,1,0:T(8,128)(2,1)} %broadcast_in_dim.14), calls=%async_computation | async-start | bytes 262144 | tf_op jit(solution)/shard_map/all_to_all | solution.py:41
  14.9 0.0 copy-done.2
  14.9 4.8 %all-to-all-done = bf16[4,64,256]{2,1,0:T(8,128)(2,1)S(1)} async-done(((bf16[4,64,256]{2,1,0:T(8,128)(2,1)}), bf16[4,64,256]{2,1,0:T(8,128)(2,1)S(1)}, u32[]{:S(2)}, u32[]{:S(2)}) %all-to-all-start) | async-done | bytes 131104 | tf_op jit(solution)/shard_map/all_to_all | solution.py:41
  19.7 0.8 broadcast_in_dim.15
  20.5 4.0 %all-to-all-start.1 = ((bf16[4,4,64,256]{3,2,1,0:T(8,128)(2,1)}), bf16[4,4,64,256]{3,2,1,0:T(8,128)(2,1)S(1)}, u32[]{:S(2)}, u32[]{:S(2)}) async-start(bf16[4,4,64,256]{3,2,1,0:T(8,128)(2,1)} %broadcast_in_dim.15), calls=%async_computation.1 | async-start | bytes 1048576 | tf_op jit(solution)/shard_map/all_to_all | solution.py:41
  24.5 0.0 all-gather.6.cloned.1.call-start
  24.5 0.0 copy-done.3
  24.6 0.0 copy-done.1
  24.7 6.8 %all-to-all-done.1 = bf16[4,4,64,256]{3,2,1,0:T(8,128)(2,1)S(1)} async-done(((bf16[4,4,64,256]{3,2,1,0:T(8,128)(2,1)}), bf16[4,4,64,256]{3,2,1,0:T(8,128)(2,1)S(1)}, u32[]{:S(2)}, u32[]{:S(2)}) %all-to-all-start.1) | async-done | bytes 524320 | tf_op jit(solution)/shard_map/all_to_all | solution.py:41
  31.5 26.9 %all_to_all.45 = bf16[4,128,128]{2,1,0:T(8,128)(2,1)S(1)} all-to-all(bf16[4,128,128]{2,1,0:T(8,128)(2,1)S(1)} %broadcast_in_dim.16), channel_id=1, replica_groups=mesh['y'=4,'x'=4,'far'=4,'near'=4,'core'=2] {'far'}, dimensions={0} | all-to-all | bytes 262144 | tf_op jit(solution)/shard_map/all_to_all | solution.py:16
  58.4 0.1 broadcast_in_dim.17
  58.5 13.0 %all_to_all.46 = bf16[4,4,128,128]{3,2,1,0:T(8,128)(2,1)S(1)} all-to-all(bf16[4,4,128,128]{3,2,1,0:T(8,128)(2,1)S(1)} %broadcast_in_dim.17), channel_id=1, replica_groups=mesh['y'=4,'x'=4,'far'=4,'near'=4,'core'=2] {'near'}, dimensions={0} | all-to-all | bytes 1048576 | tf_op jit(solution)/shard_map/all_to_all | solution.py:16
  71.6 8.3 %collective-permute-start = (bf16[16,128,128]{2,1,0:T(8,128)(2,1)S(1)}, bf16[16,128,128]{2,1,0:T(8,128)(2,1)S(1)}, u32[]{:S(2)}, u32[]{:S(2)}) collective-permute-start(bf16[16,128,128]{2,1,0:T(8,128)(2,1)S(1)} %bitcast.47), channel_id=1, source_target_pairs={{0,1},{1,0},{2,3},{3,2},{4,5},{5,4},{6,7},{7,6},{8,9},{9,8},{10,11... | collective-permute-start | bytes 1572872 | tf_op jit(solution)/shard_map/ppermute | solution.py:26
  80.0 0.2 convolution_convert_fusion.1
  80.2 1.2 collective-permute-done
  81.5 0.2 convolution_convert_fusion
  81.7 2.0 %collective-permute-start.1 = (bf16[64,1024]{1,0:T(8,128)(2,1)S(1)}, bf16[64,1024]{1,0:T(8,128)(2,1)S(1)}, u32[]{:S(2)}, u32[]{:S(2)}) collective-permute-start(bf16[64,1024]{1,0:T(8,128)(2,1)S(1)} %select_bitcast_fusion), channel_id=1, source_target_pairs={{0,32},{32,0},{64,96},{96,64},{1,33},{33,1},{65,97},{97,65},{2,34}... | collective-permute-start | bytes 393224 | tf_op jit(solution)/shard_map/ppermute | solution.py:108
  83.8 1.2 convolution_bitcast_fusion
  85.0 5.9 %collective-permute-done.1 = bf16[64,1024]{1,0:T(8,128)(2,1)S(1)} collective-permute-done((bf16[64,1024]{1,0:T(8,128)(2,1)S(1)}, bf16[64,1024]{1,0:T(8,128)(2,1)S(1)}, u32[]{:S(2)}, u32[]{:S(2)}) %collective-permute-start.1) | collective-permute-done | bytes 131104 | tf_op jit(solution)/shard_map/ppermute | solution.py:108
  90.9 0.7 fusion.12
  91.6 0.0 all-gather.6.cloned.1.call-update
  91.7 0.0 all-gather.4.cloned.1.call-done
  91.7 4.7 %fusion.5 = f32[256,1024]{0,1:T(8,128)S(1)} fusion(f32[256,1024]{0,1:T(8,128)S(1)} %convolution_bitcast_fusion, bf16[1024,2816]{1,0:T(8,128)(2,1)} %all-gather.4.cloned.1.call-done, bf16[256,3072]{1,0:T(8,128)(2,1)} %bitcast.59), kind=kOutput, calls=%fused_computation.4 | convolution fusion | flops 1476657152 | bytes 9306112 | tf_op jit(solution)/shard_map/dot_general | solution.py:47
  96.5 2.6 %collective-permute-start.2 = (bf16[128,1024]{0,1:T(8,128)(2,1)S(1)}, bf16[128,1024]{0,1:T(8,128)(2,1)S(1)}, u32[]{:S(2)}, u32[]{:S(2)}) collective-permute-start(bf16[128,1024]{0,1:T(8,128)(2,1)S(1)} %select_convert_fusion), channel_id=1, source_target_pairs={{0,1},{1,0},{2,3},{3,2},{4,5},{5,4},{6,7},{7,6},{8,9},{9,8},{10,11... | collective-permute-start | bytes 786440 | tf_op jit(solution)/shard_map/ppermute | solution.py:26
  99.1 1.1 collective-permute-done.2
  100.2 0.1 add_convert_fusion
  100.3 0.1 copy.16
  100.5 11.1 %all_to_all.47 = bf16[4,32,1024]{2,1,0:T(8,128)(2,1)S(1)} all-to-all(bf16[4,32,1024]{2,1,0:T(8,128)(2,1)S(1)} %bitcast.51), channel_id=1, replica_groups=mesh['y'=4,'x'=4,'far'=4,'near'=4,'core'=2] {'near'}, dimensions={0} | all-to-all | bytes 524288 | tf_op jit(solution)/shard_map/all_to_all | solution.py:21
  111.6 27.1 %all_to_all.48 = bf16[4,32,1024]{2,1,0:T(8,128)(2,1)S(1)} all-to-all(bf16[4,32,1024]{2,1,0:T(8,128)(2,1)S(1)} %broadcast_in_dim.18), channel_id=1, replica_groups=mesh['y'=4,'x'=4,'far'=4,'near'=4,'core'=2] {'far'}, dimensions={0} | all-to-all | bytes 524288 | tf_op jit(solution)/shard_map/all_to_all | solution.py:16
  138.8 9.7 %all_to_all.49 = bf16[4,32,1024]{2,1,0:T(8,128)(2,1)S(1)} all-to-all(bf16[4,32,1024]{2,1,0:T(8,128)(2,1)S(1)} %broadcast_in_dim.19), channel_id=1, replica_groups=mesh['y'=4,'x'=4,'far'=4,'near'=4,'core'=2] {'near'}, dimensions={0} | all-to-all | bytes 524288 | tf_op jit(solution)/shard_map/all_to_all | solution.py:16
  148.5 7.8 %collective-permute-start.3 = (bf16[128,1024]{1,0:T(8,128)(2,1)S(1)}, bf16[128,1024]{1,0:T(8,128)(2,1)S(1)}, u32[]{:S(2)}, u32[]{:S(2)}) collective-permute-start(bf16[128,1024]{1,0:T(8,128)(2,1)S(1)} %bitcast.49), channel_id=1, source_target_pairs={{0,1},{1,0},{2,3},{3,2},{4,5},{5,4},{6,7},{7,6},{8,9},{9,8},{10,11... | collective-permute-start | bytes 786440 | tf_op jit(solution)/shard_map/ppermute | solution.py:26
  156.4 0.0 all-gather.6.cloned.1.call-done
  156.4 0.0 copy-start
  156.4 1.6 copy-done
  158.0 0.4 shard_map.55
  158.3 0.2 fusion.14
  158.5 0.2 fusion.11
  158.7 0.2 fusion.18
  158.9 0.0 collective-permute-done.3
  158.9 0.2 fusion.9
  159.2 14.6 %all_to_all.50 = bf16[16,8,1024]{2,1,0:T(8,128)(2,1)S(1)} all-to-all(bf16[16,8,1024]{2,1,0:T(8,128)(2,1)S(1)} %fusion.9), channel_id=1, replica_groups=mesh['y'=4,'x'=4,'far'=4,'near'=4,'core'=2] {'y','x'}, dimensions={0} | all-to-all | bytes 524288 | tf_op jit(solution)/shard_map/all_to_all | solution.py:21
  173.8 10.2 %all_to_all.51 = bf16[16,8,1024]{2,1,0:T(8,128)(2,1)S(1)} all-to-all(bf16[16,8,1024]{2,1,0:T(8,128)(2,1)S(1)} %broadcast_in_dim.20), channel_id=1, replica_groups=mesh['y'=4,'x'=4,'far'=4,'near'=4,'core'=2] {'y','x'}, dimensions={0} | all-to-all | bytes 524288 | tf_op jit(solution)/shard_map/all_to_all | solution.py:16
  184.0 0.7 copy.20
  (17 shorter events, 0.5 us)
Async XLA Ops:
  6.5 8.3 %copy-start.2 = (bf16[2,64,128]{2,1,0:T(8,128)(2,1)S(1)}, bf16[2,64,128]{2,1,0:T(8,128)(2,1)}, u32[]{:S(2)}) copy-start(bf16[2,64,128]{2,1,0:T(8,128)(2,1)} %param.9) | copy-start | bytes 98308
  6.5 18.0 %copy-start.3 = (bf16[128,64]{0,1:T(8,128)(2,1)S(1)}, bf16[128,64]{0,1:T(8,128)(2,1)}, u32[]{:S(2)}) copy-start(bf16[128,64]{0,1:T(8,128)(2,1)} %param.8) | copy-start | bytes 49156
  6.5 18.0 %copy-start.1 = (bf16[2,128,1024]{2,1,0:T(8,128)(2,1)S(1)}, bf16[2,128,1024]{2,1,0:T(8,128)(2,1)}, u32[]{:S(2)}) copy-start(bf16[2,128,1024]{2,1,0:T(8,128)(2,1)} %param.7) | copy-start | bytes 1572868
  6.5 85.1 %all-gather.4.cloned.1.call-start = ((), (), s32[]{:S(2)}) async-start(), calls=%async_computation.9 | async-start | bytes 6127616 | tf_op jit(solution)/shard_map/all_gather | solution.py:92
  9.8 9.8 %all-to-all-start = ((bf16[4,64,256]{2,1,0:T(8,128)(2,1)}), bf16[4,64,256]{2,1,0:T(8,128)(2,1)S(1)}, u32[]{:S(2)}, u32[]{:S(2)}) async-start(bf16[4,64,256]{2,1,0:T(8,128)(2,1)} %broadcast_in_dim.14), calls=%async_computation | async-start | bytes 262144 | tf_op jit(solution)/shard_map/all_to_all | solution.py:41
  20.5 10.9 %all-to-all-start.1 = ((bf16[4,4,64,256]{3,2,1,0:T(8,128)(2,1)}), bf16[4,4,64,256]{3,2,1,0:T(8,128)(2,1)S(1)}, u32[]{:S(2)}, u32[]{:S(2)}) async-start(bf16[4,4,64,256]{3,2,1,0:T(8,128)(2,1)} %broadcast_in_dim.15), calls=%async_computation.1 | async-start | bytes 1048576 | tf_op jit(solution)/shard_map/all_to_all | solution.py:41
  24.5 131.8 %all-gather.6.cloned.1.call-start = ((), (), s32[]{:S(2)}) async-start(), calls=%async_computation.10 | async-start | bytes 2228224 | tf_op jit(solution)/shard_map/all_gather | solution.py:110
  71.6 9.9 %collective-permute-start = (bf16[16,128,128]{2,1,0:T(8,128)(2,1)S(1)}, bf16[16,128,128]{2,1,0:T(8,128)(2,1)S(1)}, u32[]{:S(2)}, u32[]{:S(2)}) collective-permute-start(bf16[16,128,128]{2,1,0:T(8,128)(2,1)S(1)} %bitcast.47), channel_id=1, source_target_pairs={{0,1},{1,0},{2,3},{3,2},{4,5},{5,4},{6,7},{7,6},{8,9},{9,8},{10,11... | collective-permute-start | bytes 1572872 | tf_op jit(solution)/shard_map/ppermute | solution.py:26
  81.7 9.2 %collective-permute-start.1 = (bf16[64,1024]{1,0:T(8,128)(2,1)S(1)}, bf16[64,1024]{1,0:T(8,128)(2,1)S(1)}, u32[]{:S(2)}, u32[]{:S(2)}) collective-permute-start(bf16[64,1024]{1,0:T(8,128)(2,1)S(1)} %select_bitcast_fusion), channel_id=1, source_target_pairs={{0,32},{32,0},{64,96},{96,64},{1,33},{33,1},{65,97},{97,65},{2,34}... | collective-permute-start | bytes 393224 | tf_op jit(solution)/shard_map/ppermute | solution.py:108
  96.5 3.7 %collective-permute-start.2 = (bf16[128,1024]{0,1:T(8,128)(2,1)S(1)}, bf16[128,1024]{0,1:T(8,128)(2,1)S(1)}, u32[]{:S(2)}, u32[]{:S(2)}) collective-permute-start(bf16[128,1024]{0,1:T(8,128)(2,1)S(1)} %select_convert_fusion), channel_id=1, source_target_pairs={{0,1},{1,0},{2,3},{3,2},{4,5},{5,4},{6,7},{7,6},{8,9},{9,8},{10,11... | collective-permute-start | bytes 786440 | tf_op jit(solution)/shard_map/ppermute | solution.py:26
  148.5 10.4 %collective-permute-start.3 = (bf16[128,1024]{1,0:T(8,128)(2,1)S(1)}, bf16[128,1024]{1,0:T(8,128)(2,1)S(1)}, u32[]{:S(2)}, u32[]{:S(2)}) collective-permute-start(bf16[128,1024]{1,0:T(8,128)(2,1)S(1)} %bitcast.49), channel_id=1, source_target_pairs={{0,1},{1,0},{2,3},{3,2},{4,5},{5,4},{6,7},{7,6},{8,9},{9,8},{10,11... | collective-permute-start | bytes 786440 | tf_op jit(solution)/shard_map/ppermute | solution.py:26
  156.4 1.6 copy-start
Sparse Core Ops, SparseCore 0:
  10.4 79.7 all-gather.3
  93.2 61.6 all-gather.5
